TPU v7x, 32 devices: a whole 2x2x4 slice. The times are simulated.
32 devices in a mesh: ctx: 8 (over y, x, core), tp: 4 (over z).
Axes of the slice: x: 2, y: 2, z: 4, core: 2. Of those that a mesh axis runs over, the one named last changes fastest.
Arguments:
- positions: int32 [1280], replicated, may hold values from 0 to 1279, as said below
- queries: bfloat16 [1280, 8192], P('ctx', 'tp'), may hold values from -6 to 6
- key_state_rows: bfloat16 [1280, 1024], P('ctx', 'tp'), may hold values from -6 to 6
- value_state_rows: bfloat16 [1280, 1024], P('ctx', 'tp'), may hold values from -6 to 6
- attn_output: bfloat16 [1280, 8192], P('ctx', 'tp'), may hold values from -6 to 6
- output_grad: bfloat16 [1280, 8192], P('ctx', 'tp'), may hold values from -48 to 48
- log_sums: float32 [1280, 64], P('ctx', 'tp')
Outputs:
- query_grad: bfloat16 [1280, 8192], P('ctx', 'tp')
- key_state_gradient: bfloat16 [1280, 1024], P(('ctx', 'tp'))
- value_state_gradient: bfloat16 [1280, 1024], P(('ctx', 'tp'))
Inputs may be any that keep to these rules, and one draw needn't show every extreme that they name: A permutation of 0 to 1279; each aligned block of 160 rows holds two runs of 80 rising consecutive positions, the first starting at c * (80) and the second at (15 - c) * 80, for a c of its own.
All inputs are finite; a program needn't handle non-finite values.
Results may differ from a plain program's by a relative error of at most 0.0059.
Values may be sent and summed in bfloat16 or wider, within the bound.
No kernel may reach another device: no remote copies, remote signals or barrier semaphores. Data moves between devices by JAX's collectives and lax.ppermute only.
A program may use at most 128 MiB of HBM per device.

v0:
```python
import math

import jax
import jax.numpy as jnp
from jax import lax
from jax.sharding import PartitionSpec as P

HEAD_SIZE = 128


def on_device(
    positions, queries, key_state_rows, value_state_rows, attn_output, output_grad, log_sums
):
    ctx_count = lax.axis_size("ctx")
    tok_rows = queries.shape[0]
    half_rows = tok_rows // 2
    head_count = log_sums.shape[1]
    key_heads = key_state_rows.shape[1] // HEAD_SIZE
    queries_per_group = head_count // key_heads
    stretch_count = 2 * ctx_count
    total_rows = tok_rows * ctx_count
    feature_cols = key_heads * HEAD_SIZE
    score_scale = 1.0 / math.sqrt(HEAD_SIZE)
    row_start = lax.axis_index("ctx") * tok_rows
    own_spots = lax.dynamic_slice_in_dim(positions, row_start, tok_rows, 0).reshape(2, half_rows)
    key_all, value_all = (
        lax.all_gather(key_state_rows, "ctx", axis=0, tiled=True),
        lax.all_gather(value_state_rows, "ctx", axis=0, tiled=True),
    )
    stretch_first = positions.reshape(stretch_count, half_rows)[:, 0] // half_rows
    sort_order = (
        jnp.zeros((stretch_count,), jnp.int32)
        .at[stretch_first]
        .set(jnp.arange(stretch_count, dtype=jnp.int32))
    )
    key_sorted = key_all.reshape(stretch_count, half_rows, key_heads, HEAD_SIZE)[
        sort_order
    ].reshape(total_rows, key_heads, HEAD_SIZE)
    value_sorted = value_all.reshape(stretch_count, half_rows, key_heads, HEAD_SIZE)[
        sort_order
    ].reshape(total_rows, key_heads, HEAD_SIZE)
    query_halves = queries.reshape(2, half_rows, key_heads, queries_per_group, HEAD_SIZE)
    grad_halves = output_grad.reshape(2, half_rows, key_heads, queries_per_group, HEAD_SIZE)
    out_halves = attn_output.reshape(2, half_rows, key_heads, queries_per_group, HEAD_SIZE)
    delta = jnp.sum(grad_halves.astype(jnp.float32) * out_halves.astype(jnp.float32), axis=-1)
    delta = jnp.transpose(delta, (0, 2, 3, 1))
    lse_rows = jnp.transpose(
        log_sums.reshape(2, half_rows, key_heads, queries_per_group), (0, 2, 3, 1)
    )

    def tile_math(which, key_block, value_block, key_spots):
        query_half = query_halves[which]
        grad_half = grad_halves[which]
        scores = (
            jnp.einsum("qgha,kga->ghqk", query_half, key_block, preferred_element_type=jnp.float32)
            * score_scale
        )
        visible = key_spots[None, :] <= own_spots[which][:, None]
        probs = jnp.where(visible, jnp.exp(scores - lse_rows[which][..., None]), jnp.float32(0.0))
        prob_grad = jnp.einsum(
            "qgha,kga->ghqk", grad_half, value_block, preferred_element_type=jnp.float32
        )
        score_grad = (probs * (prob_grad - delta[which][..., None])).astype(jnp.bfloat16)
        results = []
        results.append(
            jnp.einsum("ghqk,kga->qgha", score_grad, key_block, preferred_element_type=jnp.float32)
            * score_scale
        )
        probs_low = probs.astype(jnp.bfloat16)
        results.append(
            jnp.einsum("ghqk,qgha->kga", score_grad, query_half, preferred_element_type=jnp.float32)
            * score_scale
        )
        results.append(
            jnp.einsum("ghqk,qgha->kga", probs_low, grad_half, preferred_element_type=jnp.float32)
        )
        return tuple(results)

    span = 1
    while span < stretch_count and span * half_rows < 512 and (stretch_count % (2 * span) == 0):
        span = span * 2
    block_keys = span * half_rows
    block_count = stretch_count // span

    def block_step(carry, block_index):
        first = block_index * block_keys
        key_block = lax.dynamic_slice_in_dim(key_sorted, first, block_keys, 0)
        value_block = lax.dynamic_slice_in_dim(value_sorted, first, block_keys, 0)
        key_spots = first + jnp.arange(block_keys, dtype=jnp.int32)
        key_total = jnp.zeros((block_keys, key_heads, HEAD_SIZE), jnp.float32)
        value_total = jnp.zeros((block_keys, key_heads, HEAD_SIZE), jnp.float32)
        for which in range(2):

            def compute(which=which):
                return tile_math(which, key_block, value_block, key_spots)

            parts = compute()
            carry = carry.at[which].add(parts[0])
            key_total = key_total + parts[1]
            value_total = value_total + parts[2]
        return (carry, (key_total, value_total))

    start_acc = jnp.zeros((2, half_rows, key_heads, queries_per_group, HEAD_SIZE), jnp.float32)
    query_acc, (key_out, value_out) = lax.scan(
        block_step, start_acc, jnp.arange(block_count, dtype=jnp.int32)
    )
    key_terms = key_out.reshape(stretch_count, half_rows, feature_cols)[stretch_first].reshape(
        total_rows, feature_cols
    )
    value_terms = value_out.reshape(stretch_count, half_rows, feature_cols)[stretch_first].reshape(
        total_rows, feature_cols
    )
    partial_value = jnp.stack((key_terms, value_terms), axis=1)
    summed = lax.psum_scatter(partial_value, "ctx", scatter_dimension=0, tiled=True).astype(
        jnp.bfloat16
    )
    query_grad = query_acc.reshape(tok_rows, head_count * HEAD_SIZE).astype(jnp.bfloat16)
    spread = lax.all_to_all(summed, "tp", split_axis=0, concat_axis=2, tiled=True)
    return (query_grad, spread[:, 0], spread[:, 1])


def solution(mesh):
    placed = (
        P(),
        P("ctx", "tp"),
        P("ctx", "tp"),
        P("ctx", "tp"),
        P("ctx", "tp"),
        P("ctx", "tp"),
        P("ctx", "tp"),
    )
    return jax.shard_map(
        on_device,
        mesh=mesh,
        in_specs=placed,
        out_specs=(P("ctx", "tp"), P(("ctx", "tp"), None), P(("ctx", "tp"), None)),
        check_vma=False,
    )
```

profile of v0, /device:TPU:0, one launch (start us, length us, event | category | flops | bytes accessed | tf_op | source)
XLA Modules:
  0.0 158.9 jit_solution(15502357673961862790)
XLA Ops:
  3.1 0.8 reshape.152
  3.9 1.2 copy.70
  5.3 11.6 %all_gather.6 = bf16[1280,256]{1,0:T(8,128)(2,1)S(1)} all-gather(bf16[160,256]{1,0:T(8,128)(2,1)S(1)} %copy-done.8), channel_id=1, replica_groups=mesh['ctx'=8,'tp'=4] {'ctx'}, dimensions={0}, use_global_device_ids=true | all-gather | bytes 737280 | tf_op jit(solution)/shard_map/all_gather | solution.py:27
  18.1 10.1 %all_gather.7 = bf16[1280,256]{1,0:T(8,128)(2,1)S(1)} all-gather(bf16[160,256]{1,0:T(8,128)(2,1)S(1)} %copy-done.9), channel_id=1, replica_groups=mesh['ctx'=8,'tp'=4] {'ctx'}, dimensions={0}, use_global_device_ids=true | all-gather | bytes 737280 | tf_op jit(solution)/shard_map/all_gather | solution.py:28
  29.1 0.9 copy.46
  30.1 1.0 copy.49
  32.6 30.8 %while.18 = (s32[]{:T(128)}, f32[2,80,2,8,128]{4,1,3,2,0:T(8,128)S(1)}, f32[2,640,2,128]{3,2,1,0:T(2,128)}, f32[2,640,2,128]{3,2,1,0:T(2,128)}, s32[2]{0:T(128)S...) while((s32[]{:T(128)}, ...), condition=%wide.region_3.4_spmd, body=%wide.region_2.3_spmd.sunk | while | flops 2114785920 | bytes 67251456 | solution.py:104
  35.1 1.4 fusion.138
  37.9 1.3 fusion.140
  39.3 1.4 fusion.141
  40.7 1.4 fusion.135
  42.1 0.8 fusion.142
  45.4 1.1 copy_dynamic-update-slice_fusion.3
  46.5 1.0 copy-done.1
  50.5 1.4 fusion.138
  53.4 1.3 fusion.140
  54.7 1.4 fusion.141
  56.1 1.4 fusion.135
  57.5 0.8 fusion.142
  60.8 1.1 copy_dynamic-update-slice_fusion.3
  61.9 1.0 copy-done.1
  63.4 2.3 %reshape.157 = f32[16,80,256]{2,1,0:T(8,128)S(1)} reshape(f32[2,640,2,128]{3,2,1,0:T(2,128)} %get-tuple-element.182) | data formatting | bytes 2621440 | tf_op jit(solution)/shard_map/reshape | solution.py:110
  65.8 1.7 %gather_fusion.3 = f32[16,80,256]{2,1,0:T(8,128)} fusion(f32[16,80,256]{2,1,0:T(8,128)S(1)} %reshape.157, s32[1024]{0:T(1024)S(1)} %pad_clamp_fusion), kind=kCustom, calls=%fused_computation.3 | custom fusion | bytes 2621504 | tf_op jit(solution)/shard_map/gather | solution.py:110
  67.4 4.1 %copy.55 = f32[1280,1,256]{2,1,0:T(1,128)S(1)} copy(f32[1280,1,256]{2,0,1:T(8,128)} %bitcast.251) | data formatting | bytes 2621440 | tf_op jit(solution)/shard_map/stack;reshape | solution.py:113
  71.6 3.4 %reshape.156 = f32[16,80,256]{2,1,0:T(8,128)} reshape(f32[2,640,2,128]{3,2,1,0:T(2,128)} %get-tuple-element.181) | data formatting | bytes 2621440 | tf_op jit(solution)/shard_map/reshape | solution.py:107
  74.9 3.0 %gather_fusion.2 = f32[16,80,256]{2,1,0:T(8,128)} fusion(f32[16,80,256]{2,1,0:T(8,128)} %reshape.156, s32[1024]{0:T(1024)S(1)} %pad_clamp_fusion), kind=kCustom, calls=%fused_computation.2 | custom fusion | bytes 2621504 | tf_op jit(solution)/shard_map/gather | solution.py:107
  77.9 4.1 %copy.54 = f32[1280,1,256]{2,1,0:T(1,128)S(1)} copy(f32[1280,1,256]{2,0,1:T(8,128)} %bitcast.250) | data formatting | bytes 2621440 | tf_op jit(solution)/shard_map/stack;reshape | solution.py:113
  82.0 3.5 %pad_maximum_fusion = f32[1280,2,256]{2,1,0:T(2,128)} fusion(f32[1280,1,256]{2,1,0:T(1,128)S(1)} %copy.55, f32[1280,1,256]{2,1,0:T(1,128)S(1)} %copy.54), kind=kLoop, calls=%fused_computation.91 | loop fusion | flops 655360 | bytes 5242880 | tf_op jit(solution)/shard_map/stack | solution.py:113
  85.5 59.7 %all-reduce.2 = bf16[1280,2,256]{2,1,0:T(2,128)(2,1)S(1)} all-reduce(f32[1280,2,256]{2,1,0:T(2,128)} %pad_maximum_fusion), channel_id=2, replica_groups=mesh['ctx'=8,'tp'=4] {'ctx'}, use_global_device_ids=true, to_apply=%region_4.5.clone | all-reduce | flops 655360 | bytes 3932160
  147.2 4.9 %all-to-all-start = ((bf16[160,2,256]{2,1,0:T(2,128)(2,1)}), bf16[160,2,256]{2,1,0:T(2,128)(2,1)S(1)}, u32[]{:S(2)}, u32[]{:S(2)}) async-start(bf16[160,2,256]{2,1,0:T(2,128)(2,1)} %dynamic-slice_convert_fusion), calls=%async_computation | async-start | bytes 327680 | tf_op jit(solution)/shard_map/all_to_all | solution.py:118
  152.4 1.1 convert_element_type.46
  153.5 4.6 %all-to-all-done = bf16[160,2,256]{2,1,0:T(2,128)(2,1)S(1)} async-done(((bf16[160,2,256]{2,1,0:T(2,128)(2,1)}), bf16[160,2,256]{2,1,0:T(2,128)(2,1)S(1)}, u32[]{:S(2)}, u32[]{:S(2)}) %all-to-all-start) | async-done | bytes 163872 | tf_op jit(solution)/shard_map/all_to_all | solution.py:118
  (86 shorter events, 20.7 us)
Async XLA Ops:
  0.6 4.7 %copy-start.8 = (bf16[160,256]{1,0:T(8,128)(2,1)S(1)}, bf16[160,256]{1,0:T(8,128)(2,1)}, u32[]{:S(2)}) copy-start(bf16[160,256]{1,0:T(8,128)(2,1)} %param.15) | copy-start | bytes 245764
  17.2 0.9 copy-start.9
  28.4 1.6 copy-start.4
  30.0 1.2 copy-start.7
  31.5 1.1 copy-start.5
  34.0 1.1 copy-start.6
  43.7 1.3 copy-start
  43.7 1.7 %copy-start.2 = (f32[2,640,2,128]{3,2,1,0:T(2,128)S(1)}, f32[2,640,2,128]{3,2,1,0:T(2,128)}, u32[]{:S(2)}) copy-start(f32[2,640,2,128]{3,2,1,0:T(2,128)} %get-tuple-element.378) | copy-start | bytes 3932164 | tf_op jit(solution)/shard_map/while
  46.5 1.1 copy-start.1
  46.5 1.5 copy-start.3
  49.4 1.1 copy-start.6
  59.1 1.3 copy-start
  59.1 1.7 %copy-start.2 = (f32[2,640,2,128]{3,2,1,0:T(2,128)S(1)}, f32[2,640,2,128]{3,2,1,0:T(2,128)}, u32[]{:S(2)}) copy-start(f32[2,640,2,128]{3,2,1,0:T(2,128)} %get-tuple-element.378) | copy-start | bytes 3932164 | tf_op jit(solution)/shard_map/while
  61.9 1.1 copy-start.1
  61.9 1.5 copy-start.3
  85.5 59.7 %copy-start.10 = (u32[32]{0:T(128)S(1)}, u32[32]{0:T(128)}, u32[]{:S(2)}) copy-start(u32[32]{0:T(128)} %constant.140) | copy-start | bytes 388
  147.2 10.9 %all-to-all-start = ((bf16[160,2,256]{2,1,0:T(2,128)(2,1)}), bf16[160,2,256]{2,1,0:T(2,128)(2,1)S(1)}, u32[]{:S(2)}, u32[]{:S(2)}) async-start(bf16[160,2,256]{2,1,0:T(2,128)(2,1)} %dynamic-slice_convert_fusion), calls=%async_computation | async-start | bytes 327680 | tf_op jit(solution)/shard_map/all_to_all | solution.py:118
where the time goes:
time: 160 us; the launch traced here: 159 us
  blocking collectives  81.3 us (51%)
  local copies, waits for them, and re-layouts  40.3 us (25%)
  matrix products  19.8 us (12%)
  starting transfers between devices  4.94 us (3%)
  other arithmetic  4.66 us (3%)
  waiting for transfers between devices  4.62 us (3%)
  loops' own time  1.62 us (1%)
    unnamed x1, blocking collectives  59.7 us
    all_gather x1, blocking collectives, on_device(): lax.all_gather(key_state_rows, 'ctx', axis=0, tiled=True)  11.6 us
    all_gather x1, blocking collectives, on_device(): lax.all_gather(value_state_rows, 'ctx', axis=0, tiled=True)  10.1 us
    another operation x2, local copies, waits for them, and re-layouts, on_device(): partial_value = jnp.stack((key_terms, value_terms), axis=1)  8.2 us
    while x20, local copies, waits for them, and re-layouts  5.78 us
    dot_general x4, matrix products, tile_math(): jnp.einsum('qgha,kga->ghqk', grad_half, value_block, preferred_element_ty...  5.73 us
    dot_general x4, matrix products, tile_math(): jnp.einsum('ghqk,qgha->kga', probs_low, grad_half, preferred_element_type...  5.41 us
    all_to_all x1, starting transfers between devices, on_device(): lax.all_to_all(summed, 'tp', split_axis=0, concat_axis=2, tiled=True)  4.94 us
  transfers between devices with their start and end apart: 1, of which 1 were waited for; matrix products, arithmetic and copies ran while one was open for 1% of the time, Pallas kernels for 0%

commit v1 on v0

v1 whole, which is shorter than its diff:
```python
import functools
import math

import jax
import jax.numpy as jnp
from jax import lax
from jax.experimental import pallas as pl
from jax.experimental.pallas import tpu as pltpu
from jax.sharding import PartitionSpec as P

HEAD_SIZE = 128
SCALE = 1.0 / math.sqrt(HEAD_SIZE)
EXP2_SCALE = SCALE * math.log2(math.e)
LOG2E = math.log2(math.e)
F32 = jnp.float32
BF16 = jnp.bfloat16
VMEM = pl.BlockSpec(memory_space=pltpu.VMEM)
SMEM = pl.BlockSpec(memory_space=pltpu.SMEM)


def call(kernel, outs, ins, scratch=(), smem=0):
    specs = [SMEM] * smem + [VMEM] * (len(ins) - smem)
    return pl.pallas_call(
        kernel,
        in_specs=specs,
        out_specs=[VMEM] * len(outs),
        out_shape=[jax.ShapeDtypeStruct(shape, dtype) for shape, dtype in outs],
        scratch_shapes=list(scratch),
        compiler_params=pltpu.CompilerParams(vmem_limit_bytes=48 * 2**20),
    )(*ins)


def nt(a, b):
    return lax.dot_general(a, b, (((1,), (1,)), ((), ())), preferred_element_type=F32)


def parity():
    return lax.rem(lax.axis_index("ctx"), 2)


def pack_kv_kernel(k_ref, v_ref, same_ref, other_ref):
    rows = k_ref.shape[0]
    c = parity()
    for ref, group in ((same_ref, c), (other_ref, 1 - c)):
        cols = pl.ds(pl.multiple_of(group * HEAD_SIZE, HEAD_SIZE), HEAD_SIZE)
        ref[:rows] = k_ref[:, cols]
        ref[rows:] = v_ref[:, cols]


def split_bf16(x, terms):
    parts = []
    for _ in range(terms):
        part = x.astype(BF16)
        parts.append(part)
        x = x - part.astype(F32)
    return parts


def pack_q_kernel(heads, q_ref, g_ref, o_ref, l_ref, same_ref, other_ref, same_rows, other_rows):
    rows = q_ref.shape[0]
    half = rows // 2
    c = parity()
    ones = jnp.ones((8, HEAD_SIZE), BF16)
    ones_l = jnp.ones((8, l_ref.shape[1]), BF16)
    lane = lax.broadcasted_iota(jnp.int32, (half, l_ref.shape[1]), 1)
    for ref, row_ref, group in ((same_ref, same_rows, c), (other_ref, other_rows, 1 - c)):
        for w in range(2):
            r = slice(w * half, (w + 1) * half)
            lse = jnp.clip(l_ref[r], -1e30, 1e30)
            deltas = []
            logs = []
            for h in range(heads):
                cols = pl.ds(
                    pl.multiple_of((group * heads + h) * HEAD_SIZE, HEAD_SIZE), HEAD_SIZE
                )
                g = g_ref[r, cols]
                ref[w, h * half : (h + 1) * half, :] = q_ref[r, cols]
                ref[2 + w, h * half : (h + 1) * half, :] = g
                deltas.append(g.astype(F32) * o_ref[r, cols].astype(F32))
                logs.append(jnp.where(lane == group * heads + h, lse, 0.0))
            delta = jnp.concatenate(deltas, axis=0)
            log = jnp.concatenate(logs, axis=0)
            delta_row = sum(nt(ones, part) for part in split_bf16(delta, 2))
            log_row = sum(nt(ones_l, part) for part in split_bf16(log, 3))
            row_ref[w : w + 1, :] = log_row[0:1] * LOG2E
            row_ref[2 + w : 3 + w, :] = delta_row[0:1]


def run_starts(pos_ref, tokens, shift):
    ctx = lax.axis_index("ctx")
    return pos_ref[jnp.bitwise_xor(ctx, shift) * tokens]


def steps(base, half, block, step):
    full = lax.div(base + 1, block)
    last = lax.div(base + half + block - 1, block)

    def run(masked):
        def body(t, carry):
            step(t, masked)
            return carry

        return body

    lax.fori_loop(0, full, run(False), 0)
    lax.fori_loop(full, last, run(True), 0)


def sort_keys(pos_ref, pieces, ks, vs):
    tokens = pieces[0].shape[0] // 2
    half = tokens // 2
    total = ks.shape[0]
    for m, piece in enumerate(pieces):
        first = run_starts(pos_ref, tokens, m)
        for w, start in enumerate((first, total - half - first)):
            r = pl.ds(pl.multiple_of(start, half), half)
            ks[r, :] = piece[w * half : (w + 1) * half, :]
            vs[r, :] = piece[tokens + w * half : tokens + (w + 1) * half, :]


def kv_grad_kernel(n, block, pos_ref, own, sib, own_rows, sib_rows, *refs):
    pieces, refs = refs[:n], refs[n:]
    outs, (ks, vs, dk, dv) = refs[:n], refs[n:]
    tokens = pieces[0].shape[0] // 2
    half = tokens // 2
    total = ks.shape[0]
    lanes = own.shape[1]
    sort_keys(pos_ref, pieces, ks, vs)
    dk[...] = jnp.zeros_like(dk)
    dv[...] = jnp.zeros_like(dv)
    key_row = lax.broadcasted_iota(jnp.int32, (block, lanes), 0)
    query_row = lax.rem(lax.broadcasted_iota(jnp.int32, (block, lanes), 1), half)
    ahead = query_row - key_row
    for b, (stack, vec) in enumerate(((own, own_rows), (sib, sib_rows))):
        first = run_starts(pos_ref, tokens, b)
        for w, base in enumerate((first, total - half - first)):

            def step(t, masked, stack=stack, vec=vec, w=w, base=base):
                start = pl.multiple_of(t * block, block)
                r = pl.ds(start, block)
                s = nt(ks[r, :], stack[w])
                dp = nt(vs[r, :], stack[2 + w])
                p = jnp.exp2(s * EXP2_SCALE - vec[w : w + 1, :])
                if masked:
                    p = jnp.where(ahead >= start - base, p, 0.0)
                ds = (p * (dp - vec[2 + w : 3 + w, :])).astype(BF16)
                dv[r, :] += jnp.dot(p.astype(BF16), stack[2 + w], preferred_element_type=F32)
                dk[r, :] += jnp.dot(ds, stack[w], preferred_element_type=F32)

            steps(base, half, block, step)
    for m, out in enumerate(outs):
        first = run_starts(pos_ref, tokens, m)
        for w, start in enumerate((first, total - half - first)):
            r = pl.ds(pl.multiple_of(start, half), half)
            out[w * half : (w + 1) * half, :] = (dk[r, :] * SCALE).astype(out.dtype)
            out[tokens + w * half : tokens + (w + 1) * half, :] = dv[r, :].astype(out.dtype)


def q_grad_kernel(n, block, pos_ref, own, sib, own_rows, sib_rows, *refs):
    pieces, refs = refs[:n], refs[n:]
    outs, (ks, vs, acc) = refs[:2], refs[2:]
    tokens = pieces[0].shape[0] // 2
    half = tokens // 2
    total = ks.shape[0]
    lanes = own.shape[1]
    sort_keys(pos_ref, pieces, ks, vs)
    key_row = lax.broadcasted_iota(jnp.int32, (block, lanes), 0)
    query_row = lax.rem(lax.broadcasted_iota(jnp.int32, (block, lanes), 1), half)
    ahead = query_row - key_row
    for b, (stack, vec) in enumerate(((own, own_rows), (sib, sib_rows))):
        first = run_starts(pos_ref, tokens, b)
        for w, base in enumerate((first, total - half - first)):
            acc[...] = jnp.zeros_like(acc)

            def step(t, masked, stack=stack, vec=vec, w=w, base=base):
                start = pl.multiple_of(t * block, block)
                r = pl.ds(start, block)
                k = ks[r, :]
                s = nt(k, stack[w])
                dp = nt(vs[r, :], stack[2 + w])
                p = jnp.exp2(s * EXP2_SCALE - vec[w : w + 1, :])
                if masked:
                    p = jnp.where(ahead >= start - base, p, 0.0)
                ds = (p * (dp - vec[2 + w : 3 + w, :])).astype(BF16)
                acc[...] += lax.dot_general(
                    ds, k, (((0,), (0,)), ((), ())), preferred_element_type=F32
                )

            steps(base, half, block, step)
            outs[b][w] = (acc[...] * SCALE).astype(BF16)


def sum_kernel(n, tp_count, own_ref, *refs):
    parts, refs = refs[: n - 1], refs[n - 1 :]
    outs, (total,) = refs[:tp_count], refs[tp_count:]
    tokens = own_ref.shape[0] // 2
    share = tokens // tp_count
    c = parity()
    z = lax.axis_index("tp")
    for odd in range(2):
        terms = [parts[m - 1] for m in range(1, n) if m % 2 == odd]
        value = own_ref[...] if odd == 0 else None
        for term in terms:
            term = term[...].astype(F32)
            value = term if value is None else value + term
        group = c if odd == 0 else 1 - c
        cols = pl.ds(pl.multiple_of(group * HEAD_SIZE, HEAD_SIZE), HEAD_SIZE)
        total[:, cols] = value
    for m, out in enumerate(outs):
        start = jnp.bitwise_xor(z, m) * share
        for kind in range(2):
            r = pl.ds(pl.multiple_of(kind * tokens + start, 8), share)
            out[kind] = total[r, :].astype(BF16)


def spread_kernel(tp_count, *refs):
    parts, (key_out, value_out) = refs[:tp_count], refs[tp_count:]
    z = lax.axis_index("tp")
    width = parts[0].shape[2]
    for m, part in enumerate(parts):
        cols = pl.ds(pl.multiple_of(jnp.bitwise_xor(z, m) * width, width), width)
        key_out[:, cols] = part[0]
        value_out[:, cols] = part[1]


def unstack_kernel(heads, own, other, out):
    half = out.shape[0] // 2
    c = parity()
    for ref, group in ((own, c), (other, 1 - c)):
        for w in range(2):
            for h in range(heads):
                cols = pl.ds(
                    pl.multiple_of((group * heads + h) * HEAD_SIZE, HEAD_SIZE), HEAD_SIZE
                )
                out[w * half : (w + 1) * half, cols] = ref[w, h * half : (h + 1) * half, :]


def swap(x, axis, shift):
    count = lax.axis_size(axis)
    return lax.ppermute(x, axis, [(i, i ^ shift) for i in range(count)])


def on_device(positions, queries, keys, values, attn_output, output_grad, log_sums):
    n = lax.axis_size("ctx")
    tp_count = lax.axis_size("tp")
    tokens = queries.shape[0]
    half = tokens // 2
    heads = log_sums.shape[1] // 2
    total = tokens * n
    lanes = heads * half
    block = 4 * half

    piece = ((2 * tokens, HEAD_SIZE), BF16)
    kv_same, kv_other = call(pack_kv_kernel, [piece] * 2, [keys, values])
    pieces = [kv_same] + [swap(kv_other if m % 2 else kv_same, "ctx", m) for m in range(1, n)]

    stack = ((4, lanes, HEAD_SIZE), BF16)
    vectors = ((4, lanes), F32)
    own, other, own_rows, other_rows = call(
        functools.partial(pack_q_kernel, heads),
        [stack, stack, vectors, vectors],
        [queries, output_grad, attn_output, log_sums],
    )
    sib, sib_rows = swap(other, "ctx", 1), swap(other_rows, "ctx", 1)

    operands = [positions, own, sib, own_rows, sib_rows] + pieces
    key_scratch = [pltpu.VMEM((total, HEAD_SIZE), BF16)] * 2
    partials = call(
        functools.partial(kv_grad_kernel, n, block),
        [(piece[0], F32)] + [piece] * (n - 1),
        operands,
        key_scratch + [pltpu.VMEM((total, HEAD_SIZE), F32)] * 2,
        smem=1,
    )
    received = [swap(partials[m], "ctx", m) for m in range(1, n)]

    half_stack = ((2, lanes, HEAD_SIZE), BF16)
    dq_own, dq_sib = call(
        functools.partial(q_grad_kernel, n, block),
        [half_stack] * 2,
        operands,
        key_scratch + [pltpu.VMEM((lanes, HEAD_SIZE), F32)],
        smem=1,
    )
    dq_other = swap(dq_sib, "ctx", 1)
    (query_grad,) = call(
        functools.partial(unstack_kernel, heads), [(queries.shape, BF16)], [dq_own, dq_other]
    )

    share = ((2, tokens // tp_count, 2 * HEAD_SIZE), BF16)
    shares = call(
        functools.partial(sum_kernel, n, tp_count),
        [share] * tp_count,
        [partials[0]] + received,
        [pltpu.VMEM((2 * tokens, 2 * HEAD_SIZE), F32)],
    )
    shares = [shares[0]] + [swap(shares[m], "tp", m) for m in range(1, tp_count)]
    final = ((tokens // tp_count, 2 * HEAD_SIZE * tp_count), BF16)
    key_grad, value_grad = call(
        functools.partial(spread_kernel, tp_count), [final] * 2, shares
    )
    return (query_grad, key_grad, value_grad)


def solution(mesh):
    split = P("ctx", "tp")
    rows = P(("ctx", "tp"), None)
    return jax.shard_map(
        on_device,
        mesh=mesh,
        in_specs=(P(), split, split, split, split, split, split),
        out_specs=(split, rows, rows),
        check_vma=False,
    )
```

time: 160 us -> 61.1 us (0.38)
  blocking collectives: 81.3 us -> 0 us
  local copies, waits for them, and re-layouts: 40.3 us -> 4.09 us
  matrix products: 19.8 us -> 0 us
  Pallas kernels: 0 us -> 18.2 us
  waiting for transfers between devices: 4.62 us -> 19.4 us
  starting transfers between devices: 4.94 us -> 18.3 us
  other arithmetic: 4.66 us -> 0 us
  loops' own time: 1.62 us -> 0 us
    unnamed x1 -> x0, blocking collectives: 59.7 us -> none
    all_gather x2 -> x0, blocking collectives: 21.7 us -> none  [the longest x1 11.6 us: on_device(): lax.all_gather(key_state_rows, 'ctx', axis=0, tiled=True)]
    dot_general x20 -> x0, matrix products: 19.8 us -> none  [the longest x4 5.73 us: tile_math(): jnp.einsum('qgha,kga->ghqk', grad_half, value_block, preferred_element_ty...]
    ppermute x0 -> x20, waiting for transfers between devices: none -> 19.4 us  [swap(): return lax.ppermute(x, axis, [(i, i ^ shift) for i in range(count)])]
    ppermute x0 -> x20, starting transfers between devices: none -> 18.3 us  [swap(): return lax.ppermute(x, axis, [(i, i ^ shift) for i in range(count)])]
    pallas_call x0 -> x7, Pallas kernels: none -> 18.2 us  [call(): pl.pallas_call(kernel, in_specs=specs, out_specs=[VMEM] * len(outs), out_...]
    another operation x2 -> x0, local copies, waits for them, and re-layouts: 8.2 us -> none  [on_device(): partial_value = jnp.stack((key_terms, value_terms), axis=1)]
    reshape x9 -> x0, local copies, waits for them, and re-layouts: 7.82 us -> none  [the longest x1 3.36 us: on_device(): key_out.reshape(stretch_count, half_rows, feature_cols)[stretch_first]]
  transfers between devices with their start and end apart: 1 -> 20, of which waited for: 1 -> 14; matrix products, arithmetic and copies ran while one was open for 1% -> 0% of each run, Pallas kernels for 0% -> 13%
where the time goes in v1:
time: 61.1 us; the launch traced here: 60.8 us
  waiting for transfers between devices  19.4 us (32%)
  starting transfers between devices  18.3 us (30%)
  Pallas kernels  18.2 us (30%)
  local copies, waits for them, and re-layouts  4.09 us (7%)
  between operations  0.7 us (1%)
    ppermute x20, waiting for transfers between devices, swap(): return lax.ppermute(x, axis, [(i, i ^ shift) for i in range(count)])  19.4 us
    ppermute x20, starting transfers between devices, swap(): return lax.ppermute(x, axis, [(i, i ^ shift) for i in range(count)])  18.3 us
    pallas_call x7, Pallas kernels, call(): pl.pallas_call(kernel, in_specs=specs, out_specs=[VMEM] * len(outs), out_...  18.2 us
    unnamed x13, local copies, waits for them, and re-layouts  4.09 us
  transfers between devices with their start and end apart: 20, of which 14 were waited for; matrix products, arithmetic and copies ran while one was open for 0% of the time, Pallas kernels for 13%

profile of v1, /device:TPU:0, one launch (start us, length us, event | category | flops | bytes accessed | tf_op | source)
XLA Modules:
  0.0 60.8 jit_solution(10545057908167286026)
XLA Ops:
  0.6 0.8 %copy.10.l_ref = f32[160,16]{1,0:T(8,128)S(1)} copy(f32[160,16]{0,1:T(8,128)} %param.13) | data formatting | bytes 20480 | tf_op args[6]
  1.5 1.1 %copy-done = bf16[160,2048]{1,0:T(8,128)(2,1)S(1)} copy-done((bf16[160,2048]{1,0:T(8,128)(2,1)S(1)}, bf16[160,2048]{1,0:T(8,128)(2,1)}, u32[]{:S(2)}) %copy-start) | copy-done | bytes 655384
  2.5 1.1 %copy-done.1 = bf16[160,2048]{1,0:T(8,128)(2,1)S(1)} copy-done((bf16[160,2048]{1,0:T(8,128)(2,1)S(1)}, bf16[160,2048]{1,0:T(8,128)(2,1)}, u32[]{:S(2)}) %copy-start.1) | copy-done | bytes 655384
  3.6 1.1 %copy-done.2 = bf16[160,2048]{1,0:T(8,128)(2,1)S(1)} copy-done((bf16[160,2048]{1,0:T(8,128)(2,1)S(1)}, bf16[160,2048]{1,0:T(8,128)(2,1)}, u32[]{:S(2)}) %copy-start.2) | copy-done | bytes 655384
  4.7 1.4 %shard_map.94 = (bf16[4,640,128]{2,1,0:T(8,128)(2,1)S(1)}, bf16[4,640,128]{2,1,0:T(8,128)(2,1)S(1)}, f32[4,640]{1,0:T(4,128)S(1)}, f32[4,640]{1,0:T(4,128)S(1)}) custom-call(bf16[160,2048]{1,0:T(8,128)(2,1)S(1)} %copy-done, bf16[160,2048]{1,0:T(8,128)(2,1)S(1)} %copy-done.1, bf16[160,2048]{1,0:T(8,128)(2,1)S(1)} %copy-done.2, f32[160,16]{1,0:T(8,128)S(1)} %copy.10.l_ref), custom_call_target="tpu_custom_call" | custom-call | tf_op jit(solution)/shard_map/pallas_call | solution.py:23
  6.7 2.6 %collective-permute-start.3 = (bf16[320,128]{1,0:T(8,128)(2,1)S(1)}, bf16[320,128]{1,0:T(8,128)(2,1)S(1)}, u32[]{:S(2)}, u32[]{:S(2)}) collective-permute-start(bf16[320,128]{1,0:T(8,128)(2,1)S(1)} %get-tuple-element.29.refs_0_), channel_id=1, source_target_pairs={{0,8},{4,12},{8,0},{12,4},{16,24},{20,28},{24,16},{28,20},{1,9},{5... | collective-permute-start | bytes 245768 | tf_op jit(solution)/shard_map/ppermute | solution.py:240
  9.3 1.5 %collective-permute-start.5 = (bf16[320,128]{1,0:T(8,128)(2,1)S(1)}, bf16[320,128]{1,0:T(8,128)(2,1)S(1)}, u32[]{:S(2)}, u32[]{:S(2)}) collective-permute-start(bf16[320,128]{1,0:T(8,128)(2,1)S(1)} %get-tuple-element.29.refs_0_), channel_id=1, source_target_pairs={{0,16},{4,20},{8,24},{12,28},{16,0},{20,4},{24,8},{28,12},{1,17},{... | collective-permute-start | bytes 245768 | tf_op jit(solution)/shard_map/ppermute | solution.py:240
  10.8 1.2 %collective-permute-done.1.sib_rows = f32[4,640]{1,0:T(4,128)S(1)} collective-permute-done((f32[4,640]{1,0:T(4,128)S(1)}, f32[4,640]{1,0:T(4,128)S(1)}, u32[]{:S(2)}, u32[]{:S(2)}) %collective-permute-start.1) | collective-permute-done | bytes 10272 | tf_op jit(solution)/shard_map/ppermute | solution.py:240
  12.3 1.7 %collective-permute-start.4 = (bf16[320,128]{1,0:T(8,128)(2,1)S(1)}, bf16[320,128]{1,0:T(8,128)(2,1)S(1)}, u32[]{:S(2)}, u32[]{:S(2)}) collective-permute-start(bf16[320,128]{1,0:T(8,128)(2,1)S(1)} %get-tuple-element.30), channel_id=1, source_target_pairs={{0,12},{4,8},{8,4},{12,0},{16,28},{20,24},{24,20},{28,16},{1,13},{... | collective-permute-start | bytes 245768 | tf_op jit(solution)/shard_map/ppermute | solution.py:240
  14.0 0.6 collective-permute-done.5.refs_4_
  14.6 1.0 %collective-permute-start.6 = (bf16[320,128]{1,0:T(8,128)(2,1)S(1)}, bf16[320,128]{1,0:T(8,128)(2,1)S(1)}, u32[]{:S(2)}, u32[]{:S(2)}) collective-permute-start(bf16[320,128]{1,0:T(8,128)(2,1)S(1)} %get-tuple-element.30), channel_id=1, source_target_pairs={{0,20},{4,16},{8,28},{12,24},{16,4},{20,0},{24,12},{28,8},{1,21},{... | collective-permute-start | bytes 245768 | tf_op jit(solution)/shard_map/ppermute | solution.py:240
  16.8 1.7 %collective-permute-done.6.refs_5_ = bf16[320,128]{1,0:T(8,128)(2,1)S(1)} collective-permute-done((bf16[320,128]{1,0:T(8,128)(2,1)S(1)}, bf16[320,128]{1,0:T(8,128)(2,1)S(1)}, u32[]{:S(2)}, u32[]{:S(2)}) %collective-permute-start.6) | collective-permute-done | bytes 81952 | tf_op jit(solution)/shard_map/ppermute | solution.py:240
  18.5 2.4 %collective-permute-done.8.refs_7_ = bf16[320,128]{1,0:T(8,128)(2,1)S(1)} collective-permute-done((bf16[320,128]{1,0:T(8,128)(2,1)S(1)}, bf16[320,128]{1,0:T(8,128)(2,1)S(1)}, u32[]{:S(2)}, u32[]{:S(2)}) %collective-permute-start.8) | collective-permute-done | bytes 81952 | tf_op jit(solution)/shard_map/ppermute | solution.py:240
  20.9 7.9 %shard_map.96 = (bf16[2,640,128]{2,1,0:T(8,128)(2,1)S(1)}, bf16[2,640,128]{2,1,0:T(8,128)(2,1)S(1)}) custom-call(s32[1280]{0:T(1024)S(1)} %copy-done.5, bf16[4,640,128]{2,1,0:T(8,128)(2,1)S(1)} %get-tuple-element.25.own, bf16[4,640,128]{2,1,0:T(8,128)(2,1)S(1)} %collective-permute-done.sib, f32[4,640]{1,0:T(4,128)S(1)} %get-tuple-element.27.own_rows, ...), custom_call_target="tpu_custom_call" | custom-call | tf_op jit(solution)/shard_map/pallas_call | solution.py:23
  28.8 1.1 %collective-permute-start.9 = (bf16[2,640,128]{2,1,0:T(8,128)(2,1)S(1)}, bf16[2,640,128]{2,1,0:T(8,128)(2,1)S(1)}, u32[]{:S(2)}, u32[]{:S(2)}) collective-permute-start(bf16[2,640,128]{2,1,0:T(8,128)(2,1)S(1)} %get-tuple-element.32), channel_id=1, source_target_pairs={{0,4},{4,0},{8,12},{12,8},{16,20},{20,16},{24,28},{28,24},{1,5},{5... | collective-permute-start | bytes 983048 | tf_op jit(solution)/shard_map/ppermute | solution.py:240
  29.9 7.2 %shard_map.98 = (f32[320,128]{1,0:T(8,128)S(1)}, bf16[320,128]{1,0:T(8,128)(2,1)S(1)}, bf16[320,128]{1,0:T(8,128)(2,1)S(1)}, bf16[320,128]{1,0:T(8,128)(2,1)S(1)...) custom-call(s32[1280]{0:T(1024)S(1)} %copy-done.5, ...), custom_call_target="tpu_custom_call" | custom-call | tf_op jit(solution)/shard_map/pallas_call | solution.py:23
  37.2 0.6 collective-permute-start.11
  37.8 1.3 %collective-permute-start.12 = (bf16[320,128]{1,0:T(8,128)(2,1)S(1)}, bf16[320,128]{1,0:T(8,128)(2,1)S(1)}, u32[]{:S(2)}, u32[]{:S(2)}) collective-permute-start(bf16[320,128]{1,0:T(8,128)(2,1)S(1)} %get-tuple-element.36), channel_id=1, source_target_pairs={{0,12},{4,8},{8,4},{12,0},{16,28},{20,24},{24,20},{28,16},{1,13},{... | collective-permute-start | bytes 245768 | tf_op jit(solution)/shard_map/ppermute | solution.py:240
  39.0 0.9 %collective-permute-start.13 = (bf16[320,128]{1,0:T(8,128)(2,1)S(1)}, bf16[320,128]{1,0:T(8,128)(2,1)S(1)}, u32[]{:S(2)}, u32[]{:S(2)}) collective-permute-start(bf16[320,128]{1,0:T(8,128)(2,1)S(1)} %get-tuple-element.37), channel_id=1, source_target_pairs={{0,16},{4,20},{8,24},{12,28},{16,0},{20,4},{24,8},{28,12},{1,17},{... | collective-permute-start | bytes 245768 | tf_op jit(solution)/shard_map/ppermute | solution.py:240
  39.9 0.8 %collective-permute-start.14 = (bf16[320,128]{1,0:T(8,128)(2,1)S(1)}, bf16[320,128]{1,0:T(8,128)(2,1)S(1)}, u32[]{:S(2)}, u32[]{:S(2)}) collective-permute-start(bf16[320,128]{1,0:T(8,128)(2,1)S(1)} %get-tuple-element.38), channel_id=1, source_target_pairs={{0,20},{4,16},{8,28},{12,24},{16,4},{20,0},{24,12},{28,8},{1,21},{... | collective-permute-start | bytes 245768 | tf_op jit(solution)/shard_map/ppermute | solution.py:240
  40.7 1.7 %collective-permute-done.11.refs_1_ = bf16[320,128]{1,0:T(8,128)(2,1)S(1)} collective-permute-done((bf16[320,128]{1,0:T(8,128)(2,1)S(1)}, bf16[320,128]{1,0:T(8,128)(2,1)S(1)}, u32[]{:S(2)}, u32[]{:S(2)}) %collective-permute-start.11) | collective-permute-done | bytes 81952 | tf_op jit(solution)/shard_map/ppermute | solution.py:240
  42.8 0.5 collective-permute-done.12.refs_2_
  43.3 1.0 %collective-permute-start.16 = (bf16[320,128]{1,0:T(8,128)(2,1)S(1)}, bf16[320,128]{1,0:T(8,128)(2,1)S(1)}, u32[]{:S(2)}, u32[]{:S(2)}) collective-permute-start(bf16[320,128]{1,0:T(8,128)(2,1)S(1)} %get-tuple-element.40), channel_id=1, source_target_pairs={{0,28},{4,24},{8,20},{12,16},{16,12},{20,8},{24,4},{28,0},{1,29},{... | collective-permute-start | bytes 245768 | tf_op jit(solution)/shard_map/ppermute | solution.py:240
  44.3 0.8 %collective-permute-done.14.refs_4_ = bf16[320,128]{1,0:T(8,128)(2,1)S(1)} collective-permute-done((bf16[320,128]{1,0:T(8,128)(2,1)S(1)}, bf16[320,128]{1,0:T(8,128)(2,1)S(1)}, u32[]{:S(2)}, u32[]{:S(2)}) %collective-permute-start.14) | collective-permute-done | bytes 81952 | tf_op jit(solution)/shard_map/ppermute | solution.py:240
  45.1 3.3 %collective-permute-done.15.refs_5_ = bf16[320,128]{1,0:T(8,128)(2,1)S(1)} collective-permute-done((bf16[320,128]{1,0:T(8,128)(2,1)S(1)}, bf16[320,128]{1,0:T(8,128)(2,1)S(1)}, u32[]{:S(2)}, u32[]{:S(2)}) %collective-permute-start.15) | collective-permute-done | bytes 81952 | tf_op jit(solution)/shard_map/ppermute | solution.py:240
  48.4 0.6 collective-permute-done.16.refs_6_
  49.1 1.6 %collective-permute-start.17 = (bf16[2,40,256]{2,1,0:T(8,128)(2,1)S(1)}, bf16[2,40,256]{2,1,0:T(8,128)(2,1)S(1)}, u32[]{:S(2)}, u32[]{:S(2)}) collective-permute-start(bf16[2,40,256]{2,1,0:T(8,128)(2,1)S(1)} %get-tuple-element.42), channel_id=1, source_target_pairs={{0,1},{1,0},{2,3},{3,2},{4,5},{5,4},{6,7},{7,6},{8,9},{9,8},{10,11... | collective-permute-start | bytes 122888 | tf_op jit(solution)/shard_map/ppermute | solution.py:240
  50.7 2.6 %collective-permute-start.18 = (bf16[2,40,256]{2,1,0:T(8,128)(2,1)S(1)}, bf16[2,40,256]{2,1,0:T(8,128)(2,1)S(1)}, u32[]{:S(2)}, u32[]{:S(2)}) collective-permute-start(bf16[2,40,256]{2,1,0:T(8,128)(2,1)S(1)} %get-tuple-element.43), channel_id=1, source_target_pairs={{0,2},{1,3},{2,0},{3,1},{4,6},{5,7},{6,4},{7,5},{8,10},{9,11},{10,... | collective-permute-start | bytes 122888 | tf_op jit(solution)/shard_map/ppermute | solution.py:240
  53.5 2.9 %collective-permute-done.18.refs_2_ = bf16[2,40,256]{2,1,0:T(8,128)(2,1)S(1)} collective-permute-done((bf16[2,40,256]{2,1,0:T(8,128)(2,1)S(1)}, bf16[2,40,256]{2,1,0:T(8,128)(2,1)S(1)}, u32[]{:S(2)}, u32[]{:S(2)}) %collective-permute-start.18) | collective-permute-done | bytes 40992 | tf_op jit(solution)/shard_map/ppermute | solution.py:240
  56.5 2.6 %collective-permute-done.19.refs_3_ = bf16[2,40,256]{2,1,0:T(8,128)(2,1)S(1)} collective-permute-done((bf16[2,40,256]{2,1,0:T(8,128)(2,1)S(1)}, bf16[2,40,256]{2,1,0:T(8,128)(2,1)S(1)}, u32[]{:S(2)}, u32[]{:S(2)}) %collective-permute-start.19) | collective-permute-done | bytes 40992 | tf_op jit(solution)/shard_map/ppermute | solution.py:240
  59.1 0.7 %shard_map.100 = (bf16[40,1024]{1,0:T(8,128)(2,1)}, bf16[40,1024]{1,0:T(8,128)(2,1)}) custom-call(bf16[2,40,256]{2,1,0:T(8,128)(2,1)S(1)} %get-tuple-element.41.refs_0_, bf16[2,40,256]{2,1,0:T(8,128)(2,1)S(1)} %collective-permute-done.17.refs_1_, bf16[2,40,256]{2,1,0:T(8,128)(2,1)S(1)} %collective-permute-done.18.refs_2_, ...), custom_call_target="tpu_custom_call" | custom-call | tf_op jit(solution)/shard_map/pallas_call | solution.py:23
  59.8 1.0 %shard_map.97 = bf16[160,2048]{1,0:T(8,128)(2,1)} custom-call(bf16[2,640,128]{2,1,0:T(8,128)(2,1)S(1)} %get-tuple-element.31.own, bf16[2,640,128]{2,1,0:T(8,128)(2,1)S(1)} %collective-permute-done.9.other), custom_call_target="tpu_custom_call" | custom-call | tf_op jit(solution)/shard_map/pallas_call | solution.py:23
  (28 shorter events, 2.8 us)
Async XLA Ops:
  1.4 1.1 %copy-start = (bf16[160,2048]{1,0:T(8,128)(2,1)S(1)}, bf16[160,2048]{1,0:T(8,128)(2,1)}, u32[]{:S(2)}) copy-start(bf16[160,2048]{1,0:T(8,128)(2,1)} %q_ref.1) | copy-start | bytes 1966084
  2.5 1.1 %copy-start.1 = (bf16[160,2048]{1,0:T(8,128)(2,1)S(1)}, bf16[160,2048]{1,0:T(8,128)(2,1)}, u32[]{:S(2)}) copy-start(bf16[160,2048]{1,0:T(8,128)(2,1)} %g_ref.1) | copy-start | bytes 1966084
  3.6 1.1 %copy-start.2 = (bf16[160,2048]{1,0:T(8,128)(2,1)S(1)}, bf16[160,2048]{1,0:T(8,128)(2,1)}, u32[]{:S(2)}) copy-start(bf16[160,2048]{1,0:T(8,128)(2,1)} %o_ref.1) | copy-start | bytes 1966084
  4.7 1.9 %copy-start.3 = (bf16[160,256]{1,0:T(8,128)(2,1)S(1)}, bf16[160,256]{1,0:T(8,128)(2,1)}, u32[]{:S(2)}) copy-start(bf16[160,256]{1,0:T(8,128)(2,1)} %k_ref.1) | copy-start | bytes 245764
  4.7 1.9 %copy-start.4 = (bf16[160,256]{1,0:T(8,128)(2,1)S(1)}, bf16[160,256]{1,0:T(8,128)(2,1)}, u32[]{:S(2)}) copy-start(bf16[160,256]{1,0:T(8,128)(2,1)} %v_ref.1) | copy-start | bytes 245764
  6.1 14.8 %collective-permute-start = (bf16[4,640,128]{2,1,0:T(8,128)(2,1)S(1)}, bf16[4,640,128]{2,1,0:T(8,128)(2,1)S(1)}, u32[]{:S(2)}, u32[]{:S(2)}) collective-permute-start(bf16[4,640,128]{2,1,0:T(8,128)(2,1)S(1)} %get-tuple-element.26), channel_id=1, source_target_pairs={{0,4},{4,0},{8,12},{12,8},{16,20},{20,16},{24,28},{28,24},{1,5},{5... | collective-permute-start | bytes 1966088 | tf_op jit(solution)/shard_map/ppermute | solution.py:240
  6.6 14.2 %copy-start.5 = (s32[1280]{0:T(1024)S(1)}, s32[1280]{0:T(1024)}, u32[]{:S(2)}) copy-start(s32[1280]{0:T(1024)} %pos_ref.3) | copy-start | bytes 15364
  6.7 5.7 %collective-permute-start.3 = (bf16[320,128]{1,0:T(8,128)(2,1)S(1)}, bf16[320,128]{1,0:T(8,128)(2,1)S(1)}, u32[]{:S(2)}, u32[]{:S(2)}) collective-permute-start(bf16[320,128]{1,0:T(8,128)(2,1)S(1)} %get-tuple-element.29.refs_0_), channel_id=1, source_target_pairs={{0,8},{4,12},{8,0},{12,4},{16,24},{20,28},{24,16},{28,20},{1,9},{5... | collective-permute-start | bytes 245768 | tf_op jit(solution)/shard_map/ppermute | solution.py:240
  9.3 5.4 %collective-permute-start.5 = (bf16[320,128]{1,0:T(8,128)(2,1)S(1)}, bf16[320,128]{1,0:T(8,128)(2,1)S(1)}, u32[]{:S(2)}, u32[]{:S(2)}) collective-permute-start(bf16[320,128]{1,0:T(8,128)(2,1)S(1)} %get-tuple-element.29.refs_0_), channel_id=1, source_target_pairs={{0,16},{4,20},{8,24},{12,28},{16,0},{20,4},{24,8},{28,12},{1,17},{... | collective-permute-start | bytes 245768 | tf_op jit(solution)/shard_map/ppermute | solution.py:240
  10.8 5.3 %collective-permute-start.7 = (bf16[320,128]{1,0:T(8,128)(2,1)S(1)}, bf16[320,128]{1,0:T(8,128)(2,1)S(1)}, u32[]{:S(2)}, u32[]{:S(2)}) collective-permute-start(bf16[320,128]{1,0:T(8,128)(2,1)S(1)} %get-tuple-element.29.refs_0_), channel_id=1, source_target_pairs={{0,24},{4,28},{8,16},{12,20},{16,8},{20,12},{24,0},{28,4},{1,25},{... | collective-permute-start | bytes 245768 | tf_op jit(solution)/shard_map/ppermute | solution.py:240
  10.8 1.2 %collective-permute-start.1 = (f32[4,640]{1,0:T(4,128)S(1)}, f32[4,640]{1,0:T(4,128)S(1)}, u32[]{:S(2)}, u32[]{:S(2)}) collective-permute-start(f32[4,640]{1,0:T(4,128)S(1)} %get-tuple-element.28), channel_id=1, source_target_pairs={{0,4},{4,0},{8,12},{12,8},{16,20},{20,16},{24,28},{28,24},{1,5},{5... | collective-permute-start | bytes 30728 | tf_op jit(solution)/shard_map/ppermute | solution.py:240
  12.0 4.4 %collective-permute-start.2 = (bf16[320,128]{1,0:T(8,128)(2,1)S(1)}, bf16[320,128]{1,0:T(8,128)(2,1)S(1)}, u32[]{:S(2)}, u32[]{:S(2)}) collective-permute-start(bf16[320,128]{1,0:T(8,128)(2,1)S(1)} %get-tuple-element.30), channel_id=1, source_target_pairs={{0,4},{4,0},{8,12},{12,8},{16,20},{20,16},{24,28},{28,24},{1,5},{5... | collective-permute-start | bytes 245768 | tf_op jit(solution)/shard_map/ppermute | solution.py:240
  12.3 4.4 %collective-permute-start.4 = (bf16[320,128]{1,0:T(8,128)(2,1)S(1)}, bf16[320,128]{1,0:T(8,128)(2,1)S(1)}, u32[]{:S(2)}, u32[]{:S(2)}) collective-permute-start(bf16[320,128]{1,0:T(8,128)(2,1)S(1)} %get-tuple-element.30), channel_id=1, source_target_pairs={{0,12},{4,8},{8,4},{12,0},{16,28},{20,24},{24,20},{28,16},{1,13},{... | collective-permute-start | bytes 245768 | tf_op jit(solution)/shard_map/ppermute | solution.py:240
  14.6 3.9 %collective-permute-start.6 = (bf16[320,128]{1,0:T(8,128)(2,1)S(1)}, bf16[320,128]{1,0:T(8,128)(2,1)S(1)}, u32[]{:S(2)}, u32[]{:S(2)}) collective-permute-start(bf16[320,128]{1,0:T(8,128)(2,1)S(1)} %get-tuple-element.30), channel_id=1, source_target_pairs={{0,20},{4,16},{8,28},{12,24},{16,4},{20,0},{24,12},{28,8},{1,21},{... | collective-permute-start | bytes 245768 | tf_op jit(solution)/shard_map/ppermute | solution.py:240
  16.1 4.8 %collective-permute-start.8 = (bf16[320,128]{1,0:T(8,128)(2,1)S(1)}, bf16[320,128]{1,0:T(8,128)(2,1)S(1)}, u32[]{:S(2)}, u32[]{:S(2)}) collective-permute-start(bf16[320,128]{1,0:T(8,128)(2,1)S(1)} %get-tuple-element.30), channel_id=1, source_target_pairs={{0,28},{4,24},{8,20},{12,16},{16,12},{20,8},{24,4},{28,0},{1,29},{... | collective-permute-start | bytes 245768 | tf_op jit(solution)/shard_map/ppermute | solution.py:240
  28.8 31.0 %collective-permute-start.9 = (bf16[2,640,128]{2,1,0:T(8,128)(2,1)S(1)}, bf16[2,640,128]{2,1,0:T(8,128)(2,1)S(1)}, u32[]{:S(2)}, u32[]{:S(2)}) collective-permute-start(bf16[2,640,128]{2,1,0:T(8,128)(2,1)S(1)} %get-tuple-element.32), channel_id=1, source_target_pairs={{0,4},{4,0},{8,12},{12,8},{16,20},{20,16},{24,28},{28,24},{1,5},{5... | collective-permute-start | bytes 983048 | tf_op jit(solution)/shard_map/ppermute | solution.py:240
  37.1 2.8 %collective-permute-start.10 = (bf16[320,128]{1,0:T(8,128)(2,1)S(1)}, bf16[320,128]{1,0:T(8,128)(2,1)S(1)}, u32[]{:S(2)}, u32[]{:S(2)}) collective-permute-start(bf16[320,128]{1,0:T(8,128)(2,1)S(1)} %get-tuple-element.34), channel_id=1, source_target_pairs={{0,4},{4,0},{8,12},{12,8},{16,20},{20,16},{24,28},{28,24},{1,5},{5... | collective-permute-start | bytes 245768 | tf_op jit(solution)/shard_map/ppermute | solution.py:240
  37.2 5.3 %collective-permute-start.11 = (bf16[320,128]{1,0:T(8,128)(2,1)S(1)}, bf16[320,128]{1,0:T(8,128)(2,1)S(1)}, u32[]{:S(2)}, u32[]{:S(2)}) collective-permute-start(bf16[320,128]{1,0:T(8,128)(2,1)S(1)} %get-tuple-element.35), channel_id=1, source_target_pairs={{0,8},{4,12},{8,0},{12,4},{16,24},{20,28},{24,16},{28,20},{1,9},{5... | collective-permute-start | bytes 245768 | tf_op jit(solution)/shard_map/ppermute | solution.py:240
  37.8 5.6 %collective-permute-start.12 = (bf16[320,128]{1,0:T(8,128)(2,1)S(1)}, bf16[320,128]{1,0:T(8,128)(2,1)S(1)}, u32[]{:S(2)}, u32[]{:S(2)}) collective-permute-start(bf16[320,128]{1,0:T(8,128)(2,1)S(1)} %get-tuple-element.36), channel_id=1, source_target_pairs={{0,12},{4,8},{8,4},{12,0},{16,28},{20,24},{24,20},{28,16},{1,13},{... | collective-permute-start | bytes 245768 | tf_op jit(solution)/shard_map/ppermute | solution.py:240
  39.0 5.3 %collective-permute-start.13 = (bf16[320,128]{1,0:T(8,128)(2,1)S(1)}, bf16[320,128]{1,0:T(8,128)(2,1)S(1)}, u32[]{:S(2)}, u32[]{:S(2)}) collective-permute-start(bf16[320,128]{1,0:T(8,128)(2,1)S(1)} %get-tuple-element.37), channel_id=1, source_target_pairs={{0,16},{4,20},{8,24},{12,28},{16,0},{20,4},{24,8},{28,12},{1,17},{... | collective-permute-start | bytes 245768 | tf_op jit(solution)/shard_map/ppermute | solution.py:240
  39.9 5.2 %collective-permute-start.14 = (bf16[320,128]{1,0:T(8,128)(2,1)S(1)}, bf16[320,128]{1,0:T(8,128)(2,1)S(1)}, u32[]{:S(2)}, u32[]{:S(2)}) collective-permute-start(bf16[320,128]{1,0:T(8,128)(2,1)S(1)} %get-tuple-element.38), channel_id=1, source_target_pairs={{0,20},{4,16},{8,28},{12,24},{16,4},{20,0},{24,12},{28,8},{1,21},{... | collective-permute-start | bytes 245768 | tf_op jit(solution)/shard_map/ppermute | solution.py:240
  42.5 5.9 %collective-permute-start.15 = (bf16[320,128]{1,0:T(8,128)(2,1)S(1)}, bf16[320,128]{1,0:T(8,128)(2,1)S(1)}, u32[]{:S(2)}, u32[]{:S(2)}) collective-permute-start(bf16[320,128]{1,0:T(8,128)(2,1)S(1)} %get-tuple-element.39), channel_id=1, source_target_pairs={{0,24},{4,28},{8,16},{12,20},{16,8},{20,12},{24,0},{28,4},{1,25},{... | collective-permute-start | bytes 245768 | tf_op jit(solution)/shard_map/ppermute | solution.py:240
  43.3 5.6 %collective-permute-start.16 = (bf16[320,128]{1,0:T(8,128)(2,1)S(1)}, bf16[320,128]{1,0:T(8,128)(2,1)S(1)}, u32[]{:S(2)}, u32[]{:S(2)}) collective-permute-start(bf16[320,128]{1,0:T(8,128)(2,1)S(1)} %get-tuple-element.40), channel_id=1, source_target_pairs={{0,28},{4,24},{8,20},{12,16},{16,12},{20,8},{24,4},{28,0},{1,29},{... | collective-permute-start | bytes 245768 | tf_op jit(solution)/shard_map/ppermute | solution.py:240
  49.1 4.5 %collective-permute-start.17 = (bf16[2,40,256]{2,1,0:T(8,128)(2,1)S(1)}, bf16[2,40,256]{2,1,0:T(8,128)(2,1)S(1)}, u32[]{:S(2)}, u32[]{:S(2)}) collective-permute-start(bf16[2,40,256]{2,1,0:T(8,128)(2,1)S(1)} %get-tuple-element.42), channel_id=1, source_target_pairs={{0,1},{1,0},{2,3},{3,2},{4,5},{5,4},{6,7},{7,6},{8,9},{9,8},{10,11... | collective-permute-start | bytes 122888 | tf_op jit(solution)/shard_map/ppermute | solution.py:240
  50.7 5.8 %collective-permute-start.18 = (bf16[2,40,256]{2,1,0:T(8,128)(2,1)S(1)}, bf16[2,40,256]{2,1,0:T(8,128)(2,1)S(1)}, u32[]{:S(2)}, u32[]{:S(2)}) collective-permute-start(bf16[2,40,256]{2,1,0:T(8,128)(2,1)S(1)} %get-tuple-element.43), channel_id=1, source_target_pairs={{0,2},{1,3},{2,0},{3,1},{4,6},{5,7},{6,4},{7,5},{8,10},{9,11},{10,... | collective-permute-start | bytes 122888 | tf_op jit(solution)/shard_map/ppermute | solution.py:240
  53.3 5.8 %collective-permute-start.19 = (bf16[2,40,256]{2,1,0:T(8,128)(2,1)S(1)}, bf16[2,40,256]{2,1,0:T(8,128)(2,1)S(1)}, u32[]{:S(2)}, u32[]{:S(2)}) collective-permute-start(bf16[2,40,256]{2,1,0:T(8,128)(2,1)S(1)} %get-tuple-element.44), channel_id=1, source_target_pairs={{0,3},{1,2},{2,1},{3,0},{4,7},{5,6},{6,5},{7,4},{8,11},{9,10},{10,... | collective-permute-start | bytes 122888 | tf_op jit(solution)/shard_map/ppermute | solution.py:240

commit v2 on v1

v2 whole, which is shorter than its diff:
```python
import functools
import math

import jax
import jax.numpy as jnp
from jax import lax
from jax.experimental import pallas as pl
from jax.experimental.pallas import tpu as pltpu
from jax.sharding import PartitionSpec as P

HEAD_SIZE = 128
SCALE = 1.0 / math.sqrt(HEAD_SIZE)
EXP2_SCALE = SCALE * math.log2(math.e)
FLOPS_PER_US = 1.1e9
LOG2E = math.log2(math.e)
F32 = jnp.float32
BF16 = jnp.bfloat16
VMEM = pl.BlockSpec(memory_space=pltpu.VMEM)
ANY = pl.BlockSpec(memory_space=pl.ANY)
HBM = pl.BlockSpec(memory_space=pltpu.HBM)
SMEM = pl.BlockSpec(memory_space=pltpu.SMEM)


def call(kernel, outs, ins, scratch=(), smem=0, cost=0.1, far=(), after=()):
    ins = list(ins) + [pltpu.with_memory_space_constraint(x, pltpu.HBM) for x in far]
    specs = [SMEM] * smem + [VMEM] * (len(ins) - smem - len(far))
    specs += [HBM] * len(far) + [ANY] * len(after)
    moved = sum(x.size * x.dtype.itemsize for x in ins)
    count = len(ins)
    ins = list(ins) + list(after)

    def body(*refs):
        kernel(*refs[:count], *refs[len(ins) :])

    return pl.pallas_call(
        body,
        cost_estimate=pl.CostEstimate(
            flops=int(cost * FLOPS_PER_US), bytes_accessed=moved, transcendentals=0
        ),
        in_specs=specs,
        out_specs=[VMEM] * len(outs),
        out_shape=[jax.ShapeDtypeStruct(shape, dtype) for shape, dtype in outs],
        scratch_shapes=list(scratch),
        compiler_params=pltpu.CompilerParams(vmem_limit_bytes=48 * 2**20),
    )(*ins)


def nt(a, b):
    return lax.dot_general(a, b, (((1,), (1,)), ((), ())), preferred_element_type=F32)


def parity():
    return lax.rem(lax.axis_index("ctx"), 2)


def columns(head):
    return pl.ds(pl.multiple_of(head * HEAD_SIZE, HEAD_SIZE), HEAD_SIZE)


def copy_all(pairs, sems):
    copies = [
        pltpu.make_async_copy(src, dst, sems.at[i]) for i, (src, dst) in enumerate(pairs)
    ]
    for each in copies:
        each.start()
    for each in copies:
        each.wait()


def pack_kv_kernel(k_hbm, v_hbm, same, other, sems):
    rows = k_hbm.shape[0]
    c = parity()
    pairs = [
        (src.at[:, columns(group)], ref.at[pl.ds(kind * rows, rows), :])
        for ref, group in ((other, 1 - c), (same, c))
        for kind, src in enumerate((k_hbm, v_hbm))
    ]
    copy_all(pairs, sems)


def run_starts(pos_ref, tokens, shift):
    ctx = lax.axis_index("ctx")
    return pos_ref[jnp.bitwise_xor(ctx, shift) * tokens]


def pack_q_kernel(heads, q_hbm, g_hbm, o_hbm, pos_hbm, out, larger, pos, sems):
    tokens = q_hbm.shape[0]
    half = tokens // 2
    group = 1 - parity()
    pairs = [(pos_hbm, pos)] + [
        (
            src.at[pl.ds(w * half, half), columns(group * heads + h)],
            out.at[2 * kind + w, pl.ds(h * half, half), :],
        )
        for kind, src in enumerate((q_hbm, g_hbm, o_hbm))
        for w in range(2)
        for h in range(heads)
    ]
    copy_all(pairs, sems)
    for m in range(larger.shape[0] // 2):
        for b in range(2):
            flag = jnp.where(run_starts(pos, tokens, m) > run_starts(pos, tokens, b), 1.0, 0.0)
            larger[2 * m + b : 2 * m + b + 1, :] = jnp.full((1, HEAD_SIZE), flag, F32)


def split_bf16(x, terms):
    parts = []
    for _ in range(terms):
        part = x.astype(BF16)
        parts.append(part)
        x = x - part.astype(F32)
    return parts


def rows_kernel(heads, q_ref, g_ref, o_ref, own_log, sib, sib_log, kv, *refs):
    out, own, own_t, sib_t, kv_out = refs
    lanes = own.shape[1]
    half = lanes // heads
    c = parity()
    ones = jnp.ones((8, HEAD_SIZE), BF16)
    groups, tokens = own_log.shape
    token = lax.broadcasted_iota(jnp.int32, (tokens, lanes), 0)
    lane = lax.broadcasted_iota(jnp.int32, (tokens, lanes), 1)
    head = lax.broadcasted_iota(jnp.int32, (groups, lanes), 0)
    wanted = lax.div(lax.broadcasted_iota(jnp.int32, (groups, lanes), 1), half) + c * heads

    def stacked(ref, w):
        r = slice(w * half, (w + 1) * half)
        return jnp.concatenate([ref[r, columns(c * heads + h)] for h in range(heads)], axis=0)

    for b, (log, turned) in enumerate(((own_log, own_t), (sib_log, sib_t))):
        parts = split_bf16(jnp.clip(log[...], -1e30, 1e30), 3)
        for w in range(2):
            if b == 0:
                q, g, o = (stacked(ref, w) for ref in (q_ref, g_ref, o_ref))
                own[w] = q
                own[2 + w] = g
            else:
                q, g, o = (sib[2 * kind + w] for kind in range(3))
            turned[w] = q.T
            turned[2 + w] = g.T
            place = jnp.where(token == lax.rem(lane, half) + w * half, 1.0, 0.0).astype(BF16)
            spread = sum(jnp.dot(part, place, preferred_element_type=F32) for part in parts)
            row = jnp.sum(jnp.where(head == wanted, spread, 0.0), axis=0, keepdims=True)
            out[4 * b + w : 4 * b + w + 1, :] = row * LOG2E
            delta = g.astype(F32) * o.astype(F32)
            row = sum(nt(ones, part) for part in split_bf16(delta, 2))
            out[4 * b + 2 + w : 4 * b + 3 + w, :] = row[0:1]
    kv_out[...] = kv[...]


def seen_in_run(half, lanes):
    key_row = lax.broadcasted_iota(jnp.int32, (half, lanes), 0)
    query_row = lax.rem(lax.broadcasted_iota(jnp.int32, (half, lanes), 1), half)
    return key_row <= query_row


def probs_and_grads(k, v, turned, vec, at, which, mask=None):
    s = jnp.dot(k, turned[which], preferred_element_type=F32)
    p = jnp.exp2(s * EXP2_SCALE - vec[pl.ds(at + which, 1), :])
    if mask is not None:
        p = jnp.where(mask, p, 0.0)
    dp = jnp.dot(v, turned[2 + which], preferred_element_type=F32)
    return p, (p * (dp - vec[pl.ds(at + 2 + which, 1), :])).astype(BF16)


def first_runs(piece, tokens, half):
    rows = piece.shape[0] // 2

    def both(at):
        return jnp.concatenate(
            [piece[at + a * tokens : at + a * tokens + half, :] for a in range(2)], axis=0
        )

    return both(0), both(rows)


def one_run(piece, tokens, half, a, which):
    at = a * tokens + which * half
    if not isinstance(which, int):
        at = pl.multiple_of(at, half)
    rows = piece.shape[0] // 2
    return piece[pl.ds(at, half), :], piece[pl.ds(rows + at, half), :]


def is_larger(larger, pair, a, b):
    at = 4 * pair + 2 * a + b
    return jnp.max(larger[at : at + 1, :]) > 0.5


def kv_grad_kernel(pair, larger, own, sib, own_t, sib_t, vec, piece, out):
    tokens = piece.shape[0] // 4
    half = tokens // 2
    rows = 2 * tokens
    sides = ((own, own_t), (sib, sib_t))

    def terms(k, v, b, which, mask=None):
        stack, turned = sides[b]
        p, ds = probs_and_grads(k, v, turned, vec, 4 * b, which, mask)
        return (
            jnp.dot(ds, stack[which], preferred_element_type=F32),
            jnp.dot(p.astype(BF16), stack[2 + which], preferred_element_type=F32),
        )

    sums = {(a, w): [] for a in range(2) for w in range(2)}
    k, v = first_runs(piece, tokens, half)
    for b in range(2):
        both = terms(k, v, b, 1)
        for a in range(2):
            sums[a, 0].append([x[a * half : (a + 1) * half] for x in both])
    seen = seen_in_run(half, own.shape[1]) if pair == 0 else None
    for a in range(2):
        for b in range(2):
            if pair == 0 and a == b:
                for w in range(2):
                    k, v = one_run(piece, tokens, half, a, w)
                    sums[a, w].append(terms(k, v, b, w, seen))
                continue
            second = is_larger(larger, pair, a, b)
            which = jnp.where(second, 1, 0)
            k, v = one_run(piece, tokens, half, a, which)
            both = terms(k, v, b, which)
            sums[a, 0].append([jnp.where(second, 0.0, x) for x in both])
            sums[a, 1].append([jnp.where(second, x, 0.0) for x in both])
    for (a, w), parts in sums.items():
        at = a * tokens + w * half
        out[at : at + half, :] = (sum(x[0] for x in parts) * SCALE).astype(out.dtype)
        out[rows + at : rows + at + half, :] = sum(x[1] for x in parts).astype(out.dtype)


def q_grad_kernel(b, larger, turned, vec, *refs):
    pieces, (out, acc) = refs[:-2], refs[-2:]
    tokens = pieces[0].shape[0] // 4
    half = tokens // 2
    acc[...] = jnp.zeros_like(acc)

    def add(k, v, which, mask=None):
        _, ds = probs_and_grads(k, v, turned, vec, 4 * b, which, mask)
        acc[which] += jnp.dot(k.T, ds, preferred_element_type=F32)

    for pair, piece in enumerate(pieces):
        add(*first_runs(piece, tokens, half), 1)
        for a in range(2):
            if pair == 0 and a == b:
                seen = seen_in_run(half, turned.shape[2])
                for w in range(2):
                    add(*one_run(piece, tokens, half, a, w), w, seen)
                continue
            which = jnp.where(is_larger(larger, pair, a, b), 1, 0)
            add(*one_run(piece, tokens, half, a, which), which)
    for w in range(2):
        out[w] = (acc[w] * SCALE).T.astype(BF16)


def merge_kv_kernel(same_ref, other_ref, log, out, log_out):
    log_out[...] = log[...]
    tokens = same_ref.shape[0] // 2
    for a, ref in enumerate((same_ref, other_ref)):
        for kind in range(2):
            at = (2 * kind + a) * tokens
            out[at : at + tokens, :] = ref[kind * tokens : (kind + 1) * tokens, :]


def sum_kernel(*refs):
    parts, (same_out, other_out) = refs[:-2], refs[-2:]
    tokens = parts[0].shape[0] // 4
    for a, out in enumerate((same_out, other_out)):
        for kind in range(2):
            at = (2 * kind + a) * tokens
            value = parts[0][at : at + tokens, :]
            for part in parts[1:]:
                value = value + part[at : at + tokens, :].astype(F32)
            out[kind * tokens : (kind + 1) * tokens, :] = value.astype(BF16)


def share_kernel(tp_count, same, other, *refs):
    outs, (total,) = refs[:tp_count], refs[tp_count:]
    tokens = same.shape[0] // 2
    share = tokens // tp_count
    c = parity()
    z = lax.axis_index("tp")
    for ref, group in ((same, c), (other, 1 - c)):
        cols = pl.ds(pl.multiple_of(group * HEAD_SIZE, HEAD_SIZE), HEAD_SIZE)
        total[:, cols] = ref[...].astype(F32)
    for m, out in enumerate(outs):
        start = jnp.bitwise_xor(z, m) * share
        for kind in range(2):
            r = pl.ds(pl.multiple_of(kind * tokens + start, 8), share)
            out[kind] = total[r, :].astype(BF16)


def spread_kernel(tp_count, *refs):
    parts, (key_out, value_out) = refs[:tp_count], refs[tp_count:]
    z = lax.axis_index("tp")
    width = parts[0].shape[2]
    for m, part in enumerate(parts):
        cols = pl.ds(pl.multiple_of(jnp.bitwise_xor(z, m) * width, width), width)
        key_out[:, cols] = part[0]
        value_out[:, cols] = part[1]


def unstack_kernel(heads, own, other, out):
    half = out.shape[0] // 2
    c = parity()
    for ref, group in ((own, c), (other, 1 - c)):
        for w in range(2):
            for h in range(heads):
                cols = pl.ds(
                    pl.multiple_of((group * heads + h) * HEAD_SIZE, HEAD_SIZE), HEAD_SIZE
                )
                out[w * half : (w + 1) * half, cols] = ref[w, h * half : (h + 1) * half, :]


def swap(x, axis, shift):
    count = lax.axis_size(axis)
    return lax.ppermute(x, axis, [(i, i ^ shift) for i in range(count)])


def on_device(positions, queries, keys, values, attn_output, output_grad, log_sums):
    n = lax.axis_size("ctx")
    tp_count = lax.axis_size("tp")
    tokens = queries.shape[0]
    half = tokens // 2
    heads = log_sums.shape[1] // 2
    lanes = heads * half

    half_piece = ((2 * tokens, HEAD_SIZE), BF16)
    piece = ((4 * tokens, HEAD_SIZE), BF16)
    stack = ((6, lanes, HEAD_SIZE), BF16)
    kv_same, kv_other = call(
        pack_kv_kernel,
        [half_piece] * 2,
        [],
        [pltpu.SemaphoreType.DMA((4,))],
        far=[keys, values],
    )
    other, larger = call(
        functools.partial(pack_q_kernel, heads),
        [stack, ((2 * n, HEAD_SIZE), F32)],
        [],
        [pltpu.SMEM(positions.shape, jnp.int32), pltpu.SemaphoreType.DMA((6 * heads + 1,))],
        cost=1.0,
        far=[queries, output_grad, attn_output, positions],
        after=[kv_same],
    )
    kv_pair, other = lax.optimization_barrier((swap(kv_other, "ctx", 1), other))
    kv_chip, logs = call(
        merge_kv_kernel,
        [piece, (log_sums.T.shape, F32)],
        [kv_same, kv_pair, log_sums.T],
    )
    sib = swap(other, "ctx", 1)
    turned = ((4, HEAD_SIZE, lanes), BF16)
    vec, own, own_t, sib_t, kv_late = call(
        functools.partial(rows_kernel, heads),
        [((8, lanes), F32), ((4, lanes, HEAD_SIZE), BF16), turned, turned, piece],
        [queries, output_grad, attn_output, logs, sib, swap(logs, "ctx", 1), kv_chip],
        cost=1.0,
    )
    late = n // 2 - 1
    pieces = [kv_chip] + [
        swap(kv_late if pair == late else kv_chip, "ctx", 2 * pair) for pair in range(1, n // 2)
    ]

    def kv_grads(pair, after=()):
        (out,) = call(
            functools.partial(kv_grad_kernel, pair),
            [(piece[0], BF16 if pair else F32)],
            [larger, own, sib, own_t, sib_t, vec, pieces[pair]],
            cost=0.5,
            after=after,
        )
        return out

    partials = [kv_grads(pair) for pair in range(1, n // 2)]
    received = [swap(x, "ctx", 2 * pair + 2) for pair, x in enumerate(partials)]
    local = kv_grads(0, partials[-1:])

    def q_grads(member, member_t, after=()):
        (out,) = call(
            functools.partial(q_grad_kernel, member),
            [((2, lanes, HEAD_SIZE), BF16)],
            [larger, member_t, vec] + pieces,
            [pltpu.VMEM((2, HEAD_SIZE, lanes), F32)],
            cost=2.5,
            after=after,
        )
        return out

    dq_sib = q_grads(1, sib_t)
    dq_other = swap(dq_sib, "ctx", 1)
    sum_same, sum_other = call(
        sum_kernel, [half_piece] * 2, [local] + received, after=[dq_sib]
    )
    share = ((2, tokens // tp_count, 2 * HEAD_SIZE), BF16)
    shares = call(
        functools.partial(share_kernel, tp_count),
        [share] * tp_count,
        [sum_same, swap(sum_other, "ctx", 1)],
        [pltpu.VMEM((2 * tokens, 2 * HEAD_SIZE), F32)],
    )
    dq_own = q_grads(0, own_t, [shares[0]])
    (query_grad,) = call(
        functools.partial(unstack_kernel, heads),
        [(queries.shape, BF16)],
        [dq_own, dq_other],
        cost=1.0,
    )

    shares = [shares[0]] + [swap(shares[m], "tp", m) for m in range(1, tp_count)]
    final = ((tokens // tp_count, 2 * HEAD_SIZE * tp_count), BF16)
    key_grad, value_grad = call(
        functools.partial(spread_kernel, tp_count), [final] * 2, shares, after=[pltpu.with_memory_space_constraint(query_grad, pltpu.HBM)]
    )
    return (query_grad, key_grad, value_grad)


def solution(mesh):
    split = P("ctx", "tp")
    rows = P(("ctx", "tp"), None)
    return jax.shard_map(
        on_device,
        mesh=mesh,
        in_specs=(P(), split, split, split, split, split, split),
        out_specs=(split, rows, rows),
        check_vma=False,
    )
```

time: 61.1 us -> 40.6 us (0.66)
  waiting for transfers between devices: 19.4 us -> 4.06 us
  local copies, waits for them, and re-layouts: 4.09 us -> 0.01 us
  starting transfers between devices: 18.3 us -> 15.3 us
  Pallas kernels: 18.2 us -> 20.3 us
    ppermute x20 -> x14, waiting for transfers between devices: 19.4 us -> 4.06 us  [swap(): return lax.ppermute(x, axis, [(i, i ^ shift) for i in range(count)])]
    unnamed x13 -> x8, local copies, waits for them, and re-layouts: 4.09 us -> 0.01 us
    ppermute x20 -> x14, starting transfers between devices: 18.3 us -> 15.3 us  [swap(): return lax.ppermute(x, axis, [(i, i ^ shift) for i in range(count)])]
    pallas_call x7 -> x14, Pallas kernels: 18.2 us -> 20.3 us  [call(): pl.pallas_call(body, cost_estimate=pl.CostEstimate(flops=int(cost * FLOPS...]
  transfers between devices with their start and end apart: 20 -> 14, of which waited for: 14 -> 5; matrix products, arithmetic and copies ran while one was open for 0% -> 0% of each run, Pallas kernels for 13% -> 46%
where the time goes in v2:
time: 40.6 us; the launch traced here: 40.4 us
  Pallas kernels  20.3 us (50%)
  starting transfers between devices  15.3 us (38%)
  waiting for transfers between devices  4.06 us (10%)
  between operations  0.77 us (2%)
    pallas_call x14, Pallas kernels, call(): pl.pallas_call(body, cost_estimate=pl.CostEstimate(flops=int(cost * FLOPS...  20.3 us
    ppermute x14, starting transfers between devices, swap(): return lax.ppermute(x, axis, [(i, i ^ shift) for i in range(count)])  15.3 us
    ppermute x14, waiting for transfers between devices, swap(): return lax.ppermute(x, axis, [(i, i ^ shift) for i in range(count)])  4.06 us
  transfers between devices with their start and end apart: 14, of which 5 were waited for; matrix products, arithmetic and copies ran while one was open for 0% of the time, Pallas kernels for 46%

profile of v2, /device:TPU:0, one launch (start us, length us, event | category | flops | bytes accessed | tf_op | source)
XLA Modules:
  0.0 40.4 jit_solution(14072718955227734112)
XLA Ops:
  0.6 0.9 %shard_map.94 = (bf16[320,128]{1,0:T(8,128)(2,1)S(1)}, bf16[320,128]{1,0:T(8,128)(2,1)S(1)}) custom-call(bf16[160,256]{1,0:T(8,128)(2,1)} %refs_0_.3, bf16[160,256]{1,0:T(8,128)(2,1)} %refs_1_.3), custom_call_target="tpu_custom_call" | custom-call | flops 110000000 | bytes 163840 | tf_op jit(solution)/shard_map/pallas_call | solution.py:35
  1.5 0.5 %collective-permute-start = (bf16[320,128]{1,0:T(8,128)(2,1)S(1)}, bf16[320,128]{1,0:T(8,128)(2,1)S(1)}, u32[]{:S(2)}, u32[]{:S(2)}) collective-permute-start(bf16[320,128]{1,0:T(8,128)(2,1)S(1)} %get-tuple-element.26), channel_id=1, source_target_pairs={{0,4},{4,0},{8,12},{12,8},{16,20},{20,16},{24,28},{28,24},{1,5},{5... | collective-permute-start | bytes 245768 | tf_op jit(solution)/shard_map/ppermute | solution.py:316
  2.1 1.7 %shard_map.95 = (bf16[6,640,128]{2,1,0:T(8,128)(2,1)S(1)}, f32[16,128]{1,0:T(8,128)S(1)}) custom-call(bf16[160,2048]{1,0:T(8,128)(2,1)} %refs_0_.5, bf16[160,2048]{1,0:T(8,128)(2,1)} %refs_1_.5, bf16[160,2048]{1,0:T(8,128)(2,1)} %refs_2_.3, s32[1280]{0:T(1024)} %refs_3_.1, bf16[320,128]{1,0:T(8,128)(2,1)S(1)} %get-tuple-element.24.refs_4_.refs_0_), custom_call_target="tpu_custom_call" | custom-call | flops 1100000000 | bytes 1971200 | tf_op jit(solution)/shard_map/pallas_call | solution.py:35
  3.8 0.1 collective-permute-start.1
  4.0 0.5 %collective-permute-start.2 = (f32[16,160]{1,0:T(8,128)S(1)}, f32[16,160]{1,0:T(8,128)S(1)}, u32[]{:S(2)}, u32[]{:S(2)}) collective-permute-start(f32[16,160]{1,0:T(8,128)S(1)} %get-tuple-element.29.refs_3_), channel_id=1, source_target_pairs={{0,4},{4,0},{8,12},{12,8},{16,20},{20,16},{24,28},{28,24},{1,5},{5... | collective-permute-start | bytes 30728 | tf_op jit(solution)/shard_map/ppermute | solution.py:316
  4.5 2.6 %collective-permute-start.3 = (bf16[640,128]{1,0:T(8,128)(2,1)S(1)}, bf16[640,128]{1,0:T(8,128)(2,1)S(1)}, u32[]{:S(2)}, u32[]{:S(2)}) collective-permute-start(bf16[640,128]{1,0:T(8,128)(2,1)S(1)} %get-tuple-element.31.refs_6_.refs_3_), channel_id=1, source_target_pairs={{0,8},{4,12},{8,0},{12,4},{16,24},{20,28},{24,16},{28,20},{1,9},{5... | collective-permute-start | bytes 491528 | tf_op jit(solution)/shard_map/ppermute | solution.py:316
  7.0 1.5 %collective-permute-start.4 = (bf16[640,128]{1,0:T(8,128)(2,1)S(1)}, bf16[640,128]{1,0:T(8,128)(2,1)S(1)}, u32[]{:S(2)}, u32[]{:S(2)}) collective-permute-start(bf16[640,128]{1,0:T(8,128)(2,1)S(1)} %get-tuple-element.31.refs_6_.refs_3_), channel_id=1, source_target_pairs={{0,16},{4,20},{8,24},{12,28},{16,0},{20,4},{24,8},{28,12},{1,17},{... | collective-permute-start | bytes 491528 | tf_op jit(solution)/shard_map/ppermute | solution.py:316
  8.6 1.0 %shard_map.97 = (f32[8,640]{1,0:T(8,128)S(1)}, bf16[4,640,128]{2,1,0:T(8,128)(2,1)S(1)}, bf16[4,128,640]{2,1,0:T(8,128)(2,1)S(1)}, bf16[4,128,640]{2,1,0:T(8,128)(2,1)S(1)}, bf16[640,128]{1,0:T(8,128)(2,1)S(1)}) custom-call(bf16[160,2048]{1,0:T(8,128)(2,1)S(1)} %copy-done, bf16[160,2048]{1,0:T(8,128)(2,1)S(1)} %copy-done.1, bf16[160,2048]{1,0:T(8,128)(2,1)S(1)} %copy-done.2, ...), custom_call_target="tpu_custom_call" | custom-call | flops 1100000000 | bytes 3133440 | tf_op jit(solution)/shard_map/pallas_call | solution.py:35
  9.6 1.5 %collective-permute-start.5 = (bf16[640,128]{1,0:T(8,128)(2,1)S(1)}, bf16[640,128]{1,0:T(8,128)(2,1)S(1)}, u32[]{:S(2)}, u32[]{:S(2)}) collective-permute-start(bf16[640,128]{1,0:T(8,128)(2,1)S(1)} %get-tuple-element.34), channel_id=1, source_target_pairs={{0,24},{4,28},{8,16},{12,20},{16,8},{20,12},{24,0},{28,4},{1,25},{... | collective-permute-start | bytes 491528 | tf_op jit(solution)/shard_map/ppermute | solution.py:316
  11.1 0.7 %collective-permute-done.3.refs_6_.refs_4_ = bf16[640,128]{1,0:T(8,128)(2,1)S(1)} collective-permute-done((bf16[640,128]{1,0:T(8,128)(2,1)S(1)}, bf16[640,128]{1,0:T(8,128)(2,1)S(1)}, u32[]{:S(2)}, u32[]{:S(2)}) %collective-permute-start.3) | collective-permute-done | bytes 163872 | tf_op jit(solution)/shard_map/ppermute | solution.py:316
  11.8 1.7 %shard_map.100 = bf16[640,128]{1,0:T(8,128)(2,1)S(1)} custom-call(f32[16,128]{1,0:T(8,128)S(1)} %get-tuple-element.25.refs_0_, bf16[4,640,128]{2,1,0:T(8,128)(2,1)S(1)} %get-tuple-element.35.refs_1_, bf16[6,640,128]{2,1,0:T(8,128)(2,1)S(1)} %collective-permute-done.1.refs_4_.refs_2_, bf16[4,128,640]{2,1,0:T(8,128)(2,1)S(1)} %get-tuple-element.32.refs_3_.refs_1_, ...), custom_call_target="tpu_custom_call" | custom-call | flops 550000000 | bytes 3141632 | tf_op jit(solution)/shard_map/pallas_call | solution.py:35
  13.6 1.8 %collective-permute-start.6 = (bf16[640,128]{1,0:T(8,128)(2,1)S(1)}, bf16[640,128]{1,0:T(8,128)(2,1)S(1)}, u32[]{:S(2)}, u32[]{:S(2)}) collective-permute-start(bf16[640,128]{1,0:T(8,128)(2,1)S(1)} %shard_map.100), channel_id=1, source_target_pairs={{0,8},{4,12},{8,0},{12,4},{16,24},{20,28},{24,16},{28,20},{1,9},{5... | collective-permute-start | bytes 491528 | tf_op jit(solution)/shard_map/ppermute | solution.py:316
  15.4 1.4 %collective-permute-done.4.refs_6_.refs_5_ = bf16[640,128]{1,0:T(8,128)(2,1)S(1)} collective-permute-done((bf16[640,128]{1,0:T(8,128)(2,1)S(1)}, bf16[640,128]{1,0:T(8,128)(2,1)S(1)}, u32[]{:S(2)}, u32[]{:S(2)}) %collective-permute-start.4) | collective-permute-done | bytes 163872 | tf_op jit(solution)/shard_map/ppermute | solution.py:316
  16.8 1.7 %shard_map.101 = bf16[640,128]{1,0:T(8,128)(2,1)S(1)} custom-call(f32[16,128]{1,0:T(8,128)S(1)} %get-tuple-element.25.refs_0_, bf16[4,640,128]{2,1,0:T(8,128)(2,1)S(1)} %get-tuple-element.35.refs_1_, bf16[6,640,128]{2,1,0:T(8,128)(2,1)S(1)} %collective-permute-done.1.refs_4_.refs_2_, bf16[4,128,640]{2,1,0:T(8,128)(2,1)S(1)} %get-tuple-element.32.refs_3_.refs_1_, ...), custom_call_target="tpu_custom_call" | custom-call | flops 550000000 | bytes 3141632 | tf_op jit(solution)/shard_map/pallas_call | solution.py:35
  18.6 1.6 %collective-permute-start.7 = (bf16[640,128]{1,0:T(8,128)(2,1)S(1)}, bf16[640,128]{1,0:T(8,128)(2,1)S(1)}, u32[]{:S(2)}, u32[]{:S(2)}) collective-permute-start(bf16[640,128]{1,0:T(8,128)(2,1)S(1)} %shard_map.101), channel_id=1, source_target_pairs={{0,16},{4,20},{8,24},{12,28},{16,0},{20,4},{24,8},{28,12},{1,17},{... | collective-permute-start | bytes 491528 | tf_op jit(solution)/shard_map/ppermute | solution.py:316
  20.1 1.7 %shard_map.98.refs_7_ = bf16[640,128]{1,0:T(8,128)(2,1)S(1)} custom-call(f32[16,128]{1,0:T(8,128)S(1)} %get-tuple-element.25.refs_0_, bf16[4,640,128]{2,1,0:T(8,128)(2,1)S(1)} %get-tuple-element.35.refs_1_, bf16[6,640,128]{2,1,0:T(8,128)(2,1)S(1)} %collective-permute-done.1.refs_4_.refs_2_, bf16[4,128,640]{2,1,0:T(8,128)(2,1)S(1)} %get-tuple-element.32.refs_3_.refs_1_, ...), custom_call_target="tpu_custom_call" | custom-call | flops 550000000 | bytes 3141632 | tf_op jit(solution)/shard_map/pallas_call | solution.py:35
  21.9 0.1 collective-permute-start.8
  22.0 2.1 %shard_map.99.refs_0_ = f32[640,128]{1,0:T(8,128)S(1)} custom-call(f32[16,128]{1,0:T(8,128)S(1)} %get-tuple-element.25.refs_0_, bf16[4,640,128]{2,1,0:T(8,128)(2,1)S(1)} %get-tuple-element.35.refs_1_, bf16[6,640,128]{2,1,0:T(8,128)(2,1)S(1)} %collective-permute-done.1.refs_4_.refs_2_, bf16[4,128,640]{2,1,0:T(8,128)(2,1)S(1)} %get-tuple-element.32.refs_3_.refs_1_, ...), custom_call_target="tpu_custom_call" | custom-call | flops 550000000 | bytes 3141632 | tf_op jit(solution)/shard_map/pallas_call | solution.py:35
  24.1 3.7 %shard_map.102.refs_4_ = bf16[2,640,128]{2,1,0:T(8,128)(2,1)S(1)} custom-call(f32[16,128]{1,0:T(8,128)S(1)} %get-tuple-element.25.refs_0_, bf16[4,128,640]{2,1,0:T(8,128)(2,1)S(1)} %get-tuple-element.36.refs_4_.refs_1_, f32[8,640]{1,0:T(8,128)S(1)} %get-tuple-element.33.refs_5_.refs_2_, bf16[640,128]{1,0:T(8,128)(2,1)S(1)} %get-tuple-element.31.refs_6_.refs_3_, ...), custom_call_target="tpu_custom_call" | custom-call | flops 2750000128 | bytes 1339392 | tf_op jit(solution)/shard_map/pallas_call | solution.py:35
  27.8 0.4 %collective-permute-done.8.refs_3_ = bf16[640,128]{1,0:T(8,128)(2,1)S(1)} collective-permute-done((bf16[640,128]{1,0:T(8,128)(2,1)S(1)}, bf16[640,128]{1,0:T(8,128)(2,1)S(1)}, u32[]{:S(2)}, u32[]{:S(2)}) %collective-permute-start.8) | collective-permute-done | bytes 163872 | tf_op jit(solution)/shard_map/ppermute | solution.py:316
  28.2 0.1 shard_map.103
  28.2 0.1 collective-permute-start.9
  28.3 0.5 %collective-permute-start.10 = (bf16[2,640,128]{2,1,0:T(8,128)(2,1)S(1)}, bf16[2,640,128]{2,1,0:T(8,128)(2,1)S(1)}, u32[]{:S(2)}, u32[]{:S(2)}) collective-permute-start(bf16[2,640,128]{2,1,0:T(8,128)(2,1)S(1)} %shard_map.102.refs_4_), channel_id=1, source_target_pairs={{0,4},{4,0},{8,12},{12,8},{16,20},{20,16},{24,28},{28,24},{1,5},{5... | collective-permute-start | bytes 983048 | tf_op jit(solution)/shard_map/ppermute | solution.py:316
  28.8 0.8 %collective-permute-done.9.refs_1_ = bf16[320,128]{1,0:T(8,128)(2,1)S(1)} collective-permute-done((bf16[320,128]{1,0:T(8,128)(2,1)S(1)}, bf16[320,128]{1,0:T(8,128)(2,1)S(1)}, u32[]{:S(2)}, u32[]{:S(2)}) %collective-permute-start.9) | collective-permute-done | bytes 81952 | tf_op jit(solution)/shard_map/ppermute | solution.py:316
  29.6 0.1 shard_map.104
  29.7 1.6 %collective-permute-start.11 = (bf16[2,40,256]{2,1,0:T(8,128)(2,1)S(1)}, bf16[2,40,256]{2,1,0:T(8,128)(2,1)S(1)}, u32[]{:S(2)}, u32[]{:S(2)}) collective-permute-start(bf16[2,40,256]{2,1,0:T(8,128)(2,1)S(1)} %get-tuple-element.40), channel_id=1, source_target_pairs={{0,1},{1,0},{2,3},{3,2},{4,5},{5,4},{6,7},{7,6},{8,9},{9,8},{10,11... | collective-permute-start | bytes 122888 | tf_op jit(solution)/shard_map/ppermute | solution.py:316
  31.3 2.6 %collective-permute-start.12 = (bf16[2,40,256]{2,1,0:T(8,128)(2,1)S(1)}, bf16[2,40,256]{2,1,0:T(8,128)(2,1)S(1)}, u32[]{:S(2)}, u32[]{:S(2)}) collective-permute-start(bf16[2,40,256]{2,1,0:T(8,128)(2,1)S(1)} %get-tuple-element.41), channel_id=1, source_target_pairs={{0,2},{1,3},{2,0},{3,1},{4,6},{5,7},{6,4},{7,5},{8,10},{9,11},{10,... | collective-permute-start | bytes 122888 | tf_op jit(solution)/shard_map/ppermute | solution.py:316
  33.9 0.2 collective-permute-start.13
  34.1 3.9 %shard_map.105.refs_0_ = bf16[2,640,128]{2,1,0:T(8,128)(2,1)S(1)} custom-call(f32[16,128]{1,0:T(8,128)S(1)} %get-tuple-element.25.refs_0_, bf16[4,128,640]{2,1,0:T(8,128)(2,1)S(1)} %get-tuple-element.32.refs_3_.refs_1_, f32[8,640]{1,0:T(8,128)S(1)} %get-tuple-element.33.refs_5_.refs_2_, bf16[640,128]{1,0:T(8,128)(2,1)S(1)} %get-tuple-element.31.refs_6_.refs_3_, ...), custom_call_target="tpu_custom_call" | custom-call | flops 2750000128 | bytes 1339392 | tf_op jit(solution)/shard_map/pallas_call | solution.py:35
  38.0 1.0 %shard_map.106.refs_4_ = bf16[160,2048]{1,0:T(8,128)(2,1)} custom-call(bf16[2,640,128]{2,1,0:T(8,128)(2,1)S(1)} %shard_map.105.refs_0_, bf16[2,640,128]{2,1,0:T(8,128)(2,1)S(1)} %collective-permute-done.10.refs_1_), custom_call_target="tpu_custom_call" | custom-call | flops 1100000000 | bytes 655360 | tf_op jit(solution)/shard_map/pallas_call | solution.py:35
  39.0 0.7 %collective-permute-done.13.refs_3_ = bf16[2,40,256]{2,1,0:T(8,128)(2,1)S(1)} collective-permute-done((bf16[2,40,256]{2,1,0:T(8,128)(2,1)S(1)}, bf16[2,40,256]{2,1,0:T(8,128)(2,1)S(1)}, u32[]{:S(2)}, u32[]{:S(2)}) %collective-permute-start.13) | collective-permute-done | bytes 40992 | tf_op jit(solution)/shard_map/ppermute | solution.py:316
  39.7 0.7 %shard_map.107 = (bf16[40,1024]{1,0:T(8,128)(2,1)}, bf16[40,1024]{1,0:T(8,128)(2,1)}) custom-call(bf16[2,40,256]{2,1,0:T(8,128)(2,1)S(1)} %get-tuple-element.39.refs_7_.refs_0_, bf16[2,40,256]{2,1,0:T(8,128)(2,1)S(1)} %collective-permute-done.11.refs_1_, bf16[2,40,256]{2,1,0:T(8,128)(2,1)S(1)} %collective-permute-done.12.refs_2_, ...), custom_call_target="tpu_custom_call" | custom-call | flops 110000000 | bytes 163840 | tf_op jit(solution)/shard_map/pallas_call | solution.py:35
  (18 shorter events, 0.1 us)
Async XLA Ops:
  1.5 2.3 %collective-permute-start = (bf16[320,128]{1,0:T(8,128)(2,1)S(1)}, bf16[320,128]{1,0:T(8,128)(2,1)S(1)}, u32[]{:S(2)}, u32[]{:S(2)}) collective-permute-start(bf16[320,128]{1,0:T(8,128)(2,1)S(1)} %get-tuple-element.26), channel_id=1, source_target_pairs={{0,4},{4,0},{8,12},{12,8},{16,20},{20,16},{24,28},{28,24},{1,5},{5... | collective-permute-start | bytes 245768 | tf_op jit(solution)/shard_map/ppermute | solution.py:316
  2.0 1.9 %copy-start.3 = (f32[160,16]{0,1:T(8,128)S(1)}, f32[160,16]{0,1:T(8,128)}, u32[]{:S(2)}) copy-start(f32[160,16]{0,1:T(8,128)} %param.13) | copy-start | bytes 30724
  2.0 6.5 %copy-start = (bf16[160,2048]{1,0:T(8,128)(2,1)S(1)}, bf16[160,2048]{1,0:T(8,128)(2,1)}, u32[]{:S(2)}) copy-start(bf16[160,2048]{1,0:T(8,128)(2,1)} %refs_0_.5) | copy-start | bytes 1966084
  2.0 6.5 %copy-start.1 = (bf16[160,2048]{1,0:T(8,128)(2,1)S(1)}, bf16[160,2048]{1,0:T(8,128)(2,1)}, u32[]{:S(2)}) copy-start(bf16[160,2048]{1,0:T(8,128)(2,1)} %refs_1_.5) | copy-start | bytes 1966084
  2.0 6.5 %copy-start.2 = (bf16[160,2048]{1,0:T(8,128)(2,1)S(1)}, bf16[160,2048]{1,0:T(8,128)(2,1)}, u32[]{:S(2)}) copy-start(bf16[160,2048]{1,0:T(8,128)(2,1)} %refs_2_.3) | copy-start | bytes 1966084
  3.8 4.8 %collective-permute-start.1 = (bf16[6,640,128]{2,1,0:T(8,128)(2,1)S(1)}, bf16[6,640,128]{2,1,0:T(8,128)(2,1)S(1)}, u32[]{:S(2)}, u32[]{:S(2)}) collective-permute-start(bf16[6,640,128]{2,1,0:T(8,128)(2,1)S(1)} %get-tuple-element.30), channel_id=1, source_target_pairs={{0,4},{4,0},{8,12},{12,8},{16,20},{20,16},{24,28},{28,24},{1,5},{5... | collective-permute-start | bytes 2949128 | tf_op jit(solution)/shard_map/ppermute | solution.py:316
  4.0 4.6 %collective-permute-start.2 = (f32[16,160]{1,0:T(8,128)S(1)}, f32[16,160]{1,0:T(8,128)S(1)}, u32[]{:S(2)}, u32[]{:S(2)}) collective-permute-start(f32[16,160]{1,0:T(8,128)S(1)} %get-tuple-element.29.refs_3_), channel_id=1, source_target_pairs={{0,4},{4,0},{8,12},{12,8},{16,20},{20,16},{24,28},{28,24},{1,5},{5... | collective-permute-start | bytes 30728 | tf_op jit(solution)/shard_map/ppermute | solution.py:316
  4.5 7.4 %collective-permute-start.3 = (bf16[640,128]{1,0:T(8,128)(2,1)S(1)}, bf16[640,128]{1,0:T(8,128)(2,1)S(1)}, u32[]{:S(2)}, u32[]{:S(2)}) collective-permute-start(bf16[640,128]{1,0:T(8,128)(2,1)S(1)} %get-tuple-element.31.refs_6_.refs_3_), channel_id=1, source_target_pairs={{0,8},{4,12},{8,0},{12,4},{16,24},{20,28},{24,16},{28,20},{1,9},{5... | collective-permute-start | bytes 491528 | tf_op jit(solution)/shard_map/ppermute | solution.py:316
  7.0 9.8 %collective-permute-start.4 = (bf16[640,128]{1,0:T(8,128)(2,1)S(1)}, bf16[640,128]{1,0:T(8,128)(2,1)S(1)}, u32[]{:S(2)}, u32[]{:S(2)}) collective-permute-start(bf16[640,128]{1,0:T(8,128)(2,1)S(1)} %get-tuple-element.31.refs_6_.refs_3_), channel_id=1, source_target_pairs={{0,16},{4,20},{8,24},{12,28},{16,0},{20,4},{24,8},{28,12},{1,17},{... | collective-permute-start | bytes 491528 | tf_op jit(solution)/shard_map/ppermute | solution.py:316
  9.6 10.6 %collective-permute-start.5 = (bf16[640,128]{1,0:T(8,128)(2,1)S(1)}, bf16[640,128]{1,0:T(8,128)(2,1)S(1)}, u32[]{:S(2)}, u32[]{:S(2)}) collective-permute-start(bf16[640,128]{1,0:T(8,128)(2,1)S(1)} %get-tuple-element.34), channel_id=1, source_target_pairs={{0,24},{4,28},{8,16},{12,20},{16,8},{20,12},{24,0},{28,4},{1,25},{... | collective-permute-start | bytes 491528 | tf_op jit(solution)/shard_map/ppermute | solution.py:316
  13.6 14.2 %collective-permute-start.6 = (bf16[640,128]{1,0:T(8,128)(2,1)S(1)}, bf16[640,128]{1,0:T(8,128)(2,1)S(1)}, u32[]{:S(2)}, u32[]{:S(2)}) collective-permute-start(bf16[640,128]{1,0:T(8,128)(2,1)S(1)} %shard_map.100), channel_id=1, source_target_pairs={{0,8},{4,12},{8,0},{12,4},{16,24},{20,28},{24,16},{28,20},{1,9},{5... | collective-permute-start | bytes 491528 | tf_op jit(solution)/shard_map/ppermute | solution.py:316
  18.6 9.2 %collective-permute-start.7 = (bf16[640,128]{1,0:T(8,128)(2,1)S(1)}, bf16[640,128]{1,0:T(8,128)(2,1)S(1)}, u32[]{:S(2)}, u32[]{:S(2)}) collective-permute-start(bf16[640,128]{1,0:T(8,128)(2,1)S(1)} %shard_map.101), channel_id=1, source_target_pairs={{0,16},{4,20},{8,24},{12,28},{16,0},{20,4},{24,8},{28,12},{1,17},{... | collective-permute-start | bytes 491528 | tf_op jit(solution)/shard_map/ppermute | solution.py:316
  21.9 6.3 %collective-permute-start.8 = (bf16[640,128]{1,0:T(8,128)(2,1)S(1)}, bf16[640,128]{1,0:T(8,128)(2,1)S(1)}, u32[]{:S(2)}, u32[]{:S(2)}) collective-permute-start(bf16[640,128]{1,0:T(8,128)(2,1)S(1)} %shard_map.98.refs_7_), channel_id=1, source_target_pairs={{0,24},{4,28},{8,16},{12,20},{16,8},{20,12},{24,0},{28,4},{1,25},{... | collective-permute-start | bytes 491528 | tf_op jit(solution)/shard_map/ppermute | solution.py:316
  28.2 1.3 %collective-permute-start.9 = (bf16[320,128]{1,0:T(8,128)(2,1)S(1)}, bf16[320,128]{1,0:T(8,128)(2,1)S(1)}, u32[]{:S(2)}, u32[]{:S(2)}) collective-permute-start(bf16[320,128]{1,0:T(8,128)(2,1)S(1)} %get-tuple-element.38), channel_id=1, source_target_pairs={{0,4},{4,0},{8,12},{12,8},{16,20},{20,16},{24,28},{28,24},{1,5},{5... | collective-permute-start | bytes 245768 | tf_op jit(solution)/shard_map/ppermute | solution.py:316
  28.3 9.7 %collective-permute-start.10 = (bf16[2,640,128]{2,1,0:T(8,128)(2,1)S(1)}, bf16[2,640,128]{2,1,0:T(8,128)(2,1)S(1)}, u32[]{:S(2)}, u32[]{:S(2)}) collective-permute-start(bf16[2,640,128]{2,1,0:T(8,128)(2,1)S(1)} %shard_map.102.refs_4_), channel_id=1, source_target_pairs={{0,4},{4,0},{8,12},{12,8},{16,20},{20,16},{24,28},{28,24},{1,5},{5... | collective-permute-start | bytes 983048 | tf_op jit(solution)/shard_map/ppermute | solution.py:316
  29.7 9.3 %collective-permute-start.11 = (bf16[2,40,256]{2,1,0:T(8,128)(2,1)S(1)}, bf16[2,40,256]{2,1,0:T(8,128)(2,1)S(1)}, u32[]{:S(2)}, u32[]{:S(2)}) collective-permute-start(bf16[2,40,256]{2,1,0:T(8,128)(2,1)S(1)} %get-tuple-element.40), channel_id=1, source_target_pairs={{0,1},{1,0},{2,3},{3,2},{4,5},{5,4},{6,7},{7,6},{8,9},{9,8},{10,11... | collective-permute-start | bytes 122888 | tf_op jit(solution)/shard_map/ppermute | solution.py:316
  31.3 7.7 %collective-permute-start.12 = (bf16[2,40,256]{2,1,0:T(8,128)(2,1)S(1)}, bf16[2,40,256]{2,1,0:T(8,128)(2,1)S(1)}, u32[]{:S(2)}, u32[]{:S(2)}) collective-permute-start(bf16[2,40,256]{2,1,0:T(8,128)(2,1)S(1)} %get-tuple-element.41), channel_id=1, source_target_pairs={{0,2},{1,3},{2,0},{3,1},{4,6},{5,7},{6,4},{7,5},{8,10},{9,11},{10,... | collective-permute-start | bytes 122888 | tf_op jit(solution)/shard_map/ppermute | solution.py:316
  33.9 5.8 %collective-permute-start.13 = (bf16[2,40,256]{2,1,0:T(8,128)(2,1)S(1)}, bf16[2,40,256]{2,1,0:T(8,128)(2,1)S(1)}, u32[]{:S(2)}, u32[]{:S(2)}) collective-permute-start(bf16[2,40,256]{2,1,0:T(8,128)(2,1)S(1)} %get-tuple-element.42), channel_id=1, source_target_pairs={{0,3},{1,2},{2,1},{3,0},{4,7},{5,6},{6,5},{7,4},{8,11},{9,10},{10,... | collective-permute-start | bytes 122888 | tf_op jit(solution)/shard_map/ppermute | solution.py:316

commit v3 on v2

--- a/solution.py
+++ b/solution.py
@@ -21,7 +21,7 @@
 SMEM = pl.BlockSpec(memory_space=pltpu.SMEM)
 
 
-def call(kernel, outs, ins, scratch=(), smem=0, cost=0.1, far=(), after=()):
+def call(kernel, outs, ins, scratch=(), smem=0, cost=0.1, far=(), after=(), out_spec=VMEM):
     ins = list(ins) + [pltpu.with_memory_space_constraint(x, pltpu.HBM) for x in far]
     specs = [SMEM] * smem + [VMEM] * (len(ins) - smem - len(far))
     specs += [HBM] * len(far) + [ANY] * len(after)
@@ -38,7 +38,7 @@
             flops=int(cost * FLOPS_PER_US), bytes_accessed=moved, transcendentals=0
         ),
         in_specs=specs,
-        out_specs=[VMEM] * len(outs),
+        out_specs=[out_spec] * len(outs),
         out_shape=[jax.ShapeDtypeStruct(shape, dtype) for shape, dtype in outs],
         scratch_shapes=list(scratch),
         compiler_params=pltpu.CompilerParams(vmem_limit_bytes=48 * 2**20),
@@ -53,7 +53,7 @@
     return lax.rem(lax.axis_index("ctx"), 2)
 
 
-def columns(head):
+def columns_of(head):
     return pl.ds(pl.multiple_of(head * HEAD_SIZE, HEAD_SIZE), HEAD_SIZE)
 
 
@@ -71,7 +71,7 @@
     rows = k_hbm.shape[0]
     c = parity()
     pairs = [
-        (src.at[:, columns(group)], ref.at[pl.ds(kind * rows, rows), :])
+        (src.at[:, columns_of(group)], ref.at[pl.ds(kind * rows, rows), :])
         for ref, group in ((other, 1 - c), (same, c))
         for kind, src in enumerate((k_hbm, v_hbm))
     ]
@@ -89,7 +89,7 @@
     group = 1 - parity()
     pairs = [(pos_hbm, pos)] + [
         (
-            src.at[pl.ds(w * half, half), columns(group * heads + h)],
+            src.at[pl.ds(w * half, half), columns_of(group * heads + h)],
             out.at[2 * kind + w, pl.ds(h * half, half), :],
         )
         for kind, src in enumerate((q_hbm, g_hbm, o_hbm))
@@ -113,7 +113,7 @@
 
 
 def rows_kernel(heads, q_ref, g_ref, o_ref, own_log, sib, sib_log, kv, *refs):
-    out, own, own_t, sib_t, kv_out = refs
+    out, turned_out, own, own_t, sib_t, kv_out = refs
     lanes = own.shape[1]
     half = lanes // heads
     c = parity()
@@ -126,7 +126,7 @@
 
     def stacked(ref, w):
         r = slice(w * half, (w + 1) * half)
-        return jnp.concatenate([ref[r, columns(c * heads + h)] for h in range(heads)], axis=0)
+        return jnp.concatenate([ref[r, columns_of(c * heads + h)] for h in range(heads)], axis=0)
 
     for b, (log, turned) in enumerate(((own_log, own_t), (sib_log, sib_t))):
         parts = split_bf16(jnp.clip(log[...], -1e30, 1e30), 3)
@@ -146,33 +146,13 @@
             delta = g.astype(F32) * o.astype(F32)
             row = sum(nt(ones, part) for part in split_bf16(delta, 2))
             out[4 * b + 2 + w : 4 * b + 3 + w, :] = row[0:1]
+    out[8:16, :] = lax.rem(lax.broadcasted_iota(jnp.int32, (8, lanes), 1), half).astype(F32)
+    turned_out[...] = out[...].T
     kv_out[...] = kv[...]
 
 
-def seen_in_run(half, lanes):
-    key_row = lax.broadcasted_iota(jnp.int32, (half, lanes), 0)
-    query_row = lax.rem(lax.broadcasted_iota(jnp.int32, (half, lanes), 1), half)
-    return key_row <= query_row
-
-
-def probs_and_grads(k, v, turned, vec, at, which, mask=None):
-    s = jnp.dot(k, turned[which], preferred_element_type=F32)
-    p = jnp.exp2(s * EXP2_SCALE - vec[pl.ds(at + which, 1), :])
-    if mask is not None:
-        p = jnp.where(mask, p, 0.0)
-    dp = jnp.dot(v, turned[2 + which], preferred_element_type=F32)
-    return p, (p * (dp - vec[pl.ds(at + 2 + which, 1), :])).astype(BF16)
-
-
-def first_runs(piece, tokens, half):
-    rows = piece.shape[0] // 2
-
-    def both(at):
-        return jnp.concatenate(
-            [piece[at + a * tokens : at + a * tokens + half, :] for a in range(2)], axis=0
-        )
-
-    return both(0), both(rows)
+def is_larger(larger, m, b):
+    return jnp.max(larger[2 * m + b : 2 * m + b + 1, :]) > 0.5
 
 
 def one_run(piece, tokens, half, a, which):
@@ -183,43 +163,53 @@
     return piece[pl.ds(at, half), :], piece[pl.ds(rows + at, half), :]
 
 
-def is_larger(larger, pair, a, b):
-    at = 4 * pair + 2 * a + b
-    return jnp.max(larger[at : at + 1, :]) > 0.5
-
-
 def kv_grad_kernel(pair, larger, own, sib, own_t, sib_t, vec, piece, out):
     tokens = piece.shape[0] // 4
     half = tokens // 2
     rows = 2 * tokens
-    sides = ((own, own_t), (sib, sib_t))
-
-    def terms(k, v, b, which, mask=None):
-        stack, turned = sides[b]
-        p, ds = probs_and_grads(k, v, turned, vec, 4 * b, which, mask)
-        return (
-            jnp.dot(ds, stack[which], preferred_element_type=F32),
-            jnp.dot(p.astype(BF16), stack[2 + which], preferred_element_type=F32),
-        )
-
-    sums = {(a, w): [] for a in range(2) for w in range(2)}
-    k, v = first_runs(piece, tokens, half)
-    for b in range(2):
-        both = terms(k, v, b, 1)
-        for a in range(2):
-            sums[a, 0].append([x[a * half : (a + 1) * half] for x in both])
-    seen = seen_in_run(half, own.shape[1]) if pair == 0 else None
+    lanes = own.shape[1]
+    stacks, turned = (own, sib), (own_t, sib_t)
+    first = [one_run(piece, tokens, half, a, 0) for a in range(2)]
+    k, v = (jnp.concatenate(x, axis=0) for x in zip(*first))
+    jobs = [(k, v, b, 1, None) for b in range(2)]
     for a in range(2):
         for b in range(2):
             if pair == 0 and a == b:
-                for w in range(2):
-                    k, v = one_run(piece, tokens, half, a, w)
-                    sums[a, w].append(terms(k, v, b, w, seen))
-                continue
-            second = is_larger(larger, pair, a, b)
-            which = jnp.where(second, 1, 0)
-            k, v = one_run(piece, tokens, half, a, which)
-            both = terms(k, v, b, which)
+                jobs += [(*one_run(piece, tokens, half, a, w), b, w, (a, w)) for w in range(2)]
+            else:
+                second = is_larger(larger, 2 * pair + a, b)
+                which = jnp.where(second, 1, 0)
+                run = one_run(piece, tokens, half, a, which)
+                jobs.append((*run, b, which, (a, second)))
+    if pair == 0:
+        key_row = lax.broadcasted_iota(jnp.int32, (half, lanes), 0)
+        query_row = lax.rem(lax.broadcasted_iota(jnp.int32, (half, lanes), 1), half)
+        seen = key_row <= query_row
+
+    def products(job):
+        k, v, b, which, _ = job
+        s = jnp.dot(k, turned[b][which], preferred_element_type=F32)
+        return s, jnp.dot(v, turned[b][2 + which], preferred_element_type=F32)
+
+    sums = {(a, w): [] for a in range(2) for w in range(2)}
+    ahead = products(jobs[0])
+    for i, job in enumerate(jobs):
+        (s, dp), ahead = ahead, products(jobs[i + 1]) if i + 1 < len(jobs) else None
+        _, _, b, which, place = job
+        p = jnp.exp2(s * EXP2_SCALE - vec[pl.ds(4 * b + which, 1), :])
+        if place is not None and isinstance(which, int):
+            p = jnp.where(seen, p, 0.0)
+        ds = (p * (dp - vec[pl.ds(4 * b + 2 + which, 1), :])).astype(BF16)
+        value_term = jnp.dot(p.astype(BF16), stacks[b][2 + which], preferred_element_type=F32)
+        key_term = jnp.dot(ds, stacks[b][which], preferred_element_type=F32)
+        both = key_term, value_term
+        if place is None:
+            for a in range(2):
+                sums[a, 0].append([x[a * half : (a + 1) * half] for x in both])
+        elif isinstance(which, int):
+            sums[place].append(both)
+        else:
+            a, second = place
             sums[a, 0].append([jnp.where(second, 0.0, x) for x in both])
             sums[a, 1].append([jnp.where(second, x, 0.0) for x in both])
     for (a, w), parts in sums.items():
@@ -228,28 +218,77 @@
         out[rows + at : rows + at + half, :] = sum(x[1] for x in parts).astype(out.dtype)
 
 
-def q_grad_kernel(b, larger, turned, vec, *refs):
-    pieces, (out, acc) = refs[:-2], refs[-2:]
+def q_grads(b, larger, stack, columns, pieces):
     tokens = pieces[0].shape[0] // 4
     half = tokens // 2
-    acc[...] = jnp.zeros_like(acc)
-
-    def add(k, v, which, mask=None):
-        _, ds = probs_and_grads(k, v, turned, vec, 4 * b, which, mask)
-        acc[which] += jnp.dot(k.T, ds, preferred_element_type=F32)
-
-    for pair, piece in enumerate(pieces):
-        add(*first_runs(piece, tokens, half), 1)
-        for a in range(2):
-            if pair == 0 and a == b:
-                seen = seen_in_run(half, turned.shape[2])
-                for w in range(2):
-                    add(*one_run(piece, tokens, half, a, w), w, seen)
-                continue
-            which = jnp.where(is_larger(larger, pair, a, b), 1, 0)
-            add(*one_run(piece, tokens, half, a, which), which)
-    for w in range(2):
-        out[w] = (acc[w] * SCALE).T.astype(BF16)
+    rows = 2 * tokens
+    grads = [0.0, 0.0]
+    spot = columns[:, 8:9]
+    for start in range(0, len(pieces), 4):
+        some = pieces[start : start + 4]
+
+        def gather(at):
+            return jnp.concatenate(
+                [x[at + a * tokens : at + a * tokens + half, :] for x in some for a in range(2)],
+                axis=0,
+            )
+
+        count = 2 * len(some)
+        lane = lax.broadcasted_iota(jnp.int32, (1, count * half), 1)
+        group = lax.div(lane, half)
+        least = [lax.rem(lane, half).astype(F32)] * 2
+        for i in range(count):
+            m = 2 * start + i
+            if m != b:
+                sign = jnp.where(is_larger(larger, m, b), 1.0, -1.0) * 2 * tokens
+                least[0] = jnp.where(group == i, sign, least[0])
+                least[1] = jnp.where(group == i, -sign, least[1])
+        runs = [(gather(at), gather(rows + at)) for at in (0, half)]
+        for which, run, limit in ((0, 0, least[0]), (1, 0, None), (1, 1, least[1])):
+            k, v = runs[run]
+            p = jnp.exp2(
+                nt(stack[which], k) * EXP2_SCALE - columns[:, 4 * b + which : 4 * b + which + 1]
+            )
+            if limit is not None:
+                p = jnp.where(spot >= limit, p, 0.0)
+            at = 4 * b + 2 + which
+            ds = (p * (nt(stack[2 + which], v) - columns[:, at : at + 1])).astype(BF16)
+            grads[which] = grads[which] + jnp.dot(ds, k, preferred_element_type=F32)
+    return [(x * SCALE).astype(BF16) for x in grads]
+
+
+def sib_grad_kernel(larger, stack, columns, *refs):
+    pieces, out = refs[:-1], refs[-1]
+    out[0], out[1] = q_grads(1, larger, stack, columns, pieces)
+
+
+def own_grad_kernel(heads, larger, stack, columns, other, *refs):
+    pieces, (out, held, sems) = refs[:-3], refs[-3:]
+    half = out.shape[0] // 2
+    c = parity()
+
+    def copies(ref, group):
+        return [
+            pltpu.make_async_copy(
+                ref.at[w, pl.ds(h * half, half), :],
+                out.at[pl.ds(w * half, half), columns_of(group * heads + h)],
+                sems.at[group_sems + w * heads + h],
+            )
+            for w in range(2)
+            for h in range(heads)
+        ]
+
+    group_sems = 0
+    first = copies(other, 1 - c)
+    group_sems = 2 * heads
+    second = copies(held, c)
+    for each in first:
+        each.start()
+    held[0], held[1] = q_grads(0, larger, stack, columns, pieces)
+    for each in second:
+        each.start()
+    for each in first + second:
+        each.wait()
 
 
 def merge_kv_kernel(same_ref, other_ref, log, out, log_out):
@@ -289,26 +328,14 @@
             out[kind] = total[r, :].astype(BF16)
 
 
-def spread_kernel(tp_count, *refs):
+def spread_kernel(tp_count, order, *refs):
     parts, (key_out, value_out) = refs[:tp_count], refs[tp_count:]
     z = lax.axis_index("tp")
     width = parts[0].shape[2]
-    for m, part in enumerate(parts):
+    for m, part in zip(order, parts):
         cols = pl.ds(pl.multiple_of(jnp.bitwise_xor(z, m) * width, width), width)
         key_out[:, cols] = part[0]
         value_out[:, cols] = part[1]
-
-
-def unstack_kernel(heads, own, other, out):
-    half = out.shape[0] // 2
-    c = parity()
-    for ref, group in ((own, c), (other, 1 - c)):
-        for w in range(2):
-            for h in range(heads):
-                cols = pl.ds(
-                    pl.multiple_of((group * heads + h) * HEAD_SIZE, HEAD_SIZE), HEAD_SIZE
-                )
-                out[w * half : (w + 1) * half, cols] = ref[w, h * half : (h + 1) * half, :]
 
 
 def swap(x, axis, shift):
@@ -351,16 +378,18 @@
     )
     sib = swap(other, "ctx", 1)
     turned = ((4, HEAD_SIZE, lanes), BF16)
-    vec, own, own_t, sib_t, kv_late = call(
+    vec, columns, own, own_t, sib_t, kv_late = call(
         functools.partial(rows_kernel, heads),
-        [((8, lanes), F32), ((4, lanes, HEAD_SIZE), BF16), turned, turned, piece],
+        [((16, lanes), F32), ((lanes, 16), F32), ((4, lanes, HEAD_SIZE), BF16), turned, turned, piece],
         [queries, output_grad, attn_output, logs, sib, swap(logs, "ctx", 1), kv_chip],
         cost=1.0,
     )
     late = n // 2 - 1
-    pieces = [kv_chip] + [
-        swap(kv_late if pair == late else kv_chip, "ctx", 2 * pair) for pair in range(1, n // 2)
-    ]
+    pieces = {
+        pair: swap(kv_late if pair == late else kv_chip, "ctx", 2 * pair)
+        for pair in reversed(range(1, n // 2))
+    }
+    pieces = [kv_chip] + [pieces[pair] for pair in range(1, n // 2)]
 
     def kv_grads(pair, after=()):
         (out,) = call(
@@ -372,26 +401,25 @@
         )
         return out
 
-    partials = [kv_grads(pair) for pair in range(1, n // 2)]
-    received = [swap(x, "ctx", 2 * pair + 2) for pair, x in enumerate(partials)]
-    local = kv_grads(0, partials[-1:])
-
-    def q_grads(member, member_t, after=()):
-        (out,) = call(
-            functools.partial(q_grad_kernel, member),
-            [((2, lanes, HEAD_SIZE), BF16)],
-            [larger, member_t, vec] + pieces,
-            [pltpu.VMEM((2, HEAD_SIZE, lanes), F32)],
-            cost=2.5,
-            after=after,
-        )
-        return out
-
-    dq_sib = q_grads(1, sib_t)
-    dq_other = swap(dq_sib, "ctx", 1)
+    partials = {}
+    for pair in reversed(range(1, late)):
+        partials[pair] = kv_grads(pair, [partials[pair + 1]] if pair + 1 < late else [])
+    partials[late] = kv_grads(late)
+    local = kv_grads(0, [partials[late]])
+    received = [swap(partials[pair], "ctx", 2 * pair) for pair in range(1, n // 2)]
+
+    (dq_sib,) = call(
+        sib_grad_kernel,
+        [((2, lanes, HEAD_SIZE), BF16)],
+        [larger, sib, columns] + pieces,
+        cost=2.5,
+        after=[local],
+    )
     sum_same, sum_other = call(
         sum_kernel, [half_piece] * 2, [local] + received, after=[dq_sib]
     )
+    dq_sib, sum_other = lax.optimization_barrier((dq_sib, sum_other))
+    dq_other = swap(dq_sib, "ctx", 1)
     share = ((2, tokens // tp_count, 2 * HEAD_SIZE), BF16)
     shares = call(
         functools.partial(share_kernel, tp_count),
@@ -399,18 +427,20 @@
         [sum_same, swap(sum_other, "ctx", 1)],
         [pltpu.VMEM((2 * tokens, 2 * HEAD_SIZE), F32)],
     )
-    dq_own = q_grads(0, own_t, [shares[0]])
     (query_grad,) = call(
-        functools.partial(unstack_kernel, heads),
+        functools.partial(own_grad_kernel, heads),
         [(queries.shape, BF16)],
-        [dq_own, dq_other],
-        cost=1.0,
-    )
-
-    shares = [shares[0]] + [swap(shares[m], "tp", m) for m in range(1, tp_count)]
+        [larger, own, columns, dq_other] + pieces,
+        [pltpu.VMEM((2, lanes, HEAD_SIZE), BF16), pltpu.SemaphoreType.DMA((4 * heads,))],
+        cost=3.0,
+        after=[shares[0]],
+        out_spec=HBM,
+    )
+    order = [0, *range(2, tp_count), 1]
+    shares = [shares[0]] + [swap(shares[m], "tp", m) for m in order[1:]]
     final = ((tokens // tp_count, 2 * HEAD_SIZE * tp_count), BF16)
     key_grad, value_grad = call(
-        functools.partial(spread_kernel, tp_count), [final] * 2, shares, after=[pltpu.with_memory_space_constraint(query_grad, pltpu.HBM)]
+        functools.partial(spread_kernel, tp_count, order), [final] * 2, shares, after=[pltpu.with_memory_space_constraint(query_grad, pltpu.HBM)]
     )
     return (query_grad, key_grad, value_grad)
 

time: 40.6 us -> 36.4 us (0.90)
  Pallas kernels: 20.3 us -> 15.4 us
  starting transfers between devices: 15.3 us -> 16.8 us
  waiting for transfers between devices: 4.06 us -> 3.23 us
    pallas_call x14 -> x13, Pallas kernels: 20.3 us -> 15.4 us  [call(): pl.pallas_call(body, cost_estimate=pl.CostEstimate(flops=int(cost * FLOPS...]
    ppermute x14, starting transfers between devices: 15.3 us -> 16.8 us  [swap(): return lax.ppermute(x, axis, [(i, i ^ shift) for i in range(count)])]
    ppermute x14, waiting for transfers between devices: 4.06 us -> 3.23 us  [swap(): return lax.ppermute(x, axis, [(i, i ^ shift) for i in range(count)])]
  transfers between devices with their start and end apart: 14 -> 14, of which waited for: 5 -> 4; matrix products, arithmetic and copies ran while one was open for 0% -> 0% of each run, Pallas kernels for 46% -> 38%
where the time goes in v3:
time: 36.4 us; the launch traced here: 36.2 us
  starting transfers between devices  16.8 us (46%)
  Pallas kernels  15.4 us (42%)
  waiting for transfers between devices  3.23 us (9%)
  between operations  0.77 us (2%)
    ppermute x14, starting transfers between devices, swap(): return lax.ppermute(x, axis, [(i, i ^ shift) for i in range(count)])  16.8 us
    pallas_call x13, Pallas kernels, call(): pl.pallas_call(body, cost_estimate=pl.CostEstimate(flops=int(cost * FLOPS...  15.4 us
    ppermute x14, waiting for transfers between devices, swap(): return lax.ppermute(x, axis, [(i, i ^ shift) for i in range(count)])  3.23 us
  transfers between devices with their start and end apart: 14, of which 4 were waited for; matrix products, arithmetic and copies ran while one was open for 0% of the time, Pallas kernels for 38%

profile of v3, /device:TPU:0, one launch (start us, length us, event | category | flops | bytes accessed | tf_op | source)
XLA Modules:
  0.0 36.2 jit_solution(185972328286634481)
XLA Ops:
  0.6 0.9 %shard_map.94 = (bf16[320,128]{1,0:T(8,128)(2,1)S(1)}, bf16[320,128]{1,0:T(8,128)(2,1)S(1)}) custom-call(bf16[160,256]{1,0:T(8,128)(2,1)} %refs_0_.3, bf16[160,256]{1,0:T(8,128)(2,1)} %refs_1_.3), custom_call_target="tpu_custom_call" | custom-call | flops 110000000 | bytes 163840 | tf_op jit(solution)/shard_map/pallas_call | solution.py:35
  1.5 0.5 %collective-permute-start = (bf16[320,128]{1,0:T(8,128)(2,1)S(1)}, bf16[320,128]{1,0:T(8,128)(2,1)S(1)}, u32[]{:S(2)}, u32[]{:S(2)}) collective-permute-start(bf16[320,128]{1,0:T(8,128)(2,1)S(1)} %get-tuple-element.29), channel_id=1, source_target_pairs={{0,4},{4,0},{8,12},{12,8},{16,20},{20,16},{24,28},{28,24},{1,5},{5... | collective-permute-start | bytes 245768 | tf_op jit(solution)/shard_map/ppermute | solution.py:343
  2.1 1.7 %shard_map.95 = (bf16[6,640,128]{2,1,0:T(8,128)(2,1)S(1)}, f32[16,128]{1,0:T(8,128)S(1)}) custom-call(bf16[160,2048]{1,0:T(8,128)(2,1)} %refs_0_.5, bf16[160,2048]{1,0:T(8,128)(2,1)} %refs_1_.5, bf16[160,2048]{1,0:T(8,128)(2,1)} %refs_2_.3, s32[1280]{0:T(1024)} %refs_3_.1, bf16[320,128]{1,0:T(8,128)(2,1)S(1)} %get-tuple-element.27.refs_4_.refs_0_), custom_call_target="tpu_custom_call" | custom-call | flops 1100000000 | bytes 1971200 | tf_op jit(solution)/shard_map/pallas_call | solution.py:35
  3.8 0.0 collective-permute-done.refs_1_
  3.8 0.1 collective-permute-start.1
  4.0 0.5 %collective-permute-start.2 = (f32[16,160]{1,0:T(8,128)S(1)}, f32[16,160]{1,0:T(8,128)S(1)}, u32[]{:S(2)}, u32[]{:S(2)}) collective-permute-start(f32[16,160]{1,0:T(8,128)S(1)} %get-tuple-element.32.refs_3_), channel_id=1, source_target_pairs={{0,4},{4,0},{8,12},{12,8},{16,20},{20,16},{24,28},{28,24},{1,5},{5... | collective-permute-start | bytes 30728 | tf_op jit(solution)/shard_map/ppermute | solution.py:343
  4.5 2.6 %collective-permute-start.4 = (bf16[640,128]{1,0:T(8,128)(2,1)S(1)}, bf16[640,128]{1,0:T(8,128)(2,1)S(1)}, u32[]{:S(2)}, u32[]{:S(2)}) collective-permute-start(bf16[640,128]{1,0:T(8,128)(2,1)S(1)} %get-tuple-element.34.refs_6_.refs_3_.refs_4_), channel_id=1, source_target_pairs={{0,16},{4,20},{8,24},{12,28},{16,0},{20,4},{24,8},{28,12},{1,17},{... | collective-permute-start | bytes 491528 | tf_op jit(solution)/shard_map/ppermute | solution.py:343
  7.1 1.5 %collective-permute-start.3 = (bf16[640,128]{1,0:T(8,128)(2,1)S(1)}, bf16[640,128]{1,0:T(8,128)(2,1)S(1)}, u32[]{:S(2)}, u32[]{:S(2)}) collective-permute-start(bf16[640,128]{1,0:T(8,128)(2,1)S(1)} %get-tuple-element.34.refs_6_.refs_3_.refs_4_), channel_id=1, source_target_pairs={{0,8},{4,12},{8,0},{12,4},{16,24},{20,28},{24,16},{28,20},{1,9},{5... | collective-permute-start | bytes 491528 | tf_op jit(solution)/shard_map/ppermute | solution.py:343
  8.6 0.0 collective-permute-done.2.refs_5_
  8.6 1.2 %shard_map.97 = (f32[16,640]{1,0:T(8,128)S(1)}, f32[640,16]{1,0:T(8,128)S(1)}, bf16[4,640,128]{2,1,0:T(8,128)(2,1)S(1)}, bf16[4,128,640]{2,1,0:T(8,128)(2,1)S(1)...) custom-call(bf16[160,2048]{1,0:T(8,128)(2,1)S(1)} %copy-done, bf16[160,2048]{1,0:T(8,128)(2,1)S(1)} %copy-done.1, ...), custom_call_target="tpu_custom_call" | custom-call | flops 1100000000 | bytes 3133440 | tf_op jit(solution)/shard_map/pallas_call | solution.py:35
  9.8 1.6 %collective-permute-start.5 = (bf16[640,128]{1,0:T(8,128)(2,1)S(1)}, bf16[640,128]{1,0:T(8,128)(2,1)S(1)}, u32[]{:S(2)}, u32[]{:S(2)}) collective-permute-start(bf16[640,128]{1,0:T(8,128)(2,1)S(1)} %get-tuple-element.37), channel_id=1, source_target_pairs={{0,24},{4,28},{8,16},{12,20},{16,8},{20,12},{24,0},{28,4},{1,25},{... | collective-permute-start | bytes 491528 | tf_op jit(solution)/shard_map/ppermute | solution.py:343
  11.3 0.6 %collective-permute-done.4.refs_5_.refs_6_ = bf16[640,128]{1,0:T(8,128)(2,1)S(1)} collective-permute-done((bf16[640,128]{1,0:T(8,128)(2,1)S(1)}, bf16[640,128]{1,0:T(8,128)(2,1)S(1)}, u32[]{:S(2)}, u32[]{:S(2)}) %collective-permute-start.4) | collective-permute-done | bytes 163872 | tf_op jit(solution)/shard_map/ppermute | solution.py:343
  11.9 1.2 %shard_map.101.refs_7_ = bf16[640,128]{1,0:T(8,128)(2,1)S(1)} custom-call(f32[16,128]{1,0:T(8,128)S(1)} %get-tuple-element.28.refs_0_, bf16[4,640,128]{2,1,0:T(8,128)(2,1)S(1)} %get-tuple-element.35.refs_1_, bf16[6,640,128]{2,1,0:T(8,128)(2,1)S(1)} %collective-permute-done.1.refs_4_.refs_2_.refs_1_, bf16[4,128,640]{2,1,0:T(8,128)(2,1)S(1)} %get-tuple-element.38.refs_3_, ...), custom_call_target="tpu_custom_call" | custom-call | flops 550000000 | bytes 3162112 | tf_op jit(solution)/shard_map/pallas_call | solution.py:35
  13.0 1.8 %collective-permute-start.7 = (bf16[640,128]{1,0:T(8,128)(2,1)S(1)}, bf16[640,128]{1,0:T(8,128)(2,1)S(1)}, u32[]{:S(2)}, u32[]{:S(2)}) collective-permute-start(bf16[640,128]{1,0:T(8,128)(2,1)S(1)} %shard_map.101.refs_7_), channel_id=1, source_target_pairs={{0,16},{4,20},{8,24},{12,28},{16,0},{20,4},{24,8},{28,12},{1,17},{... | collective-permute-start | bytes 491528 | tf_op jit(solution)/shard_map/ppermute | solution.py:343
  14.9 1.2 %shard_map.102 = bf16[640,128]{1,0:T(8,128)(2,1)S(1)} custom-call(f32[16,128]{1,0:T(8,128)S(1)} %get-tuple-element.28.refs_0_, bf16[4,640,128]{2,1,0:T(8,128)(2,1)S(1)} %get-tuple-element.35.refs_1_, bf16[6,640,128]{2,1,0:T(8,128)(2,1)S(1)} %collective-permute-done.1.refs_4_.refs_2_.refs_1_, bf16[4,128,640]{2,1,0:T(8,128)(2,1)S(1)} %get-tuple-element.38.refs_3_, ...), custom_call_target="tpu_custom_call" | custom-call | flops 550000000 | bytes 3162112 | tf_op jit(solution)/shard_map/pallas_call | solution.py:35
  16.1 1.6 %collective-permute-start.6 = (bf16[640,128]{1,0:T(8,128)(2,1)S(1)}, bf16[640,128]{1,0:T(8,128)(2,1)S(1)}, u32[]{:S(2)}, u32[]{:S(2)}) collective-permute-start(bf16[640,128]{1,0:T(8,128)(2,1)S(1)} %shard_map.102), channel_id=1, source_target_pairs={{0,8},{4,12},{8,0},{12,4},{16,24},{20,28},{24,16},{28,20},{1,9},{5... | collective-permute-start | bytes 491528 | tf_op jit(solution)/shard_map/ppermute | solution.py:343
  17.6 1.2 %shard_map.98.refs_7_ = bf16[640,128]{1,0:T(8,128)(2,1)S(1)} custom-call(f32[16,128]{1,0:T(8,128)S(1)} %get-tuple-element.28.refs_0_, bf16[4,640,128]{2,1,0:T(8,128)(2,1)S(1)} %get-tuple-element.35.refs_1_, bf16[6,640,128]{2,1,0:T(8,128)(2,1)S(1)} %collective-permute-done.1.refs_4_.refs_2_.refs_1_, bf16[4,128,640]{2,1,0:T(8,128)(2,1)S(1)} %get-tuple-element.38.refs_3_, ...), custom_call_target="tpu_custom_call" | custom-call | flops 550000000 | bytes 3162112 | tf_op jit(solution)/shard_map/pallas_call | solution.py:35
  18.8 1.8 %collective-permute-start.8 = (bf16[640,128]{1,0:T(8,128)(2,1)S(1)}, bf16[640,128]{1,0:T(8,128)(2,1)S(1)}, u32[]{:S(2)}, u32[]{:S(2)}) collective-permute-start(bf16[640,128]{1,0:T(8,128)(2,1)S(1)} %shard_map.98.refs_7_), channel_id=1, source_target_pairs={{0,24},{4,28},{8,16},{12,20},{16,8},{20,12},{24,0},{28,4},{1,25},{... | collective-permute-start | bytes 491528 | tf_op jit(solution)/shard_map/ppermute | solution.py:343
  20.6 1.4 %shard_map.99.refs_7_.refs_0_ = f32[640,128]{1,0:T(8,128)S(1)} custom-call(f32[16,128]{1,0:T(8,128)S(1)} %get-tuple-element.28.refs_0_, bf16[4,640,128]{2,1,0:T(8,128)(2,1)S(1)} %get-tuple-element.35.refs_1_, bf16[6,640,128]{2,1,0:T(8,128)(2,1)S(1)} %collective-permute-done.1.refs_4_.refs_2_.refs_1_, bf16[4,128,640]{2,1,0:T(8,128)(2,1)S(1)} %get-tuple-element.38.refs_3_, ...), custom_call_target="tpu_custom_call" | custom-call | flops 550000000 | bytes 3162112 | tf_op jit(solution)/shard_map/pallas_call | solution.py:35
  22.0 2.4 %shard_map.100.refs_4_ = bf16[2,640,128]{2,1,0:T(8,128)(2,1)S(1)} custom-call(f32[16,128]{1,0:T(8,128)S(1)} %get-tuple-element.28.refs_0_, bf16[6,640,128]{2,1,0:T(8,128)(2,1)S(1)} %collective-permute-done.1.refs_4_.refs_2_.refs_1_, f32[640,16]{1,0:T(8,128)S(1)} %get-tuple-element.36.refs_2_, bf16[640,128]{1,0:T(8,128)(2,1)S(1)} %get-tuple-element.34.refs_6_.refs_3_.refs_4_, ...), custom_call_target="tpu_custom_call" | custom-call | flops 2750000128 | bytes 1687552 | tf_op jit(solution)/shard_map/pallas_call | solution.py:35
  24.5 0.6 %collective-permute-done.8.refs_3_ = bf16[640,128]{1,0:T(8,128)(2,1)S(1)} collective-permute-done((bf16[640,128]{1,0:T(8,128)(2,1)S(1)}, bf16[640,128]{1,0:T(8,128)(2,1)S(1)}, u32[]{:S(2)}, u32[]{:S(2)}) %collective-permute-start.8) | collective-permute-done | bytes 163872 | tf_op jit(solution)/shard_map/ppermute | solution.py:343
  25.1 0.1 shard_map.103
  25.2 0.1 collective-permute-start.9
  25.3 0.5 %collective-permute-start.10 = (bf16[320,128]{1,0:T(8,128)(2,1)S(1)}, bf16[320,128]{1,0:T(8,128)(2,1)S(1)}, u32[]{:S(2)}, u32[]{:S(2)}) collective-permute-start(bf16[320,128]{1,0:T(8,128)(2,1)S(1)} %get-tuple-element.44), channel_id=1, source_target_pairs={{0,4},{4,0},{8,12},{12,8},{16,20},{20,16},{24,28},{28,24},{1,5},{5... | collective-permute-start | bytes 245768 | tf_op jit(solution)/shard_map/ppermute | solution.py:343
  25.7 1.2 %collective-permute-done.10.refs_1_ = bf16[320,128]{1,0:T(8,128)(2,1)S(1)} collective-permute-done((bf16[320,128]{1,0:T(8,128)(2,1)S(1)}, bf16[320,128]{1,0:T(8,128)(2,1)S(1)}, u32[]{:S(2)}, u32[]{:S(2)}) %collective-permute-start.10) | collective-permute-done | bytes 81952 | tf_op jit(solution)/shard_map/ppermute | solution.py:343
  27.0 0.1 shard_map.104
  27.1 2.6 %collective-permute-start.11 = (bf16[2,40,256]{2,1,0:T(8,128)(2,1)S(1)}, bf16[2,40,256]{2,1,0:T(8,128)(2,1)S(1)}, u32[]{:S(2)}, u32[]{:S(2)}) collective-permute-start(bf16[2,40,256]{2,1,0:T(8,128)(2,1)S(1)} %get-tuple-element.46), channel_id=1, source_target_pairs={{0,2},{1,3},{2,0},{3,1},{4,6},{5,7},{6,4},{7,5},{8,10},{9,11},{10,... | collective-permute-start | bytes 122888 | tf_op jit(solution)/shard_map/ppermute | solution.py:343
  29.7 1.4 %collective-permute-start.12 = (bf16[2,40,256]{2,1,0:T(8,128)(2,1)S(1)}, bf16[2,40,256]{2,1,0:T(8,128)(2,1)S(1)}, u32[]{:S(2)}, u32[]{:S(2)}) collective-permute-start(bf16[2,40,256]{2,1,0:T(8,128)(2,1)S(1)} %get-tuple-element.47), channel_id=1, source_target_pairs={{0,3},{1,2},{2,1},{3,0},{4,7},{5,6},{6,5},{7,4},{8,11},{9,10},{10,... | collective-permute-start | bytes 122888 | tf_op jit(solution)/shard_map/ppermute | solution.py:343
  31.1 0.2 collective-permute-start.13
  31.3 3.4 %shard_map.105.refs_4_ = bf16[160,2048]{1,0:T(8,128)(2,1)} custom-call(f32[16,128]{1,0:T(8,128)S(1)} %get-tuple-element.28.refs_0_, bf16[4,640,128]{2,1,0:T(8,128)(2,1)S(1)} %get-tuple-element.35.refs_1_, f32[640,16]{1,0:T(8,128)S(1)} %get-tuple-element.36.refs_2_, bf16[2,640,128]{2,1,0:T(8,128)(2,1)S(1)} %collective-permute-done.9.refs_3_, ...), custom_call_target="tpu_custom_call" | custom-call | flops 3300000000 | bytes 1687552 | tf_op jit(solution)/shard_map/pallas_call | solution.py:35
  34.7 0.8 %collective-permute-done.12.refs_2_ = bf16[2,40,256]{2,1,0:T(8,128)(2,1)S(1)} collective-permute-done((bf16[2,40,256]{2,1,0:T(8,128)(2,1)S(1)}, bf16[2,40,256]{2,1,0:T(8,128)(2,1)S(1)}, u32[]{:S(2)}, u32[]{:S(2)}) %collective-permute-start.12) | collective-permute-done | bytes 40992 | tf_op jit(solution)/shard_map/ppermute | solution.py:343
  35.5 0.7 %shard_map.106 = (bf16[40,1024]{1,0:T(8,128)(2,1)}, bf16[40,1024]{1,0:T(8,128)(2,1)}) custom-call(bf16[2,40,256]{2,1,0:T(8,128)(2,1)S(1)} %get-tuple-element.45.refs_8_.refs_0_, bf16[2,40,256]{2,1,0:T(8,128)(2,1)S(1)} %collective-permute-done.11.refs_1_, bf16[2,40,256]{2,1,0:T(8,128)(2,1)S(1)} %collective-permute-done.12.refs_2_, ...), custom_call_target="tpu_custom_call" | custom-call | flops 110000000 | bytes 163840 | tf_op jit(solution)/shard_map/pallas_call | solution.py:35
  (17 shorter events, 0.0 us)
Async XLA Ops:
  1.5 2.3 %collective-permute-start = (bf16[320,128]{1,0:T(8,128)(2,1)S(1)}, bf16[320,128]{1,0:T(8,128)(2,1)S(1)}, u32[]{:S(2)}, u32[]{:S(2)}) collective-permute-start(bf16[320,128]{1,0:T(8,128)(2,1)S(1)} %get-tuple-element.29), channel_id=1, source_target_pairs={{0,4},{4,0},{8,12},{12,8},{16,20},{20,16},{24,28},{28,24},{1,5},{5... | collective-permute-start | bytes 245768 | tf_op jit(solution)/shard_map/ppermute | solution.py:343
  2.0 1.9 %copy-start.3 = (f32[160,16]{0,1:T(8,128)S(1)}, f32[160,16]{0,1:T(8,128)}, u32[]{:S(2)}) copy-start(f32[160,16]{0,1:T(8,128)} %param.13) | copy-start | bytes 30724
  2.0 6.5 %copy-start = (bf16[160,2048]{1,0:T(8,128)(2,1)S(1)}, bf16[160,2048]{1,0:T(8,128)(2,1)}, u32[]{:S(2)}) copy-start(bf16[160,2048]{1,0:T(8,128)(2,1)} %refs_0_.5) | copy-start | bytes 1966084
  2.0 6.5 %copy-start.1 = (bf16[160,2048]{1,0:T(8,128)(2,1)S(1)}, bf16[160,2048]{1,0:T(8,128)(2,1)}, u32[]{:S(2)}) copy-start(bf16[160,2048]{1,0:T(8,128)(2,1)} %refs_1_.5) | copy-start | bytes 1966084
  2.0 6.5 %copy-start.2 = (bf16[160,2048]{1,0:T(8,128)(2,1)S(1)}, bf16[160,2048]{1,0:T(8,128)(2,1)}, u32[]{:S(2)}) copy-start(bf16[160,2048]{1,0:T(8,128)(2,1)} %refs_2_.3) | copy-start | bytes 1966084
  3.8 4.8 %collective-permute-start.1 = (bf16[6,640,128]{2,1,0:T(8,128)(2,1)S(1)}, bf16[6,640,128]{2,1,0:T(8,128)(2,1)S(1)}, u32[]{:S(2)}, u32[]{:S(2)}) collective-permute-start(bf16[6,640,128]{2,1,0:T(8,128)(2,1)S(1)} %get-tuple-element.33), channel_id=1, source_target_pairs={{0,4},{4,0},{8,12},{12,8},{16,20},{20,16},{24,28},{28,24},{1,5},{5... | collective-permute-start | bytes 2949128 | tf_op jit(solution)/shard_map/ppermute | solution.py:343
  4.0 4.6 %collective-permute-start.2 = (f32[16,160]{1,0:T(8,128)S(1)}, f32[16,160]{1,0:T(8,128)S(1)}, u32[]{:S(2)}, u32[]{:S(2)}) collective-permute-start(f32[16,160]{1,0:T(8,128)S(1)} %get-tuple-element.32.refs_3_), channel_id=1, source_target_pairs={{0,4},{4,0},{8,12},{12,8},{16,20},{20,16},{24,28},{28,24},{1,5},{5... | collective-permute-start | bytes 30728 | tf_op jit(solution)/shard_map/ppermute | solution.py:343
  4.5 7.4 %collective-permute-start.4 = (bf16[640,128]{1,0:T(8,128)(2,1)S(1)}, bf16[640,128]{1,0:T(8,128)(2,1)S(1)}, u32[]{:S(2)}, u32[]{:S(2)}) collective-permute-start(bf16[640,128]{1,0:T(8,128)(2,1)S(1)} %get-tuple-element.34.refs_6_.refs_3_.refs_4_), channel_id=1, source_target_pairs={{0,16},{4,20},{8,24},{12,28},{16,0},{20,4},{24,8},{28,12},{1,17},{... | collective-permute-start | bytes 491528 | tf_op jit(solution)/shard_map/ppermute | solution.py:343
  7.1 7.8 %collective-permute-start.3 = (bf16[640,128]{1,0:T(8,128)(2,1)S(1)}, bf16[640,128]{1,0:T(8,128)(2,1)S(1)}, u32[]{:S(2)}, u32[]{:S(2)}) collective-permute-start(bf16[640,128]{1,0:T(8,128)(2,1)S(1)} %get-tuple-element.34.refs_6_.refs_3_.refs_4_), channel_id=1, source_target_pairs={{0,8},{4,12},{8,0},{12,4},{16,24},{20,28},{24,16},{28,20},{1,9},{5... | collective-permute-start | bytes 491528 | tf_op jit(solution)/shard_map/ppermute | solution.py:343
  9.8 7.9 %collective-permute-start.5 = (bf16[640,128]{1,0:T(8,128)(2,1)S(1)}, bf16[640,128]{1,0:T(8,128)(2,1)S(1)}, u32[]{:S(2)}, u32[]{:S(2)}) collective-permute-start(bf16[640,128]{1,0:T(8,128)(2,1)S(1)} %get-tuple-element.37), channel_id=1, source_target_pairs={{0,24},{4,28},{8,16},{12,20},{16,8},{20,12},{24,0},{28,4},{1,25},{... | collective-permute-start | bytes 491528 | tf_op jit(solution)/shard_map/ppermute | solution.py:343
  13.0 11.4 %collective-permute-start.7 = (bf16[640,128]{1,0:T(8,128)(2,1)S(1)}, bf16[640,128]{1,0:T(8,128)(2,1)S(1)}, u32[]{:S(2)}, u32[]{:S(2)}) collective-permute-start(bf16[640,128]{1,0:T(8,128)(2,1)S(1)} %shard_map.101.refs_7_), channel_id=1, source_target_pairs={{0,16},{4,20},{8,24},{12,28},{16,0},{20,4},{24,8},{28,12},{1,17},{... | collective-permute-start | bytes 491528 | tf_op jit(solution)/shard_map/ppermute | solution.py:343
  16.1 8.4 %collective-permute-start.6 = (bf16[640,128]{1,0:T(8,128)(2,1)S(1)}, bf16[640,128]{1,0:T(8,128)(2,1)S(1)}, u32[]{:S(2)}, u32[]{:S(2)}) collective-permute-start(bf16[640,128]{1,0:T(8,128)(2,1)S(1)} %shard_map.102), channel_id=1, source_target_pairs={{0,8},{4,12},{8,0},{12,4},{16,24},{20,28},{24,16},{28,20},{1,9},{5... | collective-permute-start | bytes 491528 | tf_op jit(solution)/shard_map/ppermute | solution.py:343
  18.8 6.3 %collective-permute-start.8 = (bf16[640,128]{1,0:T(8,128)(2,1)S(1)}, bf16[640,128]{1,0:T(8,128)(2,1)S(1)}, u32[]{:S(2)}, u32[]{:S(2)}) collective-permute-start(bf16[640,128]{1,0:T(8,128)(2,1)S(1)} %shard_map.98.refs_7_), channel_id=1, source_target_pairs={{0,24},{4,28},{8,16},{12,20},{16,8},{20,12},{24,0},{28,4},{1,25},{... | collective-permute-start | bytes 491528 | tf_op jit(solution)/shard_map/ppermute | solution.py:343
  25.2 6.1 %collective-permute-start.9 = (bf16[2,640,128]{2,1,0:T(8,128)(2,1)S(1)}, bf16[2,640,128]{2,1,0:T(8,128)(2,1)S(1)}, u32[]{:S(2)}, u32[]{:S(2)}) collective-permute-start(bf16[2,640,128]{2,1,0:T(8,128)(2,1)S(1)} %shard_map.100.refs_4_), channel_id=1, source_target_pairs={{0,4},{4,0},{8,12},{12,8},{16,20},{20,16},{24,28},{28,24},{1,5},{5... | collective-permute-start | bytes 983048 | tf_op jit(solution)/shard_map/ppermute | solution.py:343
  25.3 1.7 %collective-permute-start.10 = (bf16[320,128]{1,0:T(8,128)(2,1)S(1)}, bf16[320,128]{1,0:T(8,128)(2,1)S(1)}, u32[]{:S(2)}, u32[]{:S(2)}) collective-permute-start(bf16[320,128]{1,0:T(8,128)(2,1)S(1)} %get-tuple-element.44), channel_id=1, source_target_pairs={{0,4},{4,0},{8,12},{12,8},{16,20},{20,16},{24,28},{28,24},{1,5},{5... | collective-permute-start | bytes 245768 | tf_op jit(solution)/shard_map/ppermute | solution.py:343
  27.1 7.7 %collective-permute-start.11 = (bf16[2,40,256]{2,1,0:T(8,128)(2,1)S(1)}, bf16[2,40,256]{2,1,0:T(8,128)(2,1)S(1)}, u32[]{:S(2)}, u32[]{:S(2)}) collective-permute-start(bf16[2,40,256]{2,1,0:T(8,128)(2,1)S(1)} %get-tuple-element.46), channel_id=1, source_target_pairs={{0,2},{1,3},{2,0},{3,1},{4,6},{5,7},{6,4},{7,5},{8,10},{9,11},{10,... | collective-permute-start | bytes 122888 | tf_op jit(solution)/shard_map/ppermute | solution.py:343
  29.7 5.8 %collective-permute-start.12 = (bf16[2,40,256]{2,1,0:T(8,128)(2,1)S(1)}, bf16[2,40,256]{2,1,0:T(8,128)(2,1)S(1)}, u32[]{:S(2)}, u32[]{:S(2)}) collective-permute-start(bf16[2,40,256]{2,1,0:T(8,128)(2,1)S(1)} %get-tuple-element.47), channel_id=1, source_target_pairs={{0,3},{1,2},{2,1},{3,0},{4,7},{5,6},{6,5},{7,4},{8,11},{9,10},{10,... | collective-permute-start | bytes 122888 | tf_op jit(solution)/shard_map/ppermute | solution.py:343
  31.1 4.4 %collective-permute-start.13 = (bf16[2,40,256]{2,1,0:T(8,128)(2,1)S(1)}, bf16[2,40,256]{2,1,0:T(8,128)(2,1)S(1)}, u32[]{:S(2)}, u32[]{:S(2)}) collective-permute-start(bf16[2,40,256]{2,1,0:T(8,128)(2,1)S(1)} %get-tuple-element.48), channel_id=1, source_target_pairs={{0,1},{1,0},{2,3},{3,2},{4,5},{5,4},{6,7},{7,6},{8,9},{9,8},{10,11... | collective-permute-start | bytes 122888 | tf_op jit(solution)/shard_map/ppermute | solution.py:343

commit v4 on v3

--- a/solution.py
+++ b/solution.py
@@ -67,23 +67,12 @@
         each.wait()
 
 
-def pack_kv_kernel(k_hbm, v_hbm, same, other, sems):
-    rows = k_hbm.shape[0]
-    c = parity()
-    pairs = [
-        (src.at[:, columns_of(group)], ref.at[pl.ds(kind * rows, rows), :])
-        for ref, group in ((other, 1 - c), (same, c))
-        for kind, src in enumerate((k_hbm, v_hbm))
-    ]
-    copy_all(pairs, sems)
-
-
 def run_starts(pos_ref, tokens, shift):
     ctx = lax.axis_index("ctx")
     return pos_ref[jnp.bitwise_xor(ctx, shift) * tokens]
 
 
-def pack_q_kernel(heads, q_hbm, g_hbm, o_hbm, pos_hbm, out, larger, pos, sems):
+def pack_q_kernel(heads, q_hbm, g_hbm, pos_hbm, out, larger, pos, sems):
     tokens = q_hbm.shape[0]
     half = tokens // 2
     group = 1 - parity()
@@ -92,7 +81,7 @@
             src.at[pl.ds(w * half, half), columns_of(group * heads + h)],
             out.at[2 * kind + w, pl.ds(h * half, half), :],
         )
-        for kind, src in enumerate((q_hbm, g_hbm, o_hbm))
+        for kind, src in enumerate((q_hbm, g_hbm))
         for w in range(2)
         for h in range(heads)
     ]
@@ -112,42 +101,44 @@
     return parts
 
 
-def rows_kernel(heads, q_ref, g_ref, o_ref, own_log, sib, sib_log, kv, *refs):
-    out, turned_out, own, own_t, sib_t, kv_out = refs
+def rows_kernel(heads, q_ref, g_ref, o_ref, log, sib, kv, *refs):
+    own_rows, other_rows, own, own_t, sib_t, kv_out = refs
     lanes = own.shape[1]
     half = lanes // heads
     c = parity()
     ones = jnp.ones((8, HEAD_SIZE), BF16)
-    groups, tokens = own_log.shape
+    groups, tokens = log.shape
     token = lax.broadcasted_iota(jnp.int32, (tokens, lanes), 0)
     lane = lax.broadcasted_iota(jnp.int32, (tokens, lanes), 1)
     head = lax.broadcasted_iota(jnp.int32, (groups, lanes), 0)
-    wanted = lax.div(lax.broadcasted_iota(jnp.int32, (groups, lanes), 1), half) + c * heads
-
-    def stacked(ref, w):
+    head_of_lane = lax.div(lax.broadcasted_iota(jnp.int32, (groups, lanes), 1), half)
+    logs = split_bf16(jnp.clip(log[...], -1e30, 1e30), 3)
+    for w in range(2):
         r = slice(w * half, (w + 1) * half)
-        return jnp.concatenate([ref[r, columns_of(c * heads + h)] for h in range(heads)], axis=0)
-
-    for b, (log, turned) in enumerate(((own_log, own_t), (sib_log, sib_t))):
-        parts = split_bf16(jnp.clip(log[...], -1e30, 1e30), 3)
-        for w in range(2):
-            if b == 0:
-                q, g, o = (stacked(ref, w) for ref in (q_ref, g_ref, o_ref))
+        place = jnp.where(token == lax.rem(lane, half) + w * half, 1.0, 0.0).astype(BF16)
+        spread = sum(jnp.dot(part, place, preferred_element_type=F32) for part in logs)
+        for out, group in ((own_rows, c), (other_rows, 1 - c)):
+            cols = [columns_of(group * heads + h) for h in range(heads)]
+            g, o = (
+                jnp.concatenate([ref[r, col] for col in cols], axis=0) for ref in (g_ref, o_ref)
+            )
+            if out is own_rows:
+                q = jnp.concatenate([q_ref[r, col] for col in cols], axis=0)
                 own[w] = q
                 own[2 + w] = g
-            else:
-                q, g, o = (sib[2 * kind + w] for kind in range(3))
-            turned[w] = q.T
-            turned[2 + w] = g.T
-            place = jnp.where(token == lax.rem(lane, half) + w * half, 1.0, 0.0).astype(BF16)
-            spread = sum(jnp.dot(part, place, preferred_element_type=F32) for part in parts)
-            row = jnp.sum(jnp.where(head == wanted, spread, 0.0), axis=0, keepdims=True)
-            out[4 * b + w : 4 * b + w + 1, :] = row * LOG2E
+                own_t[w] = q.T
+                own_t[2 + w] = g.T
+            mine = head == head_of_lane + group * heads
+            row = jnp.sum(jnp.where(mine, spread, 0.0), axis=0, keepdims=True)
+            out[w : w + 1, :] = row * LOG2E
             delta = g.astype(F32) * o.astype(F32)
             row = sum(nt(ones, part) for part in split_bf16(delta, 2))
-            out[4 * b + 2 + w : 4 * b + 3 + w, :] = row[0:1]
-    out[8:16, :] = lax.rem(lax.broadcasted_iota(jnp.int32, (8, lanes), 1), half).astype(F32)
-    turned_out[...] = out[...].T
+            out[2 + w : 3 + w, :] = row[0:1]
+    spot = lax.rem(lax.broadcasted_iota(jnp.int32, (4, lanes), 1), half).astype(F32)
+    own_rows[4:8, :] = spot
+    other_rows[4:8, :] = spot
+    for i in range(4):
+        sib_t[i] = sib[i].T
     kv_out[...] = kv[...]
 
 
@@ -163,12 +154,11 @@
     return piece[pl.ds(at, half), :], piece[pl.ds(rows + at, half), :]
 
 
-def kv_grad_kernel(pair, larger, own, sib, own_t, sib_t, vec, piece, out):
+def kv_grad_kernel(pair, larger, own, sib, own_t, sib_t, own_rows, sib_rows, piece, *outs):
     tokens = piece.shape[0] // 4
     half = tokens // 2
-    rows = 2 * tokens
     lanes = own.shape[1]
-    stacks, turned = (own, sib), (own_t, sib_t)
+    stacks, turned, vectors = (own, sib), (own_t, sib_t), (own_rows, sib_rows)
     first = [one_run(piece, tokens, half, a, 0) for a in range(2)]
     k, v = (jnp.concatenate(x, axis=0) for x in zip(*first))
     jobs = [(k, v, b, 1, None) for b in range(2)]
@@ -196,10 +186,10 @@
     for i, job in enumerate(jobs):
         (s, dp), ahead = ahead, products(jobs[i + 1]) if i + 1 < len(jobs) else None
         _, _, b, which, place = job
-        p = jnp.exp2(s * EXP2_SCALE - vec[pl.ds(4 * b + which, 1), :])
+        p = jnp.exp2(s * EXP2_SCALE - vectors[b][pl.ds(which, 1), :])
         if place is not None and isinstance(which, int):
             p = jnp.where(seen, p, 0.0)
-        ds = (p * (dp - vec[pl.ds(4 * b + 2 + which, 1), :])).astype(BF16)
+        ds = (p * (dp - vectors[b][pl.ds(2 + which, 1), :])).astype(BF16)
         value_term = jnp.dot(p.astype(BF16), stacks[b][2 + which], preferred_element_type=F32)
         key_term = jnp.dot(ds, stacks[b][which], preferred_element_type=F32)
         both = key_term, value_term
@@ -213,17 +203,20 @@
             sums[a, 0].append([jnp.where(second, 0.0, x) for x in both])
             sums[a, 1].append([jnp.where(second, x, 0.0) for x in both])
     for (a, w), parts in sums.items():
-        at = a * tokens + w * half
+        out = outs[a % len(outs)]
+        at = w * half + (a * 2 * tokens if len(outs) == 1 else 0)
         out[at : at + half, :] = (sum(x[0] for x in parts) * SCALE).astype(out.dtype)
-        out[rows + at : rows + at + half, :] = sum(x[1] for x in parts).astype(out.dtype)
-
-
-def q_grads(b, larger, stack, columns, pieces):
+        at += tokens
+        out[at : at + half, :] = sum(x[1] for x in parts).astype(out.dtype)
+
+
+def q_grads(b, larger, stack, vectors, pieces):
     tokens = pieces[0].shape[0] // 4
     half = tokens // 2
     rows = 2 * tokens
     grads = [0.0, 0.0]
-    spot = columns[:, 8:9]
+    columns = vectors[...].T
+    spot = columns[:, 4:5]
     for start in range(0, len(pieces), 4):
         some = pieces[start : start + 4]
 
@@ -247,22 +240,22 @@
         for which, run, limit in ((0, 0, least[0]), (1, 0, None), (1, 1, least[1])):
             k, v = runs[run]
             p = jnp.exp2(
-                nt(stack[which], k) * EXP2_SCALE - columns[:, 4 * b + which : 4 * b + which + 1]
+                nt(stack[which], k) * EXP2_SCALE - columns[:, which : which + 1]
             )
             if limit is not None:
                 p = jnp.where(spot >= limit, p, 0.0)
-            at = 4 * b + 2 + which
-            ds = (p * (nt(stack[2 + which], v) - columns[:, at : at + 1])).astype(BF16)
+            delta = columns[:, 2 + which : 3 + which]
+            ds = (p * (nt(stack[2 + which], v) - delta)).astype(BF16)
             grads[which] = grads[which] + jnp.dot(ds, k, preferred_element_type=F32)
     return [(x * SCALE).astype(BF16) for x in grads]
 
 
-def sib_grad_kernel(larger, stack, columns, *refs):
+def sib_grad_kernel(larger, stack, vectors, *refs):
     pieces, out = refs[:-1], refs[-1]
-    out[0], out[1] = q_grads(1, larger, stack, columns, pieces)
-
-
-def own_grad_kernel(heads, larger, stack, columns, other, *refs):
+    out[0], out[1] = q_grads(1, larger, stack, vectors, pieces)
+
+
+def own_grad_kernel(heads, larger, stack, vectors, other, *refs):
     pieces, (out, held, sems) = refs[:-3], refs[-3:]
     half = out.shape[0] // 2
     c = parity()
@@ -284,43 +277,39 @@
     second = copies(held, c)
     for each in first:
         each.start()
-    held[0], held[1] = q_grads(0, larger, stack, columns, pieces)
+    held[0], held[1] = q_grads(0, larger, stack, vectors, pieces)
     for each in second:
         each.start()
     for each in first + second:
         each.wait()
 
 
-def merge_kv_kernel(same_ref, other_ref, log, out, log_out):
-    log_out[...] = log[...]
-    tokens = same_ref.shape[0] // 2
-    for a, ref in enumerate((same_ref, other_ref)):
-        for kind in range(2):
-            at = (2 * kind + a) * tokens
-            out[at : at + tokens, :] = ref[kind * tokens : (kind + 1) * tokens, :]
+def merge_kv_kernel(*refs):
+    parts, out = refs[:-1], refs[-1]
+    tokens = parts[0].shape[0]
+    cols = columns_of(parity())
+    for i, ref in enumerate(parts):
+        out[i * tokens : (i + 1) * tokens, :] = ref[:, cols]
 
 
 def sum_kernel(*refs):
-    parts, (same_out, other_out) = refs[:-2], refs[-2:]
-    tokens = parts[0].shape[0] // 4
-    for a, out in enumerate((same_out, other_out)):
-        for kind in range(2):
-            at = (2 * kind + a) * tokens
-            value = parts[0][at : at + tokens, :]
-            for part in parts[1:]:
-                value = value + part[at : at + tokens, :].astype(F32)
-            out[kind * tokens : (kind + 1) * tokens, :] = value.astype(BF16)
-
-
-def share_kernel(tp_count, same, other, *refs):
+    parts, outs = refs[:-2], refs[-2:]
+    size = outs[0].shape[0]
+    for a, out in enumerate(outs):
+        value = parts[a][...]
+        for part in parts[2:]:
+            value = value + part[a * size : (a + 1) * size, :].astype(F32)
+        out[...] = value
+
+
+def share_kernel(tp_count, same, same_last, other, other_last, *refs):
     outs, (total,) = refs[:tp_count], refs[tp_count:]
     tokens = same.shape[0] // 2
     share = tokens // tp_count
     c = parity()
     z = lax.axis_index("tp")
-    for ref, group in ((same, c), (other, 1 - c)):
-        cols = pl.ds(pl.multiple_of(group * HEAD_SIZE, HEAD_SIZE), HEAD_SIZE)
-        total[:, cols] = ref[...].astype(F32)
+    for ref, last, group in ((same, same_last, c), (other, other_last, 1 - c)):
+        total[:, columns_of(group)] = ref[...] + last[...].astype(F32)
     for m, out in enumerate(outs):
         start = jnp.bitwise_xor(z, m) * share
         for kind in range(2):
@@ -353,37 +342,28 @@
 
     half_piece = ((2 * tokens, HEAD_SIZE), BF16)
     piece = ((4 * tokens, HEAD_SIZE), BF16)
-    stack = ((6, lanes, HEAD_SIZE), BF16)
-    kv_same, kv_other = call(
-        pack_kv_kernel,
-        [half_piece] * 2,
-        [],
-        [pltpu.SemaphoreType.DMA((4,))],
-        far=[keys, values],
-    )
+    stack = ((4, lanes, HEAD_SIZE), BF16)
     other, larger = call(
         functools.partial(pack_q_kernel, heads),
         [stack, ((2 * n, HEAD_SIZE), F32)],
         [],
-        [pltpu.SMEM(positions.shape, jnp.int32), pltpu.SemaphoreType.DMA((6 * heads + 1,))],
+        [pltpu.SMEM(positions.shape, jnp.int32), pltpu.SemaphoreType.DMA((4 * heads + 1,))],
         cost=1.0,
-        far=[queries, output_grad, attn_output, positions],
-        after=[kv_same],
-    )
-    kv_pair, other = lax.optimization_barrier((swap(kv_other, "ctx", 1), other))
-    kv_chip, logs = call(
-        merge_kv_kernel,
-        [piece, (log_sums.T.shape, F32)],
-        [kv_same, kv_pair, log_sums.T],
-    )
+        far=[queries, output_grad, positions],
+    )
+    pair_keys, pair_values = swap(keys, "ctx", 1), swap(values, "ctx", 1)
+    other, pair_keys, pair_values = lax.optimization_barrier((other, pair_keys, pair_values))
+    (kv_chip,) = call(merge_kv_kernel, [piece], [keys, pair_keys, values, pair_values])
     sib = swap(other, "ctx", 1)
     turned = ((4, HEAD_SIZE, lanes), BF16)
-    vec, columns, own, own_t, sib_t, kv_late = call(
+    vectors = ((8, lanes), F32)
+    own_rows, other_rows, own, own_t, sib_t, kv_late = call(
         functools.partial(rows_kernel, heads),
-        [((16, lanes), F32), ((lanes, 16), F32), ((4, lanes, HEAD_SIZE), BF16), turned, turned, piece],
-        [queries, output_grad, attn_output, logs, sib, swap(logs, "ctx", 1), kv_chip],
+        [vectors, vectors, stack, turned, turned, piece],
+        [queries, output_grad, attn_output, log_sums.T, sib, kv_chip],
         cost=1.0,
     )
+    sib_rows = swap(other_rows, "ctx", 1)
     late = n // 2 - 1
     pieces = {
         pair: swap(kv_late if pair == late else kv_chip, "ctx", 2 * pair)
@@ -392,45 +372,49 @@
     pieces = [kv_chip] + [pieces[pair] for pair in range(1, n // 2)]
 
     def kv_grads(pair, after=()):
-        (out,) = call(
+        if pair in (0, late):
+            outs = [(half_piece[0], BF16 if pair else F32)] * 2
+        else:
+            outs = [piece]
+        return call(
             functools.partial(kv_grad_kernel, pair),
-            [(piece[0], BF16 if pair else F32)],
-            [larger, own, sib, own_t, sib_t, vec, pieces[pair]],
+            outs,
+            [larger, own, sib, own_t, sib_t, own_rows, sib_rows, pieces[pair]],
             cost=0.5,
             after=after,
         )
-        return out
 
     partials = {}
     for pair in reversed(range(1, late)):
-        partials[pair] = kv_grads(pair, [partials[pair + 1]] if pair + 1 < late else [])
+        partials[pair] = kv_grads(pair, partials[pair + 1] if pair + 1 < late else [])
     partials[late] = kv_grads(late)
-    local = kv_grads(0, [partials[late]])
-    received = [swap(partials[pair], "ctx", 2 * pair) for pair in range(1, n // 2)]
-
+    local = kv_grads(0, partials[late][:1])
+    received = [swap(partials[pair][0], "ctx", 2 * pair) for pair in range(1, late)]
+    last = [swap(x, "ctx", 2 * late + a) for a, x in enumerate(partials[late])]
+
+    sums = ((2 * tokens, HEAD_SIZE), F32)
+    sum_same, sum_other = call(sum_kernel, [sums] * 2, [*local, *received])
+    sum_pair = swap(sum_other, "ctx", 1)
     (dq_sib,) = call(
         sib_grad_kernel,
         [((2, lanes, HEAD_SIZE), BF16)],
-        [larger, sib, columns] + pieces,
+        [larger, sib, sib_rows] + pieces,
         cost=2.5,
-        after=[local],
-    )
-    sum_same, sum_other = call(
-        sum_kernel, [half_piece] * 2, [local] + received, after=[dq_sib]
-    )
-    dq_sib, sum_other = lax.optimization_barrier((dq_sib, sum_other))
-    dq_other = swap(dq_sib, "ctx", 1)
+        after=[sum_same],
+    )
     share = ((2, tokens // tp_count, 2 * HEAD_SIZE), BF16)
     shares = call(
         functools.partial(share_kernel, tp_count),
         [share] * tp_count,
-        [sum_same, swap(sum_other, "ctx", 1)],
+        [sum_same, last[0], sum_pair, last[1]],
         [pltpu.VMEM((2 * tokens, 2 * HEAD_SIZE), F32)],
     )
+    dq_sib, *shares = lax.optimization_barrier((dq_sib, *shares))
+    dq_other = swap(dq_sib, "ctx", 1)
     (query_grad,) = call(
         functools.partial(own_grad_kernel, heads),
         [(queries.shape, BF16)],
-        [larger, own, columns, dq_other] + pieces,
+        [larger, own, own_rows, dq_other] + pieces,
         [pltpu.VMEM((2, lanes, HEAD_SIZE), BF16), pltpu.SemaphoreType.DMA((4 * heads,))],
         cost=3.0,
         after=[shares[0]],

time: 36.4 us -> 34.4 us (0.945)
  Pallas kernels: 15.4 us -> 14 us
  starting transfers between devices: 16.8 us -> 15.7 us
  waiting for transfers between devices: 3.23 us -> 3.68 us
    pallas_call x13 -> x12, Pallas kernels: 15.4 us -> 14 us  [call(): pl.pallas_call(body, cost_estimate=pl.CostEstimate(flops=int(cost * FLOPS...]
    ppermute x14 -> x16, starting transfers between devices: 16.8 us -> 15.7 us  [swap(): return lax.ppermute(x, axis, [(i, i ^ shift) for i in range(count)])]
    ppermute x14 -> x16, waiting for transfers between devices: 3.23 us -> 3.68 us  [swap(): return lax.ppermute(x, axis, [(i, i ^ shift) for i in range(count)])]
  transfers between devices with their start and end apart: 14 -> 16, of which waited for: 4 -> 4; matrix products, arithmetic and copies ran while one was open for 0% -> 0% of each run, Pallas kernels for 38% -> 39%
where the time goes in v4:
time: 34.4 us; the launch traced here: 34.3 us
  starting transfers between devices  15.7 us (46%)
  Pallas kernels  14 us (41%)
  waiting for transfers between devices  3.68 us (11%)
  between operations  0.83 us (2%)
    ppermute x16, starting transfers between devices, swap(): return lax.ppermute(x, axis, [(i, i ^ shift) for i in range(count)])  15.7 us
    pallas_call x12, Pallas kernels, call(): pl.pallas_call(body, cost_estimate=pl.CostEstimate(flops=int(cost * FLOPS...  14 us
    ppermute x16, waiting for transfers between devices, swap(): return lax.ppermute(x, axis, [(i, i ^ shift) for i in range(count)])  3.68 us
  transfers between devices with their start and end apart: 16, of which 4 were waited for; matrix products, arithmetic and copies ran while one was open for 0% of the time, Pallas kernels for 39%

profile of v4, /device:TPU:0, one launch (start us, length us, event | category | flops | bytes accessed | tf_op | source)
XLA Modules:
  0.0 34.3 jit_solution(12485960283063095843)
XLA Ops:
  0.7 0.5 %collective-permute-start = (bf16[160,256]{1,0:T(8,128)(2,1)}, bf16[160,256]{1,0:T(8,128)(2,1)S(1)}, u32[]{:S(2)}, u32[]{:S(2)}) collective-permute-start(bf16[160,256]{1,0:T(8,128)(2,1)} %refs_0_.4), channel_id=1, source_target_pairs={{0,4},{4,0},{8,12},{12,8},{16,20},{20,16},{24,28},{28,24},{1,5},{5... | collective-permute-start | bytes 245768 | tf_op jit(solution)/shard_map/ppermute | solution.py:332
  1.2 0.1 collective-permute-start.1
  1.3 1.4 %shard_map.94 = (bf16[4,640,128]{2,1,0:T(8,128)(2,1)S(1)}, f32[16,128]{1,0:T(8,128)S(1)}) custom-call(bf16[160,2048]{1,0:T(8,128)(2,1)} %refs_0_.5, bf16[160,2048]{1,0:T(8,128)(2,1)} %refs_1_.3, s32[1280]{0:T(1024)} %refs_2_.3), custom_call_target="tpu_custom_call" | custom-call | flops 1100000000 | bytes 1315840 | tf_op jit(solution)/shard_map/pallas_call | solution.py:35
  2.7 0.0 collective-permute-done.1.refs_3_
  2.7 0.5 %collective-permute-start.2 = (bf16[4,640,128]{2,1,0:T(8,128)(2,1)S(1)}, bf16[4,640,128]{2,1,0:T(8,128)(2,1)S(1)}, u32[]{:S(2)}, u32[]{:S(2)}) collective-permute-start(bf16[4,640,128]{2,1,0:T(8,128)(2,1)S(1)} %get-tuple-element.33), channel_id=1, source_target_pairs={{0,4},{4,0},{8,12},{12,8},{16,20},{20,16},{24,28},{28,24},{1,5},{5... | collective-permute-start | bytes 1966088 | tf_op jit(solution)/shard_map/ppermute | solution.py:332
  3.2 2.6 %collective-permute-start.5 = (bf16[640,128]{1,0:T(8,128)(2,1)S(1)}, bf16[640,128]{1,0:T(8,128)(2,1)S(1)}, u32[]{:S(2)}, u32[]{:S(2)}) collective-permute-start(bf16[640,128]{1,0:T(8,128)(2,1)S(1)} %shard_map.95.refs_5_.refs_7_.refs_3_.refs_4_), channel_id=1, source_target_pairs={{0,16},{4,20},{8,24},{12,28},{16,0},{20,4},{24,8},{28,12},{1,17},{... | collective-permute-start | bytes 491528 | tf_op jit(solution)/shard_map/ppermute | solution.py:332
  5.9 1.5 %collective-permute-start.4 = (bf16[640,128]{1,0:T(8,128)(2,1)S(1)}, bf16[640,128]{1,0:T(8,128)(2,1)S(1)}, u32[]{:S(2)}, u32[]{:S(2)}) collective-permute-start(bf16[640,128]{1,0:T(8,128)(2,1)S(1)} %shard_map.95.refs_5_.refs_7_.refs_3_.refs_4_), channel_id=1, source_target_pairs={{0,8},{4,12},{8,0},{12,4},{16,24},{20,28},{24,16},{28,20},{1,9},{5... | collective-permute-start | bytes 491528 | tf_op jit(solution)/shard_map/ppermute | solution.py:332
  7.4 0.9 %shard_map.96 = (f32[8,640]{1,0:T(8,128)S(1)}, f32[8,640]{1,0:T(8,128)S(1)}, bf16[4,640,128]{2,1,0:T(8,128)(2,1)S(1)}, bf16[4,128,640]{2,1,0:T(8,128)(2,1)S(1)},...) custom-call(bf16[160,2048]{1,0:T(8,128)(2,1)S(1)} %copy-done.2, bf16[160,2048]{1,0:T(8,128)(2,1)S(1)} %copy-done.3, ...), custom_call_target="tpu_custom_call" | custom-call | flops 1100000000 | bytes 2795520 | tf_op jit(solution)/shard_map/pallas_call | solution.py:35
  8.3 0.1 collective-permute-start.3
  8.3 1.5 %collective-permute-start.6 = (bf16[640,128]{1,0:T(8,128)(2,1)S(1)}, bf16[640,128]{1,0:T(8,128)(2,1)S(1)}, u32[]{:S(2)}, u32[]{:S(2)}) collective-permute-start(bf16[640,128]{1,0:T(8,128)(2,1)S(1)} %get-tuple-element.39), channel_id=1, source_target_pairs={{0,24},{4,28},{8,16},{12,20},{16,8},{20,12},{24,0},{28,4},{1,25},{... | collective-permute-start | bytes 491528 | tf_op jit(solution)/shard_map/ppermute | solution.py:332
  9.9 0.8 %collective-permute-done.5.refs_7_.refs_5_.refs_6_ = bf16[640,128]{1,0:T(8,128)(2,1)S(1)} collective-permute-done((bf16[640,128]{1,0:T(8,128)(2,1)S(1)}, bf16[640,128]{1,0:T(8,128)(2,1)S(1)}, u32[]{:S(2)}, u32[]{:S(2)}) %collective-permute-start.5) | collective-permute-done | bytes 163872 | tf_op jit(solution)/shard_map/ppermute | solution.py:332
  10.7 0.0 collective-permute-done.3.refs_6_.refs_2_
  10.7 1.2 %shard_map.99.refs_8_ = bf16[640,128]{1,0:T(8,128)(2,1)S(1)} custom-call(f32[16,128]{1,0:T(8,128)S(1)} %get-tuple-element.31.refs_0_, bf16[4,640,128]{2,1,0:T(8,128)(2,1)S(1)} %get-tuple-element.36.refs_1_, bf16[4,640,128]{2,1,0:T(8,128)(2,1)S(1)} %collective-permute-done.2.refs_4_.refs_2_.refs_1_, bf16[4,128,640]{2,1,0:T(8,128)(2,1)S(1)} %get-tuple-element.40.refs_3_, ...), custom_call_target="tpu_custom_call" | custom-call | flops 550000000 | bytes 2834432 | tf_op jit(solution)/shard_map/pallas_call | solution.py:35
  11.9 1.0 %collective-permute-done.4.refs_7_.refs_4_.refs_5_ = bf16[640,128]{1,0:T(8,128)(2,1)S(1)} collective-permute-done((bf16[640,128]{1,0:T(8,128)(2,1)S(1)}, bf16[640,128]{1,0:T(8,128)(2,1)S(1)}, u32[]{:S(2)}, u32[]{:S(2)}) %collective-permute-start.4) | collective-permute-done | bytes 163872 | tf_op jit(solution)/shard_map/ppermute | solution.py:332
  12.9 1.2 %shard_map.100 = bf16[640,128]{1,0:T(8,128)(2,1)S(1)} custom-call(f32[16,128]{1,0:T(8,128)S(1)} %get-tuple-element.31.refs_0_, bf16[4,640,128]{2,1,0:T(8,128)(2,1)S(1)} %get-tuple-element.36.refs_1_, bf16[4,640,128]{2,1,0:T(8,128)(2,1)S(1)} %collective-permute-done.2.refs_4_.refs_2_.refs_1_, bf16[4,128,640]{2,1,0:T(8,128)(2,1)S(1)} %get-tuple-element.40.refs_3_, ...), custom_call_target="tpu_custom_call" | custom-call | flops 550000000 | bytes 2834432 | tf_op jit(solution)/shard_map/pallas_call | solution.py:35
  14.1 1.6 %collective-permute-start.7 = (bf16[640,128]{1,0:T(8,128)(2,1)S(1)}, bf16[640,128]{1,0:T(8,128)(2,1)S(1)}, u32[]{:S(2)}, u32[]{:S(2)}) collective-permute-start(bf16[640,128]{1,0:T(8,128)(2,1)S(1)} %shard_map.100), channel_id=1, source_target_pairs={{0,8},{4,12},{8,0},{12,4},{16,24},{20,28},{24,16},{28,20},{1,9},{5... | collective-permute-start | bytes 491528 | tf_op jit(solution)/shard_map/ppermute | solution.py:332
  15.7 0.8 %collective-permute-start.8 = (bf16[640,128]{1,0:T(8,128)(2,1)S(1)}, bf16[640,128]{1,0:T(8,128)(2,1)S(1)}, u32[]{:S(2)}, u32[]{:S(2)}) collective-permute-start(bf16[640,128]{1,0:T(8,128)(2,1)S(1)} %shard_map.99.refs_8_), channel_id=1, source_target_pairs={{0,16},{4,20},{8,24},{12,28},{16,0},{20,4},{24,8},{28,12},{1,17},{... | collective-permute-start | bytes 491528 | tf_op jit(solution)/shard_map/ppermute | solution.py:332
  16.4 1.2 %shard_map.97 = (bf16[320,128]{1,0:T(8,128)(2,1)S(1)}, bf16[320,128]{1,0:T(8,128)(2,1)S(1)}) custom-call(f32[16,128]{1,0:T(8,128)S(1)} %get-tuple-element.31.refs_0_, bf16[4,640,128]{2,1,0:T(8,128)(2,1)S(1)} %get-tuple-element.36.refs_1_, bf16[4,640,128]{2,1,0:T(8,128)(2,1)S(1)} %collective-permute-done.2.refs_4_.refs_2_.refs_1_, ...), custom_call_target="tpu_custom_call" | custom-call | flops 550000000 | bytes 2834432 | tf_op jit(solution)/shard_map/pallas_call | solution.py:35
  17.6 1.7 %collective-permute-start.9 = (bf16[320,128]{1,0:T(8,128)(2,1)S(1)}, bf16[320,128]{1,0:T(8,128)(2,1)S(1)}, u32[]{:S(2)}, u32[]{:S(2)}) collective-permute-start(bf16[320,128]{1,0:T(8,128)(2,1)S(1)} %get-tuple-element.42.refs_8_), channel_id=1, source_target_pairs={{0,24},{4,28},{8,16},{12,20},{16,8},{20,12},{24,0},{28,4},{1,25},{... | collective-permute-start | bytes 245768 | tf_op jit(solution)/shard_map/ppermute | solution.py:332
  19.3 1.4 %shard_map.98 = (f32[320,128]{1,0:T(8,128)S(1)}, f32[320,128]{1,0:T(8,128)S(1)}) custom-call(f32[16,128]{1,0:T(8,128)S(1)} %get-tuple-element.31.refs_0_, bf16[4,640,128]{2,1,0:T(8,128)(2,1)S(1)} %get-tuple-element.36.refs_1_, bf16[4,640,128]{2,1,0:T(8,128)(2,1)S(1)} %collective-permute-done.2.refs_4_.refs_2_.refs_1_, ...), custom_call_target="tpu_custom_call" | custom-call | flops 550000000 | bytes 2834432 | tf_op jit(solution)/shard_map/pallas_call | solution.py:35
  20.8 1.1 %collective-permute-done.8.refs_3_ = bf16[640,128]{1,0:T(8,128)(2,1)S(1)} collective-permute-done((bf16[640,128]{1,0:T(8,128)(2,1)S(1)}, bf16[640,128]{1,0:T(8,128)(2,1)S(1)}, u32[]{:S(2)}, u32[]{:S(2)}) %collective-permute-start.8) | collective-permute-done | bytes 163872 | tf_op jit(solution)/shard_map/ppermute | solution.py:332
  21.9 0.1 shard_map.101
  21.9 0.4 %collective-permute-start.10 = (f32[320,128]{1,0:T(8,128)S(1)}, f32[320,128]{1,0:T(8,128)S(1)}, u32[]{:S(2)}, u32[]{:S(2)}) collective-permute-start(f32[320,128]{1,0:T(8,128)S(1)} %get-tuple-element.46), channel_id=1, source_target_pairs={{0,4},{4,0},{8,12},{12,8},{16,20},{20,16},{24,28},{28,24},{1,5},{5... | collective-permute-start | bytes 491528 | tf_op jit(solution)/shard_map/ppermute | solution.py:332
  22.3 2.5 %shard_map.102 = bf16[2,640,128]{2,1,0:T(8,128)(2,1)S(1)} custom-call(f32[16,128]{1,0:T(8,128)S(1)} %get-tuple-element.31.refs_0_, bf16[4,640,128]{2,1,0:T(8,128)(2,1)S(1)} %collective-permute-done.2.refs_4_.refs_2_.refs_1_, f32[8,640]{1,0:T(8,128)S(1)} %collective-permute-done.3.refs_6_.refs_2_, ...), custom_call_target="tpu_custom_call" | custom-call | flops 2750000128 | bytes 1339392 | tf_op jit(solution)/shard_map/pallas_call | solution.py:35
  24.8 0.1 shard_map.103
  24.9 0.3 collective-permute-start.12
  25.2 2.6 %collective-permute-start.13 = (bf16[2,40,256]{2,1,0:T(8,128)(2,1)S(1)}, bf16[2,40,256]{2,1,0:T(8,128)(2,1)S(1)}, u32[]{:S(2)}, u32[]{:S(2)}) collective-permute-start(bf16[2,40,256]{2,1,0:T(8,128)(2,1)S(1)} %get-tuple-element.54), channel_id=1, source_target_pairs={{0,2},{1,3},{2,0},{3,1},{4,6},{5,7},{6,4},{7,5},{8,10},{9,11},{10,... | collective-permute-start | bytes 122888 | tf_op jit(solution)/shard_map/ppermute | solution.py:332
  27.8 1.3 %collective-permute-start.14 = (bf16[2,40,256]{2,1,0:T(8,128)(2,1)S(1)}, bf16[2,40,256]{2,1,0:T(8,128)(2,1)S(1)}, u32[]{:S(2)}, u32[]{:S(2)}) collective-permute-start(bf16[2,40,256]{2,1,0:T(8,128)(2,1)S(1)} %get-tuple-element.55), channel_id=1, source_target_pairs={{0,3},{1,2},{2,1},{3,0},{4,7},{5,6},{6,5},{7,4},{8,11},{9,10},{10,... | collective-permute-start | bytes 122888 | tf_op jit(solution)/shard_map/ppermute | solution.py:332
  29.1 0.2 collective-permute-start.15
  29.4 3.5 %shard_map.104.refs_4_ = bf16[160,2048]{1,0:T(8,128)(2,1)} custom-call(f32[16,128]{1,0:T(8,128)S(1)} %get-tuple-element.31.refs_0_, bf16[4,640,128]{2,1,0:T(8,128)(2,1)S(1)} %get-tuple-element.36.refs_1_, f32[8,640]{1,0:T(8,128)S(1)} %get-tuple-element.37.refs_5_.refs_2_, bf16[2,640,128]{2,1,0:T(8,128)(2,1)S(1)} %collective-permute-done.12.refs_3_, ...), custom_call_target="tpu_custom_call" | custom-call | flops 3300000000 | bytes 1667072 | tf_op jit(solution)/shard_map/pallas_call | solution.py:35
  32.9 0.7 %collective-permute-done.14.refs_2_ = bf16[2,40,256]{2,1,0:T(8,128)(2,1)S(1)} collective-permute-done((bf16[2,40,256]{2,1,0:T(8,128)(2,1)S(1)}, bf16[2,40,256]{2,1,0:T(8,128)(2,1)S(1)}, u32[]{:S(2)}, u32[]{:S(2)}) %collective-permute-start.14) | collective-permute-done | bytes 40992 | tf_op jit(solution)/shard_map/ppermute | solution.py:332
  33.6 0.7 %shard_map.105 = (bf16[40,1024]{1,0:T(8,128)(2,1)}, bf16[40,1024]{1,0:T(8,128)(2,1)}) custom-call(bf16[2,40,256]{2,1,0:T(8,128)(2,1)S(1)} %get-tuple-element.53.refs_8_.refs_0_, bf16[2,40,256]{2,1,0:T(8,128)(2,1)S(1)} %collective-permute-done.13.refs_1_, bf16[2,40,256]{2,1,0:T(8,128)(2,1)S(1)} %collective-permute-done.14.refs_2_, ...), custom_call_target="tpu_custom_call" | custom-call | flops 110000000 | bytes 163840 | tf_op jit(solution)/shard_map/pallas_call | solution.py:35
  (24 shorter events, 0.1 us)
Async XLA Ops:
  0.6 2.6 %copy-start = (bf16[160,256]{1,0:T(8,128)(2,1)S(1)}, bf16[160,256]{1,0:T(8,128)(2,1)}, u32[]{:S(2)}) copy-start(bf16[160,256]{1,0:T(8,128)(2,1)} %refs_0_.4) | copy-start | bytes 245764
  0.6 2.6 %copy-start.1 = (bf16[160,256]{1,0:T(8,128)(2,1)S(1)}, bf16[160,256]{1,0:T(8,128)(2,1)}, u32[]{:S(2)}) copy-start(bf16[160,256]{1,0:T(8,128)(2,1)} %refs_2_.4) | copy-start | bytes 245764
  0.7 6.7 %copy-start.2 = (bf16[160,2048]{1,0:T(8,128)(2,1)S(1)}, bf16[160,2048]{1,0:T(8,128)(2,1)}, u32[]{:S(2)}) copy-start(bf16[160,2048]{1,0:T(8,128)(2,1)} %refs_0_.5) | copy-start | bytes 1966084
  0.7 6.7 %copy-start.3 = (bf16[160,2048]{1,0:T(8,128)(2,1)S(1)}, bf16[160,2048]{1,0:T(8,128)(2,1)}, u32[]{:S(2)}) copy-start(bf16[160,2048]{1,0:T(8,128)(2,1)} %refs_1_.3) | copy-start | bytes 1966084
  0.7 6.7 %copy-start.4 = (bf16[160,2048]{1,0:T(8,128)(2,1)S(1)}, bf16[160,2048]{1,0:T(8,128)(2,1)}, u32[]{:S(2)}) copy-start(bf16[160,2048]{1,0:T(8,128)(2,1)} %refs_2_.5) | copy-start | bytes 1966084
  0.7 2.0 %collective-permute-start = (bf16[160,256]{1,0:T(8,128)(2,1)}, bf16[160,256]{1,0:T(8,128)(2,1)S(1)}, u32[]{:S(2)}, u32[]{:S(2)}) collective-permute-start(bf16[160,256]{1,0:T(8,128)(2,1)} %refs_0_.4), channel_id=1, source_target_pairs={{0,4},{4,0},{8,12},{12,8},{16,20},{20,16},{24,28},{28,24},{1,5},{5... | collective-permute-start | bytes 245768 | tf_op jit(solution)/shard_map/ppermute | solution.py:332
  1.2 1.5 %collective-permute-start.1 = (bf16[160,256]{1,0:T(8,128)(2,1)}, bf16[160,256]{1,0:T(8,128)(2,1)S(1)}, u32[]{:S(2)}, u32[]{:S(2)}) collective-permute-start(bf16[160,256]{1,0:T(8,128)(2,1)} %refs_2_.4), channel_id=1, source_target_pairs={{0,4},{4,0},{8,12},{12,8},{16,20},{20,16},{24,28},{28,24},{1,5},{5... | collective-permute-start | bytes 245768 | tf_op jit(solution)/shard_map/ppermute | solution.py:332
  2.7 4.7 %copy-start.5 = (f32[160,16]{0,1:T(8,128)S(1)}, f32[160,16]{0,1:T(8,128)}, u32[]{:S(2)}) copy-start(f32[160,16]{0,1:T(8,128)} %param.13) | copy-start | bytes 30724
  2.7 4.7 %collective-permute-start.2 = (bf16[4,640,128]{2,1,0:T(8,128)(2,1)S(1)}, bf16[4,640,128]{2,1,0:T(8,128)(2,1)S(1)}, u32[]{:S(2)}, u32[]{:S(2)}) collective-permute-start(bf16[4,640,128]{2,1,0:T(8,128)(2,1)S(1)} %get-tuple-element.33), channel_id=1, source_target_pairs={{0,4},{4,0},{8,12},{12,8},{16,20},{20,16},{24,28},{28,24},{1,5},{5... | collective-permute-start | bytes 1966088 | tf_op jit(solution)/shard_map/ppermute | solution.py:332
  3.2 7.5 %collective-permute-start.5 = (bf16[640,128]{1,0:T(8,128)(2,1)S(1)}, bf16[640,128]{1,0:T(8,128)(2,1)S(1)}, u32[]{:S(2)}, u32[]{:S(2)}) collective-permute-start(bf16[640,128]{1,0:T(8,128)(2,1)S(1)} %shard_map.95.refs_5_.refs_7_.refs_3_.refs_4_), channel_id=1, source_target_pairs={{0,16},{4,20},{8,24},{12,28},{16,0},{20,4},{24,8},{28,12},{1,17},{... | collective-permute-start | bytes 491528 | tf_op jit(solution)/shard_map/ppermute | solution.py:332
  5.9 7.0 %collective-permute-start.4 = (bf16[640,128]{1,0:T(8,128)(2,1)S(1)}, bf16[640,128]{1,0:T(8,128)(2,1)S(1)}, u32[]{:S(2)}, u32[]{:S(2)}) collective-permute-start(bf16[640,128]{1,0:T(8,128)(2,1)S(1)} %shard_map.95.refs_5_.refs_7_.refs_3_.refs_4_), channel_id=1, source_target_pairs={{0,8},{4,12},{8,0},{12,4},{16,24},{20,28},{24,16},{28,20},{1,9},{5... | collective-permute-start | bytes 491528 | tf_op jit(solution)/shard_map/ppermute | solution.py:332
  8.3 2.4 %collective-permute-start.3 = (f32[8,640]{1,0:T(8,128)S(1)}, f32[8,640]{1,0:T(8,128)S(1)}, u32[]{:S(2)}, u32[]{:S(2)}) collective-permute-start(f32[8,640]{1,0:T(8,128)S(1)} %get-tuple-element.38), channel_id=1, source_target_pairs={{0,4},{4,0},{8,12},{12,8},{16,20},{20,16},{24,28},{28,24},{1,5},{5... | collective-permute-start | bytes 61448 | tf_op jit(solution)/shard_map/ppermute | solution.py:332
  8.3 8.1 %collective-permute-start.6 = (bf16[640,128]{1,0:T(8,128)(2,1)S(1)}, bf16[640,128]{1,0:T(8,128)(2,1)S(1)}, u32[]{:S(2)}, u32[]{:S(2)}) collective-permute-start(bf16[640,128]{1,0:T(8,128)(2,1)S(1)} %get-tuple-element.39), channel_id=1, source_target_pairs={{0,24},{4,28},{8,16},{12,20},{16,8},{20,12},{24,0},{28,4},{1,25},{... | collective-permute-start | bytes 491528 | tf_op jit(solution)/shard_map/ppermute | solution.py:332
  14.1 6.7 %collective-permute-start.7 = (bf16[640,128]{1,0:T(8,128)(2,1)S(1)}, bf16[640,128]{1,0:T(8,128)(2,1)S(1)}, u32[]{:S(2)}, u32[]{:S(2)}) collective-permute-start(bf16[640,128]{1,0:T(8,128)(2,1)S(1)} %shard_map.100), channel_id=1, source_target_pairs={{0,8},{4,12},{8,0},{12,4},{16,24},{20,28},{24,16},{28,20},{1,9},{5... | collective-permute-start | bytes 491528 | tf_op jit(solution)/shard_map/ppermute | solution.py:332
  15.7 6.2 %collective-permute-start.8 = (bf16[640,128]{1,0:T(8,128)(2,1)S(1)}, bf16[640,128]{1,0:T(8,128)(2,1)S(1)}, u32[]{:S(2)}, u32[]{:S(2)}) collective-permute-start(bf16[640,128]{1,0:T(8,128)(2,1)S(1)} %shard_map.99.refs_8_), channel_id=1, source_target_pairs={{0,16},{4,20},{8,24},{12,28},{16,0},{20,4},{24,8},{28,12},{1,17},{... | collective-permute-start | bytes 491528 | tf_op jit(solution)/shard_map/ppermute | solution.py:332
  17.6 7.2 %collective-permute-start.9 = (bf16[320,128]{1,0:T(8,128)(2,1)S(1)}, bf16[320,128]{1,0:T(8,128)(2,1)S(1)}, u32[]{:S(2)}, u32[]{:S(2)}) collective-permute-start(bf16[320,128]{1,0:T(8,128)(2,1)S(1)} %get-tuple-element.42.refs_8_), channel_id=1, source_target_pairs={{0,24},{4,28},{8,16},{12,20},{16,8},{20,12},{24,0},{28,4},{1,25},{... | collective-permute-start | bytes 245768 | tf_op jit(solution)/shard_map/ppermute | solution.py:332
  19.3 5.5 %collective-permute-start.11 = (bf16[320,128]{1,0:T(8,128)(2,1)S(1)}, bf16[320,128]{1,0:T(8,128)(2,1)S(1)}, u32[]{:S(2)}, u32[]{:S(2)}) collective-permute-start(bf16[320,128]{1,0:T(8,128)(2,1)S(1)} %get-tuple-element.47), channel_id=1, source_target_pairs={{0,28},{4,24},{8,20},{12,16},{16,12},{20,8},{24,4},{28,0},{1,29},{... | collective-permute-start | bytes 245768 | tf_op jit(solution)/shard_map/ppermute | solution.py:332
  21.9 2.9 %collective-permute-start.10 = (f32[320,128]{1,0:T(8,128)S(1)}, f32[320,128]{1,0:T(8,128)S(1)}, u32[]{:S(2)}, u32[]{:S(2)}) collective-permute-start(f32[320,128]{1,0:T(8,128)S(1)} %get-tuple-element.46), channel_id=1, source_target_pairs={{0,4},{4,0},{8,12},{12,8},{16,20},{20,16},{24,28},{28,24},{1,5},{5... | collective-permute-start | bytes 491528 | tf_op jit(solution)/shard_map/ppermute | solution.py:332
  24.9 4.5 %collective-permute-start.12 = (bf16[2,640,128]{2,1,0:T(8,128)(2,1)S(1)}, bf16[2,640,128]{2,1,0:T(8,128)(2,1)S(1)}, u32[]{:S(2)}, u32[]{:S(2)}) collective-permute-start(bf16[2,640,128]{2,1,0:T(8,128)(2,1)S(1)} %shard_map.102), channel_id=1, source_target_pairs={{0,4},{4,0},{8,12},{12,8},{16,20},{20,16},{24,28},{28,24},{1,5},{5... | collective-permute-start | bytes 983048 | tf_op jit(solution)/shard_map/ppermute | solution.py:332
  25.2 7.7 %collective-permute-start.13 = (bf16[2,40,256]{2,1,0:T(8,128)(2,1)S(1)}, bf16[2,40,256]{2,1,0:T(8,128)(2,1)S(1)}, u32[]{:S(2)}, u32[]{:S(2)}) collective-permute-start(bf16[2,40,256]{2,1,0:T(8,128)(2,1)S(1)} %get-tuple-element.54), channel_id=1, source_target_pairs={{0,2},{1,3},{2,0},{3,1},{4,6},{5,7},{6,4},{7,5},{8,10},{9,11},{10,... | collective-permute-start | bytes 122888 | tf_op jit(solution)/shard_map/ppermute | solution.py:332
  27.8 5.8 %collective-permute-start.14 = (bf16[2,40,256]{2,1,0:T(8,128)(2,1)S(1)}, bf16[2,40,256]{2,1,0:T(8,128)(2,1)S(1)}, u32[]{:S(2)}, u32[]{:S(2)}) collective-permute-start(bf16[2,40,256]{2,1,0:T(8,128)(2,1)S(1)} %get-tuple-element.55), channel_id=1, source_target_pairs={{0,3},{1,2},{2,1},{3,0},{4,7},{5,6},{6,5},{7,4},{8,11},{9,10},{10,... | collective-permute-start | bytes 122888 | tf_op jit(solution)/shard_map/ppermute | solution.py:332
  29.1 4.5 %collective-permute-start.15 = (bf16[2,40,256]{2,1,0:T(8,128)(2,1)S(1)}, bf16[2,40,256]{2,1,0:T(8,128)(2,1)S(1)}, u32[]{:S(2)}, u32[]{:S(2)}) collective-permute-start(bf16[2,40,256]{2,1,0:T(8,128)(2,1)S(1)} %get-tuple-element.56), channel_id=1, source_target_pairs={{0,1},{1,0},{2,3},{3,2},{4,5},{5,4},{6,7},{7,6},{8,9},{9,8},{10,11... | collective-permute-start | bytes 122888 | tf_op jit(solution)/shard_map/ppermute | solution.py:332

commit v5 on v4

--- a/solution.py
+++ b/solution.py
@@ -72,19 +72,10 @@
     return pos_ref[jnp.bitwise_xor(ctx, shift) * tokens]
 
 
-def pack_q_kernel(heads, q_hbm, g_hbm, pos_hbm, out, larger, pos, sems):
-    tokens = q_hbm.shape[0]
-    half = tokens // 2
-    group = 1 - parity()
-    pairs = [(pos_hbm, pos)] + [
-        (
-            src.at[pl.ds(w * half, half), columns_of(group * heads + h)],
-            out.at[2 * kind + w, pl.ds(h * half, half), :],
-        )
-        for kind, src in enumerate((q_hbm, g_hbm))
-        for w in range(2)
-        for h in range(heads)
-    ]
+def pack_q_kernel(q_hbm, g_hbm, pos_hbm, out, larger, pos, sems):
+    tokens, width = q_hbm.shape[0], out.shape[2]
+    cols = pl.ds(pl.multiple_of((1 - parity()) * width, width), width)
+    pairs = [(pos_hbm, pos), (q_hbm.at[:, cols], out.at[0]), (g_hbm.at[:, cols], out.at[1])]
     copy_all(pairs, sems)
     for m in range(larger.shape[0] // 2):
         for b in range(2):
@@ -101,8 +92,8 @@
     return parts
 
 
-def rows_kernel(heads, q_ref, g_ref, o_ref, log, sib, kv, *refs):
-    own_rows, other_rows, own, own_t, sib_t, kv_out = refs
+def rows_kernel(heads, q_ref, g_ref, o_ref, log, raw, kv, *refs):
+    own_rows, other_rows, own, own_t, sib, sib_t, kv_out = refs
     lanes = own.shape[1]
     half = lanes // heads
     c = parity()
@@ -137,8 +128,13 @@
     spot = lax.rem(lax.broadcasted_iota(jnp.int32, (4, lanes), 1), half).astype(F32)
     own_rows[4:8, :] = spot
     other_rows[4:8, :] = spot
-    for i in range(4):
-        sib_t[i] = sib[i].T
+    for kind in range(2):
+        for w in range(2):
+            r = slice(w * half, (w + 1) * half)
+            cols = [slice(h * HEAD_SIZE, (h + 1) * HEAD_SIZE) for h in range(heads)]
+            x = jnp.concatenate([raw[kind, r, col] for col in cols], axis=0)
+            sib[2 * kind + w] = x
+            sib_t[2 * kind + w] = x.T
     kv_out[...] = kv[...]
 
 
@@ -344,23 +340,23 @@
     piece = ((4 * tokens, HEAD_SIZE), BF16)
     stack = ((4, lanes, HEAD_SIZE), BF16)
     other, larger = call(
-        functools.partial(pack_q_kernel, heads),
-        [stack, ((2 * n, HEAD_SIZE), F32)],
+        pack_q_kernel,
+        [((2, tokens, heads * HEAD_SIZE), BF16), ((2 * n, HEAD_SIZE), F32)],
         [],
-        [pltpu.SMEM(positions.shape, jnp.int32), pltpu.SemaphoreType.DMA((4 * heads + 1,))],
+        [pltpu.SMEM(positions.shape, jnp.int32), pltpu.SemaphoreType.DMA((3,))],
         cost=1.0,
         far=[queries, output_grad, positions],
     )
     pair_keys, pair_values = swap(keys, "ctx", 1), swap(values, "ctx", 1)
     other, pair_keys, pair_values = lax.optimization_barrier((other, pair_keys, pair_values))
     (kv_chip,) = call(merge_kv_kernel, [piece], [keys, pair_keys, values, pair_values])
-    sib = swap(other, "ctx", 1)
+    raw = swap(other, "ctx", 1)
     turned = ((4, HEAD_SIZE, lanes), BF16)
     vectors = ((8, lanes), F32)
-    own_rows, other_rows, own, own_t, sib_t, kv_late = call(
+    own_rows, other_rows, own, own_t, sib, sib_t, kv_late = call(
         functools.partial(rows_kernel, heads),
-        [vectors, vectors, stack, turned, turned, piece],
-        [queries, output_grad, attn_output, log_sums.T, sib, kv_chip],
+        [vectors, vectors, stack, turned, stack, turned, piece],
+        [queries, output_grad, attn_output, log_sums.T, raw, kv_chip],
         cost=1.0,
     )
     sib_rows = swap(other_rows, "ctx", 1)

time: 34.4 us -> 34.1 us (level)
  waiting for transfers between devices: 3.68 us -> 3.24 us
    ppermute x16, waiting for transfers between devices: 3.68 us -> 3.24 us  [swap(): return lax.ppermute(x, axis, [(i, i ^ shift) for i in range(count)])]
  transfers between devices with their start and end apart: 16 -> 16, of which waited for: 4 -> 5; matrix products, arithmetic and copies ran while one was open for 0% -> 0% of each run, Pallas kernels for 39% -> 39%
where the time goes in v5:
time: 34.1 us; the launch traced here: 34 us
  starting transfers between devices  15.9 us (47%)
  Pallas kernels  13.9 us (41%)
  waiting for transfers between devices  3.24 us (10%)
  between operations  0.83 us (2%)
    ppermute x16, starting transfers between devices, swap(): return lax.ppermute(x, axis, [(i, i ^ shift) for i in range(count)])  15.9 us
    pallas_call x12, Pallas kernels, call(): pl.pallas_call(body, cost_estimate=pl.CostEstimate(flops=int(cost * FLOPS...  13.9 us
    ppermute x16, waiting for transfers between devices, swap(): return lax.ppermute(x, axis, [(i, i ^ shift) for i in range(count)])  3.24 us
  transfers between devices with their start and end apart: 16, of which 5 were waited for; matrix products, arithmetic and copies ran while one was open for 0% of the time, Pallas kernels for 39%

profile of v5, /device:TPU:0, one launch (start us, length us, event | category | flops | bytes accessed | tf_op | source)
XLA Modules:
  0.0 34.0 jit_solution(182183672344693711)
XLA Ops:
  0.7 0.5 %collective-permute-start = (bf16[160,256]{1,0:T(8,128)(2,1)}, bf16[160,256]{1,0:T(8,128)(2,1)S(1)}, u32[]{:S(2)}, u32[]{:S(2)}) collective-permute-start(bf16[160,256]{1,0:T(8,128)(2,1)} %refs_0_.4), channel_id=1, source_target_pairs={{0,4},{4,0},{8,12},{12,8},{16,20},{20,16},{24,28},{28,24},{1,5},{5... | collective-permute-start | bytes 245768 | tf_op jit(solution)/shard_map/ppermute | solution.py:328
  1.2 0.1 collective-permute-start.1
  1.3 1.1 %shard_map.94 = (bf16[2,160,1024]{2,1,0:T(8,128)(2,1)S(1)}, f32[16,128]{1,0:T(8,128)S(1)}) custom-call(bf16[160,2048]{1,0:T(8,128)(2,1)} %refs_0_.5, bf16[160,2048]{1,0:T(8,128)(2,1)} %refs_1_.3, s32[1280]{0:T(1024)} %refs_2_.3), custom_call_target="tpu_custom_call" | custom-call | flops 1100000000 | bytes 1315840 | tf_op jit(solution)/shard_map/pallas_call | solution.py:35
  2.4 0.0 collective-permute-done.refs_1_
  2.4 0.2 collective-permute-done.1.refs_3_
  2.7 0.3 collective-permute-start.2
  3.0 2.8 %collective-permute-start.5 = (bf16[640,128]{1,0:T(8,128)(2,1)S(1)}, bf16[640,128]{1,0:T(8,128)(2,1)S(1)}, u32[]{:S(2)}, u32[]{:S(2)}) collective-permute-start(bf16[640,128]{1,0:T(8,128)(2,1)S(1)} %shard_map.95.refs_5_.refs_7_.refs_3_.refs_4_), channel_id=1, source_target_pairs={{0,16},{4,20},{8,24},{12,28},{16,0},{20,4},{24,8},{28,12},{1,17},{... | collective-permute-start | bytes 491528 | tf_op jit(solution)/shard_map/ppermute | solution.py:328
  5.8 1.5 %collective-permute-start.4 = (bf16[640,128]{1,0:T(8,128)(2,1)S(1)}, bf16[640,128]{1,0:T(8,128)(2,1)S(1)}, u32[]{:S(2)}, u32[]{:S(2)}) collective-permute-start(bf16[640,128]{1,0:T(8,128)(2,1)S(1)} %shard_map.95.refs_5_.refs_7_.refs_3_.refs_4_), channel_id=1, source_target_pairs={{0,8},{4,12},{8,0},{12,4},{16,24},{20,28},{24,16},{28,20},{1,9},{5... | collective-permute-start | bytes 491528 | tf_op jit(solution)/shard_map/ppermute | solution.py:328
  7.3 0.9 %shard_map.96 = (f32[8,640]{1,0:T(8,128)S(1)}, f32[8,640]{1,0:T(8,128)S(1)}, bf16[4,640,128]{2,1,0:T(8,128)(2,1)S(1)}, bf16[4,128,640]{2,1,0:T(8,128)(2,1)S(1)},...) custom-call(bf16[160,2048]{1,0:T(8,128)(2,1)S(1)} %copy-done.2, ...), custom_call_target="tpu_custom_call" | custom-call | flops 1100000000 | bytes 2795520 | tf_op jit(solution)/shard_map/pallas_call | solution.py:35
  8.3 0.1 collective-permute-start.3
  8.4 1.4 %collective-permute-start.6 = (bf16[640,128]{1,0:T(8,128)(2,1)S(1)}, bf16[640,128]{1,0:T(8,128)(2,1)S(1)}, u32[]{:S(2)}, u32[]{:S(2)}) collective-permute-start(bf16[640,128]{1,0:T(8,128)(2,1)S(1)} %get-tuple-element.41), channel_id=1, source_target_pairs={{0,24},{4,28},{8,16},{12,20},{16,8},{20,12},{24,0},{28,4},{1,25},{... | collective-permute-start | bytes 491528 | tf_op jit(solution)/shard_map/ppermute | solution.py:328
  9.8 0.7 %collective-permute-done.5.refs_7_.refs_5_.refs_6_ = bf16[640,128]{1,0:T(8,128)(2,1)S(1)} collective-permute-done((bf16[640,128]{1,0:T(8,128)(2,1)S(1)}, bf16[640,128]{1,0:T(8,128)(2,1)S(1)}, u32[]{:S(2)}, u32[]{:S(2)}) %collective-permute-start.5) | collective-permute-done | bytes 163872 | tf_op jit(solution)/shard_map/ppermute | solution.py:328
  10.5 1.2 %shard_map.99.refs_8_ = bf16[640,128]{1,0:T(8,128)(2,1)S(1)} custom-call(f32[16,128]{1,0:T(8,128)S(1)} %get-tuple-element.32.refs_0_, bf16[4,640,128]{2,1,0:T(8,128)(2,1)S(1)} %get-tuple-element.37.refs_1_, bf16[4,640,128]{2,1,0:T(8,128)(2,1)S(1)} %get-tuple-element.39.refs_2_.refs_1_, bf16[4,128,640]{2,1,0:T(8,128)(2,1)S(1)} %get-tuple-element.42.refs_3_, ...), custom_call_target="tpu_custom_call" | custom-call | flops 550000000 | bytes 2834432 | tf_op jit(solution)/shard_map/pallas_call | solution.py:35
  11.7 0.7 %collective-permute-done.4.refs_7_.refs_4_.refs_5_ = bf16[640,128]{1,0:T(8,128)(2,1)S(1)} collective-permute-done((bf16[640,128]{1,0:T(8,128)(2,1)S(1)}, bf16[640,128]{1,0:T(8,128)(2,1)S(1)}, u32[]{:S(2)}, u32[]{:S(2)}) %collective-permute-start.4) | collective-permute-done | bytes 163872 | tf_op jit(solution)/shard_map/ppermute | solution.py:328
  12.4 1.2 %shard_map.100 = bf16[640,128]{1,0:T(8,128)(2,1)S(1)} custom-call(f32[16,128]{1,0:T(8,128)S(1)} %get-tuple-element.32.refs_0_, bf16[4,640,128]{2,1,0:T(8,128)(2,1)S(1)} %get-tuple-element.37.refs_1_, bf16[4,640,128]{2,1,0:T(8,128)(2,1)S(1)} %get-tuple-element.39.refs_2_.refs_1_, bf16[4,128,640]{2,1,0:T(8,128)(2,1)S(1)} %get-tuple-element.42.refs_3_, ...), custom_call_target="tpu_custom_call" | custom-call | flops 550000000 | bytes 2834432 | tf_op jit(solution)/shard_map/pallas_call | solution.py:35
  13.6 1.8 %collective-permute-start.7 = (bf16[640,128]{1,0:T(8,128)(2,1)S(1)}, bf16[640,128]{1,0:T(8,128)(2,1)S(1)}, u32[]{:S(2)}, u32[]{:S(2)}) collective-permute-start(bf16[640,128]{1,0:T(8,128)(2,1)S(1)} %shard_map.100), channel_id=1, source_target_pairs={{0,8},{4,12},{8,0},{12,4},{16,24},{20,28},{24,16},{28,20},{1,9},{5... | collective-permute-start | bytes 491528 | tf_op jit(solution)/shard_map/ppermute | solution.py:328
  15.4 0.8 %collective-permute-start.8 = (bf16[640,128]{1,0:T(8,128)(2,1)S(1)}, bf16[640,128]{1,0:T(8,128)(2,1)S(1)}, u32[]{:S(2)}, u32[]{:S(2)}) collective-permute-start(bf16[640,128]{1,0:T(8,128)(2,1)S(1)} %shard_map.99.refs_8_), channel_id=1, source_target_pairs={{0,16},{4,20},{8,24},{12,28},{16,0},{20,4},{24,8},{28,12},{1,17},{... | collective-permute-start | bytes 491528 | tf_op jit(solution)/shard_map/ppermute | solution.py:328
  16.1 1.2 %shard_map.97 = (bf16[320,128]{1,0:T(8,128)(2,1)S(1)}, bf16[320,128]{1,0:T(8,128)(2,1)S(1)}) custom-call(f32[16,128]{1,0:T(8,128)S(1)} %get-tuple-element.32.refs_0_, bf16[4,640,128]{2,1,0:T(8,128)(2,1)S(1)} %get-tuple-element.37.refs_1_, bf16[4,640,128]{2,1,0:T(8,128)(2,1)S(1)} %get-tuple-element.39.refs_2_.refs_1_, ...), custom_call_target="tpu_custom_call" | custom-call | flops 550000000 | bytes 2834432 | tf_op jit(solution)/shard_map/pallas_call | solution.py:35
  17.3 1.9 %collective-permute-start.9 = (bf16[320,128]{1,0:T(8,128)(2,1)S(1)}, bf16[320,128]{1,0:T(8,128)(2,1)S(1)}, u32[]{:S(2)}, u32[]{:S(2)}) collective-permute-start(bf16[320,128]{1,0:T(8,128)(2,1)S(1)} %get-tuple-element.44.refs_8_), channel_id=1, source_target_pairs={{0,24},{4,28},{8,16},{12,20},{16,8},{20,12},{24,0},{28,4},{1,25},{... | collective-permute-start | bytes 245768 | tf_op jit(solution)/shard_map/ppermute | solution.py:328
  19.2 1.4 %shard_map.98 = (f32[320,128]{1,0:T(8,128)S(1)}, f32[320,128]{1,0:T(8,128)S(1)}) custom-call(f32[16,128]{1,0:T(8,128)S(1)} %get-tuple-element.32.refs_0_, bf16[4,640,128]{2,1,0:T(8,128)(2,1)S(1)} %get-tuple-element.37.refs_1_, bf16[4,640,128]{2,1,0:T(8,128)(2,1)S(1)} %get-tuple-element.39.refs_2_.refs_1_, ...), custom_call_target="tpu_custom_call" | custom-call | flops 550000000 | bytes 2834432 | tf_op jit(solution)/shard_map/pallas_call | solution.py:35
  20.7 0.9 %collective-permute-done.8.refs_3_ = bf16[640,128]{1,0:T(8,128)(2,1)S(1)} collective-permute-done((bf16[640,128]{1,0:T(8,128)(2,1)S(1)}, bf16[640,128]{1,0:T(8,128)(2,1)S(1)}, u32[]{:S(2)}, u32[]{:S(2)}) %collective-permute-start.8) | collective-permute-done | bytes 163872 | tf_op jit(solution)/shard_map/ppermute | solution.py:328
  21.6 0.1 shard_map.101
  21.6 0.4 %collective-permute-start.10 = (f32[320,128]{1,0:T(8,128)S(1)}, f32[320,128]{1,0:T(8,128)S(1)}, u32[]{:S(2)}, u32[]{:S(2)}) collective-permute-start(f32[320,128]{1,0:T(8,128)S(1)} %get-tuple-element.48), channel_id=1, source_target_pairs={{0,4},{4,0},{8,12},{12,8},{16,20},{20,16},{24,28},{28,24},{1,5},{5... | collective-permute-start | bytes 491528 | tf_op jit(solution)/shard_map/ppermute | solution.py:328
  22.0 2.5 %shard_map.102 = bf16[2,640,128]{2,1,0:T(8,128)(2,1)S(1)} custom-call(f32[16,128]{1,0:T(8,128)S(1)} %get-tuple-element.32.refs_0_, bf16[4,640,128]{2,1,0:T(8,128)(2,1)S(1)} %get-tuple-element.39.refs_2_.refs_1_, f32[8,640]{1,0:T(8,128)S(1)} %collective-permute-done.3.refs_6_.refs_2_, bf16[640,128]{1,0:T(8,128)(2,1)S(1)} %shard_map.95.refs_5_.refs_7_.refs_3_.refs_4_, ...), custom_call_target="tpu_custom_call" | custom-call | flops 2750000128 | bytes 1339392 | tf_op jit(solution)/shard_map/pallas_call | solution.py:35
  24.6 0.1 shard_map.103
  24.7 0.2 collective-permute-start.12
  24.9 2.6 %collective-permute-start.13 = (bf16[2,40,256]{2,1,0:T(8,128)(2,1)S(1)}, bf16[2,40,256]{2,1,0:T(8,128)(2,1)S(1)}, u32[]{:S(2)}, u32[]{:S(2)}) collective-permute-start(bf16[2,40,256]{2,1,0:T(8,128)(2,1)S(1)} %get-tuple-element.56), channel_id=1, source_target_pairs={{0,2},{1,3},{2,0},{3,1},{4,6},{5,7},{6,4},{7,5},{8,10},{9,11},{10,... | collective-permute-start | bytes 122888 | tf_op jit(solution)/shard_map/ppermute | solution.py:328
  27.5 1.3 %collective-permute-start.14 = (bf16[2,40,256]{2,1,0:T(8,128)(2,1)S(1)}, bf16[2,40,256]{2,1,0:T(8,128)(2,1)S(1)}, u32[]{:S(2)}, u32[]{:S(2)}) collective-permute-start(bf16[2,40,256]{2,1,0:T(8,128)(2,1)S(1)} %get-tuple-element.57), channel_id=1, source_target_pairs={{0,3},{1,2},{2,1},{3,0},{4,7},{5,6},{6,5},{7,4},{8,11},{9,10},{10,... | collective-permute-start | bytes 122888 | tf_op jit(solution)/shard_map/ppermute | solution.py:328
  28.8 0.2 collective-permute-start.15
  29.1 3.5 %shard_map.104.refs_4_ = bf16[160,2048]{1,0:T(8,128)(2,1)} custom-call(f32[16,128]{1,0:T(8,128)S(1)} %get-tuple-element.32.refs_0_, bf16[4,640,128]{2,1,0:T(8,128)(2,1)S(1)} %get-tuple-element.37.refs_1_, f32[8,640]{1,0:T(8,128)S(1)} %get-tuple-element.38.refs_5_.refs_2_, bf16[2,640,128]{2,1,0:T(8,128)(2,1)S(1)} %collective-permute-done.12.refs_3_, ...), custom_call_target="tpu_custom_call" | custom-call | flops 3300000000 | bytes 1667072 | tf_op jit(solution)/shard_map/pallas_call | solution.py:35
  32.6 0.7 %collective-permute-done.14.refs_2_ = bf16[2,40,256]{2,1,0:T(8,128)(2,1)S(1)} collective-permute-done((bf16[2,40,256]{2,1,0:T(8,128)(2,1)S(1)}, bf16[2,40,256]{2,1,0:T(8,128)(2,1)S(1)}, u32[]{:S(2)}, u32[]{:S(2)}) %collective-permute-start.14) | collective-permute-done | bytes 40992 | tf_op jit(solution)/shard_map/ppermute | solution.py:328
  33.3 0.7 %shard_map.105 = (bf16[40,1024]{1,0:T(8,128)(2,1)}, bf16[40,1024]{1,0:T(8,128)(2,1)}) custom-call(bf16[2,40,256]{2,1,0:T(8,128)(2,1)S(1)} %get-tuple-element.55.refs_8_.refs_0_, bf16[2,40,256]{2,1,0:T(8,128)(2,1)S(1)} %collective-permute-done.13.refs_1_, bf16[2,40,256]{2,1,0:T(8,128)(2,1)S(1)} %collective-permute-done.14.refs_2_, ...), custom_call_target="tpu_custom_call" | custom-call | flops 110000000 | bytes 163840 | tf_op jit(solution)/shard_map/pallas_call | solution.py:35
  (24 shorter events, 0.1 us)
Async XLA Ops:
  0.6 2.3 %copy-start = (bf16[160,256]{1,0:T(8,128)(2,1)S(1)}, bf16[160,256]{1,0:T(8,128)(2,1)}, u32[]{:S(2)}) copy-start(bf16[160,256]{1,0:T(8,128)(2,1)} %refs_0_.4) | copy-start | bytes 245764
  0.6 2.3 %copy-start.1 = (bf16[160,256]{1,0:T(8,128)(2,1)S(1)}, bf16[160,256]{1,0:T(8,128)(2,1)}, u32[]{:S(2)}) copy-start(bf16[160,256]{1,0:T(8,128)(2,1)} %refs_2_.4) | copy-start | bytes 245764
  0.7 6.7 %copy-start.2 = (bf16[160,2048]{1,0:T(8,128)(2,1)S(1)}, bf16[160,2048]{1,0:T(8,128)(2,1)}, u32[]{:S(2)}) copy-start(bf16[160,2048]{1,0:T(8,128)(2,1)} %refs_0_.5) | copy-start | bytes 1966084
  0.7 6.7 %copy-start.3 = (bf16[160,2048]{1,0:T(8,128)(2,1)S(1)}, bf16[160,2048]{1,0:T(8,128)(2,1)}, u32[]{:S(2)}) copy-start(bf16[160,2048]{1,0:T(8,128)(2,1)} %refs_1_.3) | copy-start | bytes 1966084
  0.7 6.7 %copy-start.4 = (bf16[160,2048]{1,0:T(8,128)(2,1)S(1)}, bf16[160,2048]{1,0:T(8,128)(2,1)}, u32[]{:S(2)}) copy-start(bf16[160,2048]{1,0:T(8,128)(2,1)} %refs_2_.5) | copy-start | bytes 1966084
  0.7 1.8 %collective-permute-start = (bf16[160,256]{1,0:T(8,128)(2,1)}, bf16[160,256]{1,0:T(8,128)(2,1)S(1)}, u32[]{:S(2)}, u32[]{:S(2)}) collective-permute-start(bf16[160,256]{1,0:T(8,128)(2,1)} %refs_0_.4), channel_id=1, source_target_pairs={{0,4},{4,0},{8,12},{12,8},{16,20},{20,16},{24,28},{28,24},{1,5},{5... | collective-permute-start | bytes 245768 | tf_op jit(solution)/shard_map/ppermute | solution.py:328
  1.2 1.5 %collective-permute-start.1 = (bf16[160,256]{1,0:T(8,128)(2,1)}, bf16[160,256]{1,0:T(8,128)(2,1)S(1)}, u32[]{:S(2)}, u32[]{:S(2)}) collective-permute-start(bf16[160,256]{1,0:T(8,128)(2,1)} %refs_2_.4), channel_id=1, source_target_pairs={{0,4},{4,0},{8,12},{12,8},{16,20},{20,16},{24,28},{28,24},{1,5},{5... | collective-permute-start | bytes 245768 | tf_op jit(solution)/shard_map/ppermute | solution.py:328
  2.7 4.6 %copy-start.5 = (f32[160,16]{0,1:T(8,128)S(1)}, f32[160,16]{0,1:T(8,128)}, u32[]{:S(2)}) copy-start(f32[160,16]{0,1:T(8,128)} %param.13) | copy-start | bytes 30724
  2.7 4.6 %collective-permute-start.2 = (bf16[2,160,1024]{2,1,0:T(8,128)(2,1)S(1)}, bf16[2,160,1024]{2,1,0:T(8,128)(2,1)S(1)}, u32[]{:S(2)}, u32[]{:S(2)}) collective-permute-start(bf16[2,160,1024]{2,1,0:T(8,128)(2,1)S(1)} %get-tuple-element.34), channel_id=1, source_target_pairs={{0,4},{4,0},{8,12},{12,8},{16,20},{20,16},{24,28},{28,24},{1,5},{5... | collective-permute-start | bytes 1966088 | tf_op jit(solution)/shard_map/ppermute | solution.py:328
  3.0 7.5 %collective-permute-start.5 = (bf16[640,128]{1,0:T(8,128)(2,1)S(1)}, bf16[640,128]{1,0:T(8,128)(2,1)S(1)}, u32[]{:S(2)}, u32[]{:S(2)}) collective-permute-start(bf16[640,128]{1,0:T(8,128)(2,1)S(1)} %shard_map.95.refs_5_.refs_7_.refs_3_.refs_4_), channel_id=1, source_target_pairs={{0,16},{4,20},{8,24},{12,28},{16,0},{20,4},{24,8},{28,12},{1,17},{... | collective-permute-start | bytes 491528 | tf_op jit(solution)/shard_map/ppermute | solution.py:328
  5.8 6.6 %collective-permute-start.4 = (bf16[640,128]{1,0:T(8,128)(2,1)S(1)}, bf16[640,128]{1,0:T(8,128)(2,1)S(1)}, u32[]{:S(2)}, u32[]{:S(2)}) collective-permute-start(bf16[640,128]{1,0:T(8,128)(2,1)S(1)} %shard_map.95.refs_5_.refs_7_.refs_3_.refs_4_), channel_id=1, source_target_pairs={{0,8},{4,12},{8,0},{12,4},{16,24},{20,28},{24,16},{28,20},{1,9},{5... | collective-permute-start | bytes 491528 | tf_op jit(solution)/shard_map/ppermute | solution.py:328
  8.3 2.2 %collective-permute-start.3 = (f32[8,640]{1,0:T(8,128)S(1)}, f32[8,640]{1,0:T(8,128)S(1)}, u32[]{:S(2)}, u32[]{:S(2)}) collective-permute-start(f32[8,640]{1,0:T(8,128)S(1)} %get-tuple-element.40), channel_id=1, source_target_pairs={{0,4},{4,0},{8,12},{12,8},{16,20},{20,16},{24,28},{28,24},{1,5},{5... | collective-permute-start | bytes 61448 | tf_op jit(solution)/shard_map/ppermute | solution.py:328
  8.4 7.8 %collective-permute-start.6 = (bf16[640,128]{1,0:T(8,128)(2,1)S(1)}, bf16[640,128]{1,0:T(8,128)(2,1)S(1)}, u32[]{:S(2)}, u32[]{:S(2)}) collective-permute-start(bf16[640,128]{1,0:T(8,128)(2,1)S(1)} %get-tuple-element.41), channel_id=1, source_target_pairs={{0,24},{4,28},{8,16},{12,20},{16,8},{20,12},{24,0},{28,4},{1,25},{... | collective-permute-start | bytes 491528 | tf_op jit(solution)/shard_map/ppermute | solution.py:328
  13.6 7.1 %collective-permute-start.7 = (bf16[640,128]{1,0:T(8,128)(2,1)S(1)}, bf16[640,128]{1,0:T(8,128)(2,1)S(1)}, u32[]{:S(2)}, u32[]{:S(2)}) collective-permute-start(bf16[640,128]{1,0:T(8,128)(2,1)S(1)} %shard_map.100), channel_id=1, source_target_pairs={{0,8},{4,12},{8,0},{12,4},{16,24},{20,28},{24,16},{28,20},{1,9},{5... | collective-permute-start | bytes 491528 | tf_op jit(solution)/shard_map/ppermute | solution.py:328
  15.4 6.2 %collective-permute-start.8 = (bf16[640,128]{1,0:T(8,128)(2,1)S(1)}, bf16[640,128]{1,0:T(8,128)(2,1)S(1)}, u32[]{:S(2)}, u32[]{:S(2)}) collective-permute-start(bf16[640,128]{1,0:T(8,128)(2,1)S(1)} %shard_map.99.refs_8_), channel_id=1, source_target_pairs={{0,16},{4,20},{8,24},{12,28},{16,0},{20,4},{24,8},{28,12},{1,17},{... | collective-permute-start | bytes 491528 | tf_op jit(solution)/shard_map/ppermute | solution.py:328
  17.3 7.2 %collective-permute-start.9 = (bf16[320,128]{1,0:T(8,128)(2,1)S(1)}, bf16[320,128]{1,0:T(8,128)(2,1)S(1)}, u32[]{:S(2)}, u32[]{:S(2)}) collective-permute-start(bf16[320,128]{1,0:T(8,128)(2,1)S(1)} %get-tuple-element.44.refs_8_), channel_id=1, source_target_pairs={{0,24},{4,28},{8,16},{12,20},{16,8},{20,12},{24,0},{28,4},{1,25},{... | collective-permute-start | bytes 245768 | tf_op jit(solution)/shard_map/ppermute | solution.py:328
  19.2 5.3 %collective-permute-start.11 = (bf16[320,128]{1,0:T(8,128)(2,1)S(1)}, bf16[320,128]{1,0:T(8,128)(2,1)S(1)}, u32[]{:S(2)}, u32[]{:S(2)}) collective-permute-start(bf16[320,128]{1,0:T(8,128)(2,1)S(1)} %get-tuple-element.49), channel_id=1, source_target_pairs={{0,28},{4,24},{8,20},{12,16},{16,12},{20,8},{24,4},{28,0},{1,29},{... | collective-permute-start | bytes 245768 | tf_op jit(solution)/shard_map/ppermute | solution.py:328
  21.6 3.0 %collective-permute-start.10 = (f32[320,128]{1,0:T(8,128)S(1)}, f32[320,128]{1,0:T(8,128)S(1)}, u32[]{:S(2)}, u32[]{:S(2)}) collective-permute-start(f32[320,128]{1,0:T(8,128)S(1)} %get-tuple-element.48), channel_id=1, source_target_pairs={{0,4},{4,0},{8,12},{12,8},{16,20},{20,16},{24,28},{28,24},{1,5},{5... | collective-permute-start | bytes 491528 | tf_op jit(solution)/shard_map/ppermute | solution.py:328
  24.7 4.4 %collective-permute-start.12 = (bf16[2,640,128]{2,1,0:T(8,128)(2,1)S(1)}, bf16[2,640,128]{2,1,0:T(8,128)(2,1)S(1)}, u32[]{:S(2)}, u32[]{:S(2)}) collective-permute-start(bf16[2,640,128]{2,1,0:T(8,128)(2,1)S(1)} %shard_map.102), channel_id=1, source_target_pairs={{0,4},{4,0},{8,12},{12,8},{16,20},{20,16},{24,28},{28,24},{1,5},{5... | collective-permute-start | bytes 983048 | tf_op jit(solution)/shard_map/ppermute | solution.py:328
  24.9 7.7 %collective-permute-start.13 = (bf16[2,40,256]{2,1,0:T(8,128)(2,1)S(1)}, bf16[2,40,256]{2,1,0:T(8,128)(2,1)S(1)}, u32[]{:S(2)}, u32[]{:S(2)}) collective-permute-start(bf16[2,40,256]{2,1,0:T(8,128)(2,1)S(1)} %get-tuple-element.56), channel_id=1, source_target_pairs={{0,2},{1,3},{2,0},{3,1},{4,6},{5,7},{6,4},{7,5},{8,10},{9,11},{10,... | collective-permute-start | bytes 122888 | tf_op jit(solution)/shard_map/ppermute | solution.py:328
  27.5 5.8 %collective-permute-start.14 = (bf16[2,40,256]{2,1,0:T(8,128)(2,1)S(1)}, bf16[2,40,256]{2,1,0:T(8,128)(2,1)S(1)}, u32[]{:S(2)}, u32[]{:S(2)}) collective-permute-start(bf16[2,40,256]{2,1,0:T(8,128)(2,1)S(1)} %get-tuple-element.57), channel_id=1, source_target_pairs={{0,3},{1,2},{2,1},{3,0},{4,7},{5,6},{6,5},{7,4},{8,11},{9,10},{10,... | collective-permute-start | bytes 122888 | tf_op jit(solution)/shard_map/ppermute | solution.py:328
  28.8 4.5 %collective-permute-start.15 = (bf16[2,40,256]{2,1,0:T(8,128)(2,1)S(1)}, bf16[2,40,256]{2,1,0:T(8,128)(2,1)S(1)}, u32[]{:S(2)}, u32[]{:S(2)}) collective-permute-start(bf16[2,40,256]{2,1,0:T(8,128)(2,1)S(1)} %get-tuple-element.58), channel_id=1, source_target_pairs={{0,1},{1,0},{2,3},{3,2},{4,5},{5,4},{6,7},{7,6},{8,9},{9,8},{10,11... | collective-permute-start | bytes 122888 | tf_op jit(solution)/shard_map/ppermute | solution.py:328

commit v6 on v5

--- a/solution.py
+++ b/solution.py
@@ -210,7 +210,7 @@
     tokens = pieces[0].shape[0] // 4
     half = tokens // 2
     rows = 2 * tokens
-    grads = [0.0, 0.0]
+    jobs = {0: [], 1: []}
     columns = vectors[...].T
     spot = columns[:, 4:5]
     for start in range(0, len(pieces), 4):
@@ -233,22 +233,32 @@
                 least[0] = jnp.where(group == i, sign, least[0])
                 least[1] = jnp.where(group == i, -sign, least[1])
         runs = [(gather(at), gather(rows + at)) for at in (0, half)]
-        for which, run, limit in ((0, 0, least[0]), (1, 0, None), (1, 1, least[1])):
-            k, v = runs[run]
-            p = jnp.exp2(
-                nt(stack[which], k) * EXP2_SCALE - columns[:, which : which + 1]
-            )
-            if limit is not None:
-                p = jnp.where(spot >= limit, p, 0.0)
-            delta = columns[:, 2 + which : 3 + which]
-            ds = (p * (nt(stack[2 + which], v) - delta)).astype(BF16)
-            grads[which] = grads[which] + jnp.dot(ds, k, preferred_element_type=F32)
-    return [(x * SCALE).astype(BF16) for x in grads]
+        jobs[1] += [(1, runs[0], None), (1, runs[1], least[1])]
+        jobs[0].append((0, runs[0], least[0]))
+    listed = jobs[1] + jobs[0]
+
+    def products(job):
+        which, (k, v), _ = job
+        return nt(stack[which], k), nt(stack[2 + which], v)
+
+    grad = 0.0
+    ahead = products(listed[0])
+    for i, (which, (k, _), limit) in enumerate(listed):
+        (s, dp), ahead = ahead, products(listed[i + 1]) if i + 1 < len(listed) else None
+        p = jnp.exp2(s * EXP2_SCALE - columns[:, which : which + 1])
+        if limit is not None:
+            p = jnp.where(spot >= limit, p, 0.0)
+        ds = (p * (dp - columns[:, 2 + which : 3 + which])).astype(BF16)
+        grad = grad + jnp.dot(ds, k, preferred_element_type=F32)
+        if i + 1 == len(listed) or listed[i + 1][0] != which:
+            yield which, (grad * SCALE).astype(BF16)
+            grad = 0.0
 
 
 def sib_grad_kernel(larger, stack, vectors, *refs):
     pieces, out = refs[:-1], refs[-1]
-    out[0], out[1] = q_grads(1, larger, stack, vectors, pieces)
+    for which, grad in q_grads(1, larger, stack, vectors, pieces):
+        out[which] = grad
 
 
 def own_grad_kernel(heads, larger, stack, vectors, other, *refs):
@@ -273,9 +283,10 @@
     second = copies(held, c)
     for each in first:
         each.start()
-    held[0], held[1] = q_grads(0, larger, stack, vectors, pieces)
-    for each in second:
-        each.start()
+    for which, grad in q_grads(0, larger, stack, vectors, pieces):
+        held[which] = grad
+        for each in second[which * heads : (which + 1) * heads]:
+            each.start()
     for each in first + second:
         each.wait()
 

time: 34.1 us -> 34.1 us (level)
  waiting for transfers between devices: 3.24 us -> 3.71 us
  Pallas kernels: 13.9 us -> 13.5 us
    ppermute x16, waiting for transfers between devices: 3.24 us -> 3.71 us  [swap(): return lax.ppermute(x, axis, [(i, i ^ shift) for i in range(count)])]
    pallas_call x12, Pallas kernels: 13.9 us -> 13.5 us  [call(): pl.pallas_call(body, cost_estimate=pl.CostEstimate(flops=int(cost * FLOPS...]
  transfers between devices with their start and end apart: 16 -> 16, of which waited for: 5 -> 6; matrix products, arithmetic and copies ran while one was open for 0% -> 0% of each run, Pallas kernels for 39% -> 38%
where the time goes in v6:
time: 34.1 us; the launch traced here: 33.9 us
  starting transfers between devices  15.9 us (47%)
  Pallas kernels  13.5 us (40%)
  waiting for transfers between devices  3.71 us (11%)
  between operations  0.81 us (2%)
    ppermute x16, starting transfers between devices, swap(): return lax.ppermute(x, axis, [(i, i ^ shift) for i in range(count)])  15.9 us
    pallas_call x12, Pallas kernels, call(): pl.pallas_call(body, cost_estimate=pl.CostEstimate(flops=int(cost * FLOPS...  13.5 us
    ppermute x16, waiting for transfers between devices, swap(): return lax.ppermute(x, axis, [(i, i ^ shift) for i in range(count)])  3.71 us
  transfers between devices with their start and end apart: 16, of which 6 were waited for; matrix products, arithmetic and copies ran while one was open for 0% of the time, Pallas kernels for 38%

profile of v6, /device:TPU:0, one launch (start us, length us, event | category | flops | bytes accessed | tf_op | source)
XLA Modules:
  0.0 33.9 jit_solution(9806301963863614904)
XLA Ops:
  0.7 0.5 %collective-permute-start = (bf16[160,256]{1,0:T(8,128)(2,1)}, bf16[160,256]{1,0:T(8,128)(2,1)S(1)}, u32[]{:S(2)}, u32[]{:S(2)}) collective-permute-start(bf16[160,256]{1,0:T(8,128)(2,1)} %refs_0_.4), channel_id=1, source_target_pairs={{0,4},{4,0},{8,12},{12,8},{16,20},{20,16},{24,28},{28,24},{1,5},{5... | collective-permute-start | bytes 245768 | tf_op jit(solution)/shard_map/ppermute | solution.py:339
  1.2 0.1 collective-permute-start.1
  1.3 1.1 %shard_map.94 = (bf16[2,160,1024]{2,1,0:T(8,128)(2,1)S(1)}, f32[16,128]{1,0:T(8,128)S(1)}) custom-call(bf16[160,2048]{1,0:T(8,128)(2,1)} %refs_0_.5, bf16[160,2048]{1,0:T(8,128)(2,1)} %refs_1_.3, s32[1280]{0:T(1024)} %refs_2_.3), custom_call_target="tpu_custom_call" | custom-call | flops 1100000000 | bytes 1315840 | tf_op jit(solution)/shard_map/pallas_call | solution.py:35
  2.4 0.2 collective-permute-done.1.refs_3_
  2.7 0.3 collective-permute-start.2
  3.0 2.8 %collective-permute-start.5 = (bf16[640,128]{1,0:T(8,128)(2,1)S(1)}, bf16[640,128]{1,0:T(8,128)(2,1)S(1)}, u32[]{:S(2)}, u32[]{:S(2)}) collective-permute-start(bf16[640,128]{1,0:T(8,128)(2,1)S(1)} %shard_map.95.refs_5_.refs_7_.refs_3_.refs_4_), channel_id=1, source_target_pairs={{0,16},{4,20},{8,24},{12,28},{16,0},{20,4},{24,8},{28,12},{1,17},{... | collective-permute-start | bytes 491528 | tf_op jit(solution)/shard_map/ppermute | solution.py:339
  5.8 1.5 %collective-permute-start.4 = (bf16[640,128]{1,0:T(8,128)(2,1)S(1)}, bf16[640,128]{1,0:T(8,128)(2,1)S(1)}, u32[]{:S(2)}, u32[]{:S(2)}) collective-permute-start(bf16[640,128]{1,0:T(8,128)(2,1)S(1)} %shard_map.95.refs_5_.refs_7_.refs_3_.refs_4_), channel_id=1, source_target_pairs={{0,8},{4,12},{8,0},{12,4},{16,24},{20,28},{24,16},{28,20},{1,9},{5... | collective-permute-start | bytes 491528 | tf_op jit(solution)/shard_map/ppermute | solution.py:339
  7.3 0.9 %shard_map.96 = (f32[8,640]{1,0:T(8,128)S(1)}, f32[8,640]{1,0:T(8,128)S(1)}, bf16[4,640,128]{2,1,0:T(8,128)(2,1)S(1)}, bf16[4,128,640]{2,1,0:T(8,128)(2,1)S(1)},...) custom-call(bf16[160,2048]{1,0:T(8,128)(2,1)S(1)} %copy-done.2, ...), custom_call_target="tpu_custom_call" | custom-call | flops 1100000000 | bytes 2795520 | tf_op jit(solution)/shard_map/pallas_call | solution.py:35
  8.3 0.1 collective-permute-start.3
  8.4 1.4 %collective-permute-start.6 = (bf16[640,128]{1,0:T(8,128)(2,1)S(1)}, bf16[640,128]{1,0:T(8,128)(2,1)S(1)}, u32[]{:S(2)}, u32[]{:S(2)}) collective-permute-start(bf16[640,128]{1,0:T(8,128)(2,1)S(1)} %get-tuple-element.41), channel_id=1, source_target_pairs={{0,24},{4,28},{8,16},{12,20},{16,8},{20,12},{24,0},{28,4},{1,25},{... | collective-permute-start | bytes 491528 | tf_op jit(solution)/shard_map/ppermute | solution.py:339
  9.8 0.7 %collective-permute-done.5.refs_7_.refs_5_.refs_6_ = bf16[640,128]{1,0:T(8,128)(2,1)S(1)} collective-permute-done((bf16[640,128]{1,0:T(8,128)(2,1)S(1)}, bf16[640,128]{1,0:T(8,128)(2,1)S(1)}, u32[]{:S(2)}, u32[]{:S(2)}) %collective-permute-start.5) | collective-permute-done | bytes 163872 | tf_op jit(solution)/shard_map/ppermute | solution.py:339
  10.5 1.2 %shard_map.99.refs_8_ = bf16[640,128]{1,0:T(8,128)(2,1)S(1)} custom-call(f32[16,128]{1,0:T(8,128)S(1)} %get-tuple-element.32.refs_0_, bf16[4,640,128]{2,1,0:T(8,128)(2,1)S(1)} %get-tuple-element.37.refs_1_, bf16[4,640,128]{2,1,0:T(8,128)(2,1)S(1)} %get-tuple-element.39.refs_2_.refs_1_, bf16[4,128,640]{2,1,0:T(8,128)(2,1)S(1)} %get-tuple-element.42.refs_3_, ...), custom_call_target="tpu_custom_call" | custom-call | flops 550000000 | bytes 2834432 | tf_op jit(solution)/shard_map/pallas_call | solution.py:35
  11.6 0.7 %collective-permute-done.4.refs_7_.refs_4_.refs_5_ = bf16[640,128]{1,0:T(8,128)(2,1)S(1)} collective-permute-done((bf16[640,128]{1,0:T(8,128)(2,1)S(1)}, bf16[640,128]{1,0:T(8,128)(2,1)S(1)}, u32[]{:S(2)}, u32[]{:S(2)}) %collective-permute-start.4) | collective-permute-done | bytes 163872 | tf_op jit(solution)/shard_map/ppermute | solution.py:339
  12.4 1.2 %shard_map.100 = bf16[640,128]{1,0:T(8,128)(2,1)S(1)} custom-call(f32[16,128]{1,0:T(8,128)S(1)} %get-tuple-element.32.refs_0_, bf16[4,640,128]{2,1,0:T(8,128)(2,1)S(1)} %get-tuple-element.37.refs_1_, bf16[4,640,128]{2,1,0:T(8,128)(2,1)S(1)} %get-tuple-element.39.refs_2_.refs_1_, bf16[4,128,640]{2,1,0:T(8,128)(2,1)S(1)} %get-tuple-element.42.refs_3_, ...), custom_call_target="tpu_custom_call" | custom-call | flops 550000000 | bytes 2834432 | tf_op jit(solution)/shard_map/pallas_call | solution.py:35
  13.5 1.8 %collective-permute-start.7 = (bf16[640,128]{1,0:T(8,128)(2,1)S(1)}, bf16[640,128]{1,0:T(8,128)(2,1)S(1)}, u32[]{:S(2)}, u32[]{:S(2)}) collective-permute-start(bf16[640,128]{1,0:T(8,128)(2,1)S(1)} %shard_map.100), channel_id=1, source_target_pairs={{0,8},{4,12},{8,0},{12,4},{16,24},{20,28},{24,16},{28,20},{1,9},{5... | collective-permute-start | bytes 491528 | tf_op jit(solution)/shard_map/ppermute | solution.py:339
  15.4 0.8 %collective-permute-start.8 = (bf16[640,128]{1,0:T(8,128)(2,1)S(1)}, bf16[640,128]{1,0:T(8,128)(2,1)S(1)}, u32[]{:S(2)}, u32[]{:S(2)}) collective-permute-start(bf16[640,128]{1,0:T(8,128)(2,1)S(1)} %shard_map.99.refs_8_), channel_id=1, source_target_pairs={{0,16},{4,20},{8,24},{12,28},{16,0},{20,4},{24,8},{28,12},{1,17},{... | collective-permute-start | bytes 491528 | tf_op jit(solution)/shard_map/ppermute | solution.py:339
  16.2 1.2 %shard_map.97 = (bf16[320,128]{1,0:T(8,128)(2,1)S(1)}, bf16[320,128]{1,0:T(8,128)(2,1)S(1)}) custom-call(f32[16,128]{1,0:T(8,128)S(1)} %get-tuple-element.32.refs_0_, bf16[4,640,128]{2,1,0:T(8,128)(2,1)S(1)} %get-tuple-element.37.refs_1_, bf16[4,640,128]{2,1,0:T(8,128)(2,1)S(1)} %get-tuple-element.39.refs_2_.refs_1_, ...), custom_call_target="tpu_custom_call" | custom-call | flops 550000000 | bytes 2834432 | tf_op jit(solution)/shard_map/pallas_call | solution.py:35
  17.4 1.9 %collective-permute-start.9 = (bf16[320,128]{1,0:T(8,128)(2,1)S(1)}, bf16[320,128]{1,0:T(8,128)(2,1)S(1)}, u32[]{:S(2)}, u32[]{:S(2)}) collective-permute-start(bf16[320,128]{1,0:T(8,128)(2,1)S(1)} %get-tuple-element.44.refs_8_), channel_id=1, source_target_pairs={{0,24},{4,28},{8,16},{12,20},{16,8},{20,12},{24,0},{28,4},{1,25},{... | collective-permute-start | bytes 245768 | tf_op jit(solution)/shard_map/ppermute | solution.py:339
  19.3 1.4 %shard_map.98 = (f32[320,128]{1,0:T(8,128)S(1)}, f32[320,128]{1,0:T(8,128)S(1)}) custom-call(f32[16,128]{1,0:T(8,128)S(1)} %get-tuple-element.32.refs_0_, bf16[4,640,128]{2,1,0:T(8,128)(2,1)S(1)} %get-tuple-element.37.refs_1_, bf16[4,640,128]{2,1,0:T(8,128)(2,1)S(1)} %get-tuple-element.39.refs_2_.refs_1_, ...), custom_call_target="tpu_custom_call" | custom-call | flops 550000000 | bytes 2834432 | tf_op jit(solution)/shard_map/pallas_call | solution.py:35
  20.7 0.9 %collective-permute-done.8.refs_3_ = bf16[640,128]{1,0:T(8,128)(2,1)S(1)} collective-permute-done((bf16[640,128]{1,0:T(8,128)(2,1)S(1)}, bf16[640,128]{1,0:T(8,128)(2,1)S(1)}, u32[]{:S(2)}, u32[]{:S(2)}) %collective-permute-start.8) | collective-permute-done | bytes 163872 | tf_op jit(solution)/shard_map/ppermute | solution.py:339
  21.6 0.1 shard_map.101
  21.6 0.4 %collective-permute-start.10 = (f32[320,128]{1,0:T(8,128)S(1)}, f32[320,128]{1,0:T(8,128)S(1)}, u32[]{:S(2)}, u32[]{:S(2)}) collective-permute-start(f32[320,128]{1,0:T(8,128)S(1)} %get-tuple-element.48), channel_id=1, source_target_pairs={{0,4},{4,0},{8,12},{12,8},{16,20},{20,16},{24,28},{28,24},{1,5},{5... | collective-permute-start | bytes 491528 | tf_op jit(solution)/shard_map/ppermute | solution.py:339
  22.0 2.3 %shard_map.102 = bf16[2,640,128]{2,1,0:T(8,128)(2,1)S(1)} custom-call(f32[16,128]{1,0:T(8,128)S(1)} %get-tuple-element.32.refs_0_, bf16[4,640,128]{2,1,0:T(8,128)(2,1)S(1)} %get-tuple-element.39.refs_2_.refs_1_, f32[8,640]{1,0:T(8,128)S(1)} %collective-permute-done.3.refs_6_.refs_2_, bf16[640,128]{1,0:T(8,128)(2,1)S(1)} %shard_map.95.refs_5_.refs_7_.refs_3_.refs_4_, ...), custom_call_target="tpu_custom_call" | custom-call | flops 2750000128 | bytes 1339392 | tf_op jit(solution)/shard_map/pallas_call | solution.py:35
  24.4 0.1 collective-permute-done.11.refs_3_
  24.5 0.1 shard_map.103
  24.6 0.1 collective-permute-start.12
  24.7 2.6 %collective-permute-start.13 = (bf16[2,40,256]{2,1,0:T(8,128)(2,1)S(1)}, bf16[2,40,256]{2,1,0:T(8,128)(2,1)S(1)}, u32[]{:S(2)}, u32[]{:S(2)}) collective-permute-start(bf16[2,40,256]{2,1,0:T(8,128)(2,1)S(1)} %get-tuple-element.56), channel_id=1, source_target_pairs={{0,2},{1,3},{2,0},{3,1},{4,6},{5,7},{6,4},{7,5},{8,10},{9,11},{10,... | collective-permute-start | bytes 122888 | tf_op jit(solution)/shard_map/ppermute | solution.py:339
  27.3 1.4 %collective-permute-start.14 = (bf16[2,40,256]{2,1,0:T(8,128)(2,1)S(1)}, bf16[2,40,256]{2,1,0:T(8,128)(2,1)S(1)}, u32[]{:S(2)}, u32[]{:S(2)}) collective-permute-start(bf16[2,40,256]{2,1,0:T(8,128)(2,1)S(1)} %get-tuple-element.57), channel_id=1, source_target_pairs={{0,3},{1,2},{2,1},{3,0},{4,7},{5,6},{6,5},{7,4},{8,11},{9,10},{10,... | collective-permute-start | bytes 122888 | tf_op jit(solution)/shard_map/ppermute | solution.py:339
  28.7 0.2 collective-permute-start.15
  28.9 3.3 %shard_map.104.refs_4_ = bf16[160,2048]{1,0:T(8,128)(2,1)} custom-call(f32[16,128]{1,0:T(8,128)S(1)} %get-tuple-element.32.refs_0_, bf16[4,640,128]{2,1,0:T(8,128)(2,1)S(1)} %get-tuple-element.37.refs_1_, f32[8,640]{1,0:T(8,128)S(1)} %get-tuple-element.38.refs_5_.refs_2_, bf16[2,640,128]{2,1,0:T(8,128)(2,1)S(1)} %collective-permute-done.12.refs_3_, ...), custom_call_target="tpu_custom_call" | custom-call | flops 3300000000 | bytes 1667072 | tf_op jit(solution)/shard_map/pallas_call | solution.py:35
  32.2 1.0 %collective-permute-done.14.refs_2_ = bf16[2,40,256]{2,1,0:T(8,128)(2,1)S(1)} collective-permute-done((bf16[2,40,256]{2,1,0:T(8,128)(2,1)S(1)}, bf16[2,40,256]{2,1,0:T(8,128)(2,1)S(1)}, u32[]{:S(2)}, u32[]{:S(2)}) %collective-permute-start.14) | collective-permute-done | bytes 40992 | tf_op jit(solution)/shard_map/ppermute | solution.py:339
  33.3 0.7 %shard_map.105 = (bf16[40,1024]{1,0:T(8,128)(2,1)}, bf16[40,1024]{1,0:T(8,128)(2,1)}) custom-call(bf16[2,40,256]{2,1,0:T(8,128)(2,1)S(1)} %get-tuple-element.55.refs_8_.refs_0_, bf16[2,40,256]{2,1,0:T(8,128)(2,1)S(1)} %collective-permute-done.13.refs_1_, bf16[2,40,256]{2,1,0:T(8,128)(2,1)S(1)} %collective-permute-done.14.refs_2_, ...), custom_call_target="tpu_custom_call" | custom-call | flops 110000000 | bytes 163840 | tf_op jit(solution)/shard_map/pallas_call | solution.py:35
  (24 shorter events, 0.1 us)
Async XLA Ops:
  0.6 2.3 %copy-start = (bf16[160,256]{1,0:T(8,128)(2,1)S(1)}, bf16[160,256]{1,0:T(8,128)(2,1)}, u32[]{:S(2)}) copy-start(bf16[160,256]{1,0:T(8,128)(2,1)} %refs_0_.4) | copy-start | bytes 245764
  0.6 2.3 %copy-start.1 = (bf16[160,256]{1,0:T(8,128)(2,1)S(1)}, bf16[160,256]{1,0:T(8,128)(2,1)}, u32[]{:S(2)}) copy-start(bf16[160,256]{1,0:T(8,128)(2,1)} %refs_2_.4) | copy-start | bytes 245764
  0.7 6.7 %copy-start.2 = (bf16[160,2048]{1,0:T(8,128)(2,1)S(1)}, bf16[160,2048]{1,0:T(8,128)(2,1)}, u32[]{:S(2)}) copy-start(bf16[160,2048]{1,0:T(8,128)(2,1)} %refs_0_.5) | copy-start | bytes 1966084
  0.7 6.7 %copy-start.3 = (bf16[160,2048]{1,0:T(8,128)(2,1)S(1)}, bf16[160,2048]{1,0:T(8,128)(2,1)}, u32[]{:S(2)}) copy-start(bf16[160,2048]{1,0:T(8,128)(2,1)} %refs_1_.3) | copy-start | bytes 1966084
  0.7 6.7 %copy-start.4 = (bf16[160,2048]{1,0:T(8,128)(2,1)S(1)}, bf16[160,2048]{1,0:T(8,128)(2,1)}, u32[]{:S(2)}) copy-start(bf16[160,2048]{1,0:T(8,128)(2,1)} %refs_2_.5) | copy-start | bytes 1966084
  0.7 1.8 %collective-permute-start = (bf16[160,256]{1,0:T(8,128)(2,1)}, bf16[160,256]{1,0:T(8,128)(2,1)S(1)}, u32[]{:S(2)}, u32[]{:S(2)}) collective-permute-start(bf16[160,256]{1,0:T(8,128)(2,1)} %refs_0_.4), channel_id=1, source_target_pairs={{0,4},{4,0},{8,12},{12,8},{16,20},{20,16},{24,28},{28,24},{1,5},{5... | collective-permute-start | bytes 245768 | tf_op jit(solution)/shard_map/ppermute | solution.py:339
  1.2 1.5 %collective-permute-start.1 = (bf16[160,256]{1,0:T(8,128)(2,1)}, bf16[160,256]{1,0:T(8,128)(2,1)S(1)}, u32[]{:S(2)}, u32[]{:S(2)}) collective-permute-start(bf16[160,256]{1,0:T(8,128)(2,1)} %refs_2_.4), channel_id=1, source_target_pairs={{0,4},{4,0},{8,12},{12,8},{16,20},{20,16},{24,28},{28,24},{1,5},{5... | collective-permute-start | bytes 245768 | tf_op jit(solution)/shard_map/ppermute | solution.py:339
  2.7 4.6 %copy-start.5 = (f32[160,16]{0,1:T(8,128)S(1)}, f32[160,16]{0,1:T(8,128)}, u32[]{:S(2)}) copy-start(f32[160,16]{0,1:T(8,128)} %param.13) | copy-start | bytes 30724
  2.7 4.6 %collective-permute-start.2 = (bf16[2,160,1024]{2,1,0:T(8,128)(2,1)S(1)}, bf16[2,160,1024]{2,1,0:T(8,128)(2,1)S(1)}, u32[]{:S(2)}, u32[]{:S(2)}) collective-permute-start(bf16[2,160,1024]{2,1,0:T(8,128)(2,1)S(1)} %get-tuple-element.34), channel_id=1, source_target_pairs={{0,4},{4,0},{8,12},{12,8},{16,20},{20,16},{24,28},{28,24},{1,5},{5... | collective-permute-start | bytes 1966088 | tf_op jit(solution)/shard_map/ppermute | solution.py:339
  3.0 7.5 %collective-permute-start.5 = (bf16[640,128]{1,0:T(8,128)(2,1)S(1)}, bf16[640,128]{1,0:T(8,128)(2,1)S(1)}, u32[]{:S(2)}, u32[]{:S(2)}) collective-permute-start(bf16[640,128]{1,0:T(8,128)(2,1)S(1)} %shard_map.95.refs_5_.refs_7_.refs_3_.refs_4_), channel_id=1, source_target_pairs={{0,16},{4,20},{8,24},{12,28},{16,0},{20,4},{24,8},{28,12},{1,17},{... | collective-permute-start | bytes 491528 | tf_op jit(solution)/shard_map/ppermute | solution.py:339
  5.8 6.6 %collective-permute-start.4 = (bf16[640,128]{1,0:T(8,128)(2,1)S(1)}, bf16[640,128]{1,0:T(8,128)(2,1)S(1)}, u32[]{:S(2)}, u32[]{:S(2)}) collective-permute-start(bf16[640,128]{1,0:T(8,128)(2,1)S(1)} %shard_map.95.refs_5_.refs_7_.refs_3_.refs_4_), channel_id=1, source_target_pairs={{0,8},{4,12},{8,0},{12,4},{16,24},{20,28},{24,16},{28,20},{1,9},{5... | collective-permute-start | bytes 491528 | tf_op jit(solution)/shard_map/ppermute | solution.py:339
  8.3 2.2 %collective-permute-start.3 = (f32[8,640]{1,0:T(8,128)S(1)}, f32[8,640]{1,0:T(8,128)S(1)}, u32[]{:S(2)}, u32[]{:S(2)}) collective-permute-start(f32[8,640]{1,0:T(8,128)S(1)} %get-tuple-element.40), channel_id=1, source_target_pairs={{0,4},{4,0},{8,12},{12,8},{16,20},{20,16},{24,28},{28,24},{1,5},{5... | collective-permute-start | bytes 61448 | tf_op jit(solution)/shard_map/ppermute | solution.py:339
  8.4 7.8 %collective-permute-start.6 = (bf16[640,128]{1,0:T(8,128)(2,1)S(1)}, bf16[640,128]{1,0:T(8,128)(2,1)S(1)}, u32[]{:S(2)}, u32[]{:S(2)}) collective-permute-start(bf16[640,128]{1,0:T(8,128)(2,1)S(1)} %get-tuple-element.41), channel_id=1, source_target_pairs={{0,24},{4,28},{8,16},{12,20},{16,8},{20,12},{24,0},{28,4},{1,25},{... | collective-permute-start | bytes 491528 | tf_op jit(solution)/shard_map/ppermute | solution.py:339
  13.5 7.2 %collective-permute-start.7 = (bf16[640,128]{1,0:T(8,128)(2,1)S(1)}, bf16[640,128]{1,0:T(8,128)(2,1)S(1)}, u32[]{:S(2)}, u32[]{:S(2)}) collective-permute-start(bf16[640,128]{1,0:T(8,128)(2,1)S(1)} %shard_map.100), channel_id=1, source_target_pairs={{0,8},{4,12},{8,0},{12,4},{16,24},{20,28},{24,16},{28,20},{1,9},{5... | collective-permute-start | bytes 491528 | tf_op jit(solution)/shard_map/ppermute | solution.py:339
  15.4 6.2 %collective-permute-start.8 = (bf16[640,128]{1,0:T(8,128)(2,1)S(1)}, bf16[640,128]{1,0:T(8,128)(2,1)S(1)}, u32[]{:S(2)}, u32[]{:S(2)}) collective-permute-start(bf16[640,128]{1,0:T(8,128)(2,1)S(1)} %shard_map.99.refs_8_), channel_id=1, source_target_pairs={{0,16},{4,20},{8,24},{12,28},{16,0},{20,4},{24,8},{28,12},{1,17},{... | collective-permute-start | bytes 491528 | tf_op jit(solution)/shard_map/ppermute | solution.py:339
  17.4 7.0 %collective-permute-start.9 = (bf16[320,128]{1,0:T(8,128)(2,1)S(1)}, bf16[320,128]{1,0:T(8,128)(2,1)S(1)}, u32[]{:S(2)}, u32[]{:S(2)}) collective-permute-start(bf16[320,128]{1,0:T(8,128)(2,1)S(1)} %get-tuple-element.44.refs_8_), channel_id=1, source_target_pairs={{0,24},{4,28},{8,16},{12,20},{16,8},{20,12},{24,0},{28,4},{1,25},{... | collective-permute-start | bytes 245768 | tf_op jit(solution)/shard_map/ppermute | solution.py:339
  19.3 5.3 %collective-permute-start.11 = (bf16[320,128]{1,0:T(8,128)(2,1)S(1)}, bf16[320,128]{1,0:T(8,128)(2,1)S(1)}, u32[]{:S(2)}, u32[]{:S(2)}) collective-permute-start(bf16[320,128]{1,0:T(8,128)(2,1)S(1)} %get-tuple-element.49), channel_id=1, source_target_pairs={{0,28},{4,24},{8,20},{12,16},{16,12},{20,8},{24,4},{28,0},{1,29},{... | collective-permute-start | bytes 245768 | tf_op jit(solution)/shard_map/ppermute | solution.py:339
  21.6 2.9 %collective-permute-start.10 = (f32[320,128]{1,0:T(8,128)S(1)}, f32[320,128]{1,0:T(8,128)S(1)}, u32[]{:S(2)}, u32[]{:S(2)}) collective-permute-start(f32[320,128]{1,0:T(8,128)S(1)} %get-tuple-element.48), channel_id=1, source_target_pairs={{0,4},{4,0},{8,12},{12,8},{16,20},{20,16},{24,28},{28,24},{1,5},{5... | collective-permute-start | bytes 491528 | tf_op jit(solution)/shard_map/ppermute | solution.py:339
  24.6 4.3 %collective-permute-start.12 = (bf16[2,640,128]{2,1,0:T(8,128)(2,1)S(1)}, bf16[2,640,128]{2,1,0:T(8,128)(2,1)S(1)}, u32[]{:S(2)}, u32[]{:S(2)}) collective-permute-start(bf16[2,640,128]{2,1,0:T(8,128)(2,1)S(1)} %shard_map.102), channel_id=1, source_target_pairs={{0,4},{4,0},{8,12},{12,8},{16,20},{20,16},{24,28},{28,24},{1,5},{5... | collective-permute-start | bytes 983048 | tf_op jit(solution)/shard_map/ppermute | solution.py:339
  24.7 7.5 %collective-permute-start.13 = (bf16[2,40,256]{2,1,0:T(8,128)(2,1)S(1)}, bf16[2,40,256]{2,1,0:T(8,128)(2,1)S(1)}, u32[]{:S(2)}, u32[]{:S(2)}) collective-permute-start(bf16[2,40,256]{2,1,0:T(8,128)(2,1)S(1)} %get-tuple-element.56), channel_id=1, source_target_pairs={{0,2},{1,3},{2,0},{3,1},{4,6},{5,7},{6,4},{7,5},{8,10},{9,11},{10,... | collective-permute-start | bytes 122888 | tf_op jit(solution)/shard_map/ppermute | solution.py:339
  27.3 5.9 %collective-permute-start.14 = (bf16[2,40,256]{2,1,0:T(8,128)(2,1)S(1)}, bf16[2,40,256]{2,1,0:T(8,128)(2,1)S(1)}, u32[]{:S(2)}, u32[]{:S(2)}) collective-permute-start(bf16[2,40,256]{2,1,0:T(8,128)(2,1)S(1)} %get-tuple-element.57), channel_id=1, source_target_pairs={{0,3},{1,2},{2,1},{3,0},{4,7},{5,6},{6,5},{7,4},{8,11},{9,10},{10,... | collective-permute-start | bytes 122888 | tf_op jit(solution)/shard_map/ppermute | solution.py:339
  28.7 4.5 %collective-permute-start.15 = (bf16[2,40,256]{2,1,0:T(8,128)(2,1)S(1)}, bf16[2,40,256]{2,1,0:T(8,128)(2,1)S(1)}, u32[]{:S(2)}, u32[]{:S(2)}) collective-permute-start(bf16[2,40,256]{2,1,0:T(8,128)(2,1)S(1)} %get-tuple-element.58), channel_id=1, source_target_pairs={{0,1},{1,0},{2,3},{3,2},{4,5},{5,4},{6,7},{7,6},{8,9},{9,8},{10,11... | collective-permute-start | bytes 122888 | tf_op jit(solution)/shard_map/ppermute | solution.py:339

commit v7 on v6

--- a/solution.py
+++ b/solution.py
@@ -150,15 +150,15 @@
     return piece[pl.ds(at, half), :], piece[pl.ds(rows + at, half), :]
 
 
-def kv_grad_kernel(pair, larger, own, sib, own_t, sib_t, own_rows, sib_rows, piece, *outs):
+def kv_grad_kernel(pair, members, larger, own, sib, own_t, sib_t, own_rows, sib_rows, piece, *outs):
     tokens = piece.shape[0] // 4
     half = tokens // 2
     lanes = own.shape[1]
     stacks, turned, vectors = (own, sib), (own_t, sib_t), (own_rows, sib_rows)
-    first = [one_run(piece, tokens, half, a, 0) for a in range(2)]
+    first = [one_run(piece, tokens, half, a, 0) for a in members]
     k, v = (jnp.concatenate(x, axis=0) for x in zip(*first))
     jobs = [(k, v, b, 1, None) for b in range(2)]
-    for a in range(2):
+    for a in members:
         for b in range(2):
             if pair == 0 and a == b:
                 jobs += [(*one_run(piece, tokens, half, a, w), b, w, (a, w)) for w in range(2)]
@@ -177,7 +177,7 @@
         s = jnp.dot(k, turned[b][which], preferred_element_type=F32)
         return s, jnp.dot(v, turned[b][2 + which], preferred_element_type=F32)
 
-    sums = {(a, w): [] for a in range(2) for w in range(2)}
+    sums = {(a, w): [] for a in members for w in range(2)}
     ahead = products(jobs[0])
     for i, job in enumerate(jobs):
         (s, dp), ahead = ahead, products(jobs[i + 1]) if i + 1 < len(jobs) else None
@@ -190,8 +190,8 @@
         key_term = jnp.dot(ds, stacks[b][which], preferred_element_type=F32)
         both = key_term, value_term
         if place is None:
-            for a in range(2):
-                sums[a, 0].append([x[a * half : (a + 1) * half] for x in both])
+            for i, a in enumerate(members):
+                sums[a, 0].append([x[i * half : (i + 1) * half] for x in both])
         elif isinstance(which, int):
             sums[place].append(both)
         else:
@@ -199,8 +199,9 @@
             sums[a, 0].append([jnp.where(second, 0.0, x) for x in both])
             sums[a, 1].append([jnp.where(second, x, 0.0) for x in both])
     for (a, w), parts in sums.items():
-        out = outs[a % len(outs)]
-        at = w * half + (a * 2 * tokens if len(outs) == 1 else 0)
+        i = members.index(a)
+        out = outs[i % len(outs)]
+        at = w * half + (i * 2 * tokens if len(outs) == 1 else 0)
         out[at : at + half, :] = (sum(x[0] for x in parts) * SCALE).astype(out.dtype)
         at += tokens
         out[at : at + half, :] = sum(x[1] for x in parts).astype(out.dtype)
@@ -378,26 +379,26 @@
     }
     pieces = [kv_chip] + [pieces[pair] for pair in range(1, n // 2)]
 
-    def kv_grads(pair, after=()):
-        if pair in (0, late):
-            outs = [(half_piece[0], BF16 if pair else F32)] * 2
-        else:
-            outs = [piece]
+    def kv_grads(pair, outs, members=(0, 1), after=()):
         return call(
-            functools.partial(kv_grad_kernel, pair),
+            functools.partial(kv_grad_kernel, pair, members),
             outs,
             [larger, own, sib, own_t, sib_t, own_rows, sib_rows, pieces[pair]],
-            cost=0.5,
+            cost=0.25 * len(members),
             after=after,
         )
 
     partials = {}
     for pair in reversed(range(1, late)):
-        partials[pair] = kv_grads(pair, partials[pair + 1] if pair + 1 < late else [])
-    partials[late] = kv_grads(late)
-    local = kv_grads(0, partials[late][:1])
-    received = [swap(partials[pair][0], "ctx", 2 * pair) for pair in range(1, late)]
-    last = [swap(x, "ctx", 2 * late + a) for a, x in enumerate(partials[late])]
+        earlier = partials[pair + 1] if pair + 1 < late else []
+        partials[pair] = kv_grads(pair, [piece], after=earlier)
+    crossing = kv_grads(late, [half_piece], (1,))
+    diagonal = kv_grads(late, [half_piece], (0,), crossing) + crossing
+    local = kv_grads(0, [(half_piece[0], F32)] * 2, after=diagonal[:1])
+    flat = lax.optimization_barrier(tuple(partials[pair][0] for pair in (2, 1)))
+    flat = dict(zip((2, 1), flat))
+    received = [swap(flat[pair], "ctx", 2 * pair) for pair in (2, 1)]
+    last = [swap(x, "ctx", 2 * late + a) for a, x in enumerate(diagonal)]
 
     sums = ((2 * tokens, HEAD_SIZE), F32)
     sum_same, sum_other = call(sum_kernel, [sums] * 2, [*local, *received])

time: 34.1 us -> 34 us (level)
  waiting for transfers between devices: 3.71 us -> 2.67 us
  starting transfers between devices: 15.9 us -> 16.5 us
    ppermute x16, waiting for transfers between devices: 3.71 us -> 2.67 us  [swap(): return lax.ppermute(x, axis, [(i, i ^ shift) for i in range(count)])]
    ppermute x16, starting transfers between devices: 15.9 us -> 16.5 us  [swap(): return lax.ppermute(x, axis, [(i, i ^ shift) for i in range(count)])]
    pallas_call x12 -> x13, Pallas kernels: 13.5 us -> 13.8 us  [call(): pl.pallas_call(body, cost_estimate=pl.CostEstimate(flops=int(cost * FLOPS...]
  transfers between devices with their start and end apart: 16 -> 16, of which waited for: 6 -> 5; matrix products, arithmetic and copies ran while one was open for 0% -> 0% of each run, Pallas kernels for 38% -> 39%
where the time goes in v7:
time: 34 us; the launch traced here: 33.8 us
  starting transfers between devices  16.5 us (49%)
  Pallas kernels  13.8 us (41%)
  waiting for transfers between devices  2.67 us (8%)
  between operations  0.81 us (2%)
    ppermute x16, starting transfers between devices, swap(): return lax.ppermute(x, axis, [(i, i ^ shift) for i in range(count)])  16.5 us
    pallas_call x13, Pallas kernels, call(): pl.pallas_call(body, cost_estimate=pl.CostEstimate(flops=int(cost * FLOPS...  13.8 us
    ppermute x16, waiting for transfers between devices, swap(): return lax.ppermute(x, axis, [(i, i ^ shift) for i in range(count)])  2.67 us
  transfers between devices with their start and end apart: 16, of which 5 were waited for; matrix products, arithmetic and copies ran while one was open for 0% of the time, Pallas kernels for 39%

profile of v7, /device:TPU:0, one launch (start us, length us, event | category | flops | bytes accessed | tf_op | source)
XLA Modules:
  0.0 33.8 jit_solution(845696240908224116)
XLA Ops:
  0.7 0.5 %collective-permute-start = (bf16[160,256]{1,0:T(8,128)(2,1)}, bf16[160,256]{1,0:T(8,128)(2,1)S(1)}, u32[]{:S(2)}, u32[]{:S(2)}) collective-permute-start(bf16[160,256]{1,0:T(8,128)(2,1)} %refs_0_.4), channel_id=1, source_target_pairs={{0,4},{4,0},{8,12},{12,8},{16,20},{20,16},{24,28},{28,24},{1,5},{5... | collective-permute-start | bytes 245768 | tf_op jit(solution)/shard_map/ppermute | solution.py:340
  1.2 0.1 collective-permute-start.1
  1.3 1.1 %shard_map.94 = (bf16[2,160,1024]{2,1,0:T(8,128)(2,1)S(1)}, f32[16,128]{1,0:T(8,128)S(1)}) custom-call(bf16[160,2048]{1,0:T(8,128)(2,1)} %refs_0_.5, bf16[160,2048]{1,0:T(8,128)(2,1)} %refs_1_.3, s32[1280]{0:T(1024)} %refs_2_.3), custom_call_target="tpu_custom_call" | custom-call | flops 1100000000 | bytes 1315840 | tf_op jit(solution)/shard_map/pallas_call | solution.py:35
  2.4 0.2 collective-permute-done.1.refs_3_
  2.7 0.3 collective-permute-start.2
  3.0 2.8 %collective-permute-start.5 = (bf16[640,128]{1,0:T(8,128)(2,1)S(1)}, bf16[640,128]{1,0:T(8,128)(2,1)S(1)}, u32[]{:S(2)}, u32[]{:S(2)}) collective-permute-start(bf16[640,128]{1,0:T(8,128)(2,1)S(1)} %shard_map.95.refs_5_.refs_7_.refs_3_.refs_4_), channel_id=1, source_target_pairs={{0,16},{4,20},{8,24},{12,28},{16,0},{20,4},{24,8},{28,12},{1,17},{... | collective-permute-start | bytes 491528 | tf_op jit(solution)/shard_map/ppermute | solution.py:340
  5.8 1.5 %collective-permute-start.4 = (bf16[640,128]{1,0:T(8,128)(2,1)S(1)}, bf16[640,128]{1,0:T(8,128)(2,1)S(1)}, u32[]{:S(2)}, u32[]{:S(2)}) collective-permute-start(bf16[640,128]{1,0:T(8,128)(2,1)S(1)} %shard_map.95.refs_5_.refs_7_.refs_3_.refs_4_), channel_id=1, source_target_pairs={{0,8},{4,12},{8,0},{12,4},{16,24},{20,28},{24,16},{28,20},{1,9},{5... | collective-permute-start | bytes 491528 | tf_op jit(solution)/shard_map/ppermute | solution.py:340
  7.3 0.9 %shard_map.96 = (f32[8,640]{1,0:T(8,128)S(1)}, f32[8,640]{1,0:T(8,128)S(1)}, bf16[4,640,128]{2,1,0:T(8,128)(2,1)S(1)}, bf16[4,128,640]{2,1,0:T(8,128)(2,1)S(1)},...) custom-call(bf16[160,2048]{1,0:T(8,128)(2,1)S(1)} %copy-done.2, ...), custom_call_target="tpu_custom_call" | custom-call | flops 1100000000 | bytes 2795520 | tf_op jit(solution)/shard_map/pallas_call | solution.py:35
  8.3 0.1 collective-permute-start.3
  8.4 1.4 %collective-permute-start.6 = (bf16[640,128]{1,0:T(8,128)(2,1)S(1)}, bf16[640,128]{1,0:T(8,128)(2,1)S(1)}, u32[]{:S(2)}, u32[]{:S(2)}) collective-permute-start(bf16[640,128]{1,0:T(8,128)(2,1)S(1)} %get-tuple-element.41), channel_id=1, source_target_pairs={{0,24},{4,28},{8,16},{12,20},{16,8},{20,12},{24,0},{28,4},{1,25},{... | collective-permute-start | bytes 491528 | tf_op jit(solution)/shard_map/ppermute | solution.py:340
  9.8 0.7 %collective-permute-done.5.refs_7_.refs_5_.refs_6_ = bf16[640,128]{1,0:T(8,128)(2,1)S(1)} collective-permute-done((bf16[640,128]{1,0:T(8,128)(2,1)S(1)}, bf16[640,128]{1,0:T(8,128)(2,1)S(1)}, u32[]{:S(2)}, u32[]{:S(2)}) %collective-permute-start.5) | collective-permute-done | bytes 163872 | tf_op jit(solution)/shard_map/ppermute | solution.py:340
  10.5 1.2 %shard_map.100.refs_8_ = bf16[640,128]{1,0:T(8,128)(2,1)S(1)} custom-call(f32[16,128]{1,0:T(8,128)S(1)} %get-tuple-element.32.refs_0_, bf16[4,640,128]{2,1,0:T(8,128)(2,1)S(1)} %get-tuple-element.37.refs_1_, bf16[4,640,128]{2,1,0:T(8,128)(2,1)S(1)} %get-tuple-element.39.refs_2_.refs_1_, bf16[4,128,640]{2,1,0:T(8,128)(2,1)S(1)} %get-tuple-element.42.refs_3_, ...), custom_call_target="tpu_custom_call" | custom-call | flops 550000000 | bytes 2834432 | tf_op jit(solution)/shard_map/pallas_call | solution.py:35
  11.7 0.7 %collective-permute-done.4.refs_7_.refs_4_.refs_5_ = bf16[640,128]{1,0:T(8,128)(2,1)S(1)} collective-permute-done((bf16[640,128]{1,0:T(8,128)(2,1)S(1)}, bf16[640,128]{1,0:T(8,128)(2,1)S(1)}, u32[]{:S(2)}, u32[]{:S(2)}) %collective-permute-start.4) | collective-permute-done | bytes 163872 | tf_op jit(solution)/shard_map/ppermute | solution.py:340
  12.4 1.2 %shard_map.101 = bf16[640,128]{1,0:T(8,128)(2,1)S(1)} custom-call(f32[16,128]{1,0:T(8,128)S(1)} %get-tuple-element.32.refs_0_, bf16[4,640,128]{2,1,0:T(8,128)(2,1)S(1)} %get-tuple-element.37.refs_1_, bf16[4,640,128]{2,1,0:T(8,128)(2,1)S(1)} %get-tuple-element.39.refs_2_.refs_1_, bf16[4,128,640]{2,1,0:T(8,128)(2,1)S(1)} %get-tuple-element.42.refs_3_, ...), custom_call_target="tpu_custom_call" | custom-call | flops 550000000 | bytes 2834432 | tf_op jit(solution)/shard_map/pallas_call | solution.py:35
  13.6 1.1 %collective-permute-start.7 = (bf16[640,128]{1,0:T(8,128)(2,1)S(1)}, bf16[640,128]{1,0:T(8,128)(2,1)S(1)}, u32[]{:S(2)}, u32[]{:S(2)}) collective-permute-start(bf16[640,128]{1,0:T(8,128)(2,1)S(1)} %shard_map.100.refs_8_), channel_id=1, source_target_pairs={{0,16},{4,20},{8,24},{12,28},{16,0},{20,4},{24,8},{28,12},{1,17},{... | collective-permute-start | bytes 491528 | tf_op jit(solution)/shard_map/ppermute | solution.py:340
  14.7 1.5 %collective-permute-start.8 = (bf16[640,128]{1,0:T(8,128)(2,1)S(1)}, bf16[640,128]{1,0:T(8,128)(2,1)S(1)}, u32[]{:S(2)}, u32[]{:S(2)}) collective-permute-start(bf16[640,128]{1,0:T(8,128)(2,1)S(1)} %shard_map.101), channel_id=1, source_target_pairs={{0,8},{4,12},{8,0},{12,4},{16,24},{20,28},{24,16},{28,20},{1,9},{5... | collective-permute-start | bytes 491528 | tf_op jit(solution)/shard_map/ppermute | solution.py:340
  16.1 0.7 %shard_map.97.refs_8_ = bf16[320,128]{1,0:T(8,128)(2,1)S(1)} custom-call(f32[16,128]{1,0:T(8,128)S(1)} %get-tuple-element.32.refs_0_, bf16[4,640,128]{2,1,0:T(8,128)(2,1)S(1)} %get-tuple-element.37.refs_1_, bf16[4,640,128]{2,1,0:T(8,128)(2,1)S(1)} %get-tuple-element.39.refs_2_.refs_1_, bf16[4,128,640]{2,1,0:T(8,128)(2,1)S(1)} %get-tuple-element.42.refs_3_, ...), custom_call_target="tpu_custom_call" | custom-call | flops 275000000 | bytes 2834432 | tf_op jit(solution)/shard_map/pallas_call | solution.py:35
  16.8 0.8 %collective-permute-start.11 = (bf16[320,128]{1,0:T(8,128)(2,1)S(1)}, bf16[320,128]{1,0:T(8,128)(2,1)S(1)}, u32[]{:S(2)}, u32[]{:S(2)}) collective-permute-start(bf16[320,128]{1,0:T(8,128)(2,1)S(1)} %shard_map.97.refs_8_), channel_id=1, source_target_pairs={{0,28},{4,24},{8,20},{12,16},{16,12},{20,8},{24,4},{28,0},{1,29},{... | collective-permute-start | bytes 245768 | tf_op jit(solution)/shard_map/ppermute | solution.py:340
  17.6 0.7 %shard_map.98.refs_8_ = bf16[320,128]{1,0:T(8,128)(2,1)S(1)} custom-call(f32[16,128]{1,0:T(8,128)S(1)} %get-tuple-element.32.refs_0_, bf16[4,640,128]{2,1,0:T(8,128)(2,1)S(1)} %get-tuple-element.37.refs_1_, bf16[4,640,128]{2,1,0:T(8,128)(2,1)S(1)} %get-tuple-element.39.refs_2_.refs_1_, bf16[4,128,640]{2,1,0:T(8,128)(2,1)S(1)} %get-tuple-element.42.refs_3_, ...), custom_call_target="tpu_custom_call" | custom-call | flops 275000000 | bytes 2834432 | tf_op jit(solution)/shard_map/pallas_call | solution.py:35
  18.3 1.3 %collective-permute-start.9 = (bf16[320,128]{1,0:T(8,128)(2,1)S(1)}, bf16[320,128]{1,0:T(8,128)(2,1)S(1)}, u32[]{:S(2)}, u32[]{:S(2)}) collective-permute-start(bf16[320,128]{1,0:T(8,128)(2,1)S(1)} %shard_map.98.refs_8_), channel_id=1, source_target_pairs={{0,24},{4,28},{8,16},{12,20},{16,8},{20,12},{24,0},{28,4},{1,25},{... | collective-permute-start | bytes 245768 | tf_op jit(solution)/shard_map/ppermute | solution.py:340
  19.6 1.4 %shard_map.99 = (f32[320,128]{1,0:T(8,128)S(1)}, f32[320,128]{1,0:T(8,128)S(1)}) custom-call(f32[16,128]{1,0:T(8,128)S(1)} %get-tuple-element.32.refs_0_, bf16[4,640,128]{2,1,0:T(8,128)(2,1)S(1)} %get-tuple-element.37.refs_1_, bf16[4,640,128]{2,1,0:T(8,128)(2,1)S(1)} %get-tuple-element.39.refs_2_.refs_1_, ...), custom_call_target="tpu_custom_call" | custom-call | flops 550000000 | bytes 2834432 | tf_op jit(solution)/shard_map/pallas_call | solution.py:35
  21.1 0.9 %collective-permute-start.10 = (f32[320,128]{1,0:T(8,128)S(1)}, f32[320,128]{1,0:T(8,128)S(1)}, u32[]{:S(2)}, u32[]{:S(2)}) collective-permute-start(f32[320,128]{1,0:T(8,128)S(1)} %get-tuple-element.49), channel_id=1, source_target_pairs={{0,4},{4,0},{8,12},{12,8},{16,20},{20,16},{24,28},{28,24},{1,5},{5... | collective-permute-start | bytes 491528 | tf_op jit(solution)/shard_map/ppermute | solution.py:340
  22.0 2.3 %shard_map.103 = bf16[2,640,128]{2,1,0:T(8,128)(2,1)S(1)} custom-call(f32[16,128]{1,0:T(8,128)S(1)} %get-tuple-element.32.refs_0_, bf16[4,640,128]{2,1,0:T(8,128)(2,1)S(1)} %get-tuple-element.39.refs_2_.refs_1_, f32[8,640]{1,0:T(8,128)S(1)} %collective-permute-done.3.refs_6_.refs_2_, bf16[640,128]{1,0:T(8,128)(2,1)S(1)} %shard_map.95.refs_5_.refs_7_.refs_3_.refs_4_, ...), custom_call_target="tpu_custom_call" | custom-call | flops 2750000128 | bytes 1339392 | tf_op jit(solution)/shard_map/pallas_call | solution.py:35
  24.4 0.1 collective-permute-done.9.refs_1_
  24.5 0.1 shard_map.104
  24.5 0.2 collective-permute-start.12
  24.7 2.6 %collective-permute-start.13 = (bf16[2,40,256]{2,1,0:T(8,128)(2,1)S(1)}, bf16[2,40,256]{2,1,0:T(8,128)(2,1)S(1)}, u32[]{:S(2)}, u32[]{:S(2)}) collective-permute-start(bf16[2,40,256]{2,1,0:T(8,128)(2,1)S(1)} %get-tuple-element.56), channel_id=1, source_target_pairs={{0,2},{1,3},{2,0},{3,1},{4,6},{5,7},{6,4},{7,5},{8,10},{9,11},{10,... | collective-permute-start | bytes 122888 | tf_op jit(solution)/shard_map/ppermute | solution.py:340
  27.3 1.3 %collective-permute-start.14 = (bf16[2,40,256]{2,1,0:T(8,128)(2,1)S(1)}, bf16[2,40,256]{2,1,0:T(8,128)(2,1)S(1)}, u32[]{:S(2)}, u32[]{:S(2)}) collective-permute-start(bf16[2,40,256]{2,1,0:T(8,128)(2,1)S(1)} %get-tuple-element.57), channel_id=1, source_target_pairs={{0,3},{1,2},{2,1},{3,0},{4,7},{5,6},{6,5},{7,4},{8,11},{9,10},{10,... | collective-permute-start | bytes 122888 | tf_op jit(solution)/shard_map/ppermute | solution.py:340
  28.7 0.2 collective-permute-start.15
  28.9 3.3 %shard_map.105.refs_4_ = bf16[160,2048]{1,0:T(8,128)(2,1)} custom-call(f32[16,128]{1,0:T(8,128)S(1)} %get-tuple-element.32.refs_0_, bf16[4,640,128]{2,1,0:T(8,128)(2,1)S(1)} %get-tuple-element.37.refs_1_, f32[8,640]{1,0:T(8,128)S(1)} %get-tuple-element.38.refs_5_.refs_2_, bf16[2,640,128]{2,1,0:T(8,128)(2,1)S(1)} %collective-permute-done.12.refs_3_, ...), custom_call_target="tpu_custom_call" | custom-call | flops 3300000000 | bytes 1667072 | tf_op jit(solution)/shard_map/pallas_call | solution.py:35
  32.2 0.9 %collective-permute-done.14.refs_2_ = bf16[2,40,256]{2,1,0:T(8,128)(2,1)S(1)} collective-permute-done((bf16[2,40,256]{2,1,0:T(8,128)(2,1)S(1)}, bf16[2,40,256]{2,1,0:T(8,128)(2,1)S(1)}, u32[]{:S(2)}, u32[]{:S(2)}) %collective-permute-start.14) | collective-permute-done | bytes 40992 | tf_op jit(solution)/shard_map/ppermute | solution.py:340
  33.2 0.7 %shard_map.106 = (bf16[40,1024]{1,0:T(8,128)(2,1)}, bf16[40,1024]{1,0:T(8,128)(2,1)}) custom-call(bf16[2,40,256]{2,1,0:T(8,128)(2,1)S(1)} %get-tuple-element.55.refs_8_.refs_0_, bf16[2,40,256]{2,1,0:T(8,128)(2,1)S(1)} %collective-permute-done.13.refs_1_, bf16[2,40,256]{2,1,0:T(8,128)(2,1)S(1)} %collective-permute-done.14.refs_2_, ...), custom_call_target="tpu_custom_call" | custom-call | flops 110000000 | bytes 163840 | tf_op jit(solution)/shard_map/pallas_call | solution.py:35
  (25 shorter events, 0.1 us)
Async XLA Ops:
  0.6 2.3 %copy-start = (bf16[160,256]{1,0:T(8,128)(2,1)S(1)}, bf16[160,256]{1,0:T(8,128)(2,1)}, u32[]{:S(2)}) copy-start(bf16[160,256]{1,0:T(8,128)(2,1)} %refs_0_.4) | copy-start | bytes 245764
  0.6 2.3 %copy-start.1 = (bf16[160,256]{1,0:T(8,128)(2,1)S(1)}, bf16[160,256]{1,0:T(8,128)(2,1)}, u32[]{:S(2)}) copy-start(bf16[160,256]{1,0:T(8,128)(2,1)} %refs_2_.4) | copy-start | bytes 245764
  0.7 6.7 %copy-start.2 = (bf16[160,2048]{1,0:T(8,128)(2,1)S(1)}, bf16[160,2048]{1,0:T(8,128)(2,1)}, u32[]{:S(2)}) copy-start(bf16[160,2048]{1,0:T(8,128)(2,1)} %refs_0_.5) | copy-start | bytes 1966084
  0.7 6.7 %copy-start.3 = (bf16[160,2048]{1,0:T(8,128)(2,1)S(1)}, bf16[160,2048]{1,0:T(8,128)(2,1)}, u32[]{:S(2)}) copy-start(bf16[160,2048]{1,0:T(8,128)(2,1)} %refs_1_.3) | copy-start | bytes 1966084
  0.7 6.7 %copy-start.4 = (bf16[160,2048]{1,0:T(8,128)(2,1)S(1)}, bf16[160,2048]{1,0:T(8,128)(2,1)}, u32[]{:S(2)}) copy-start(bf16[160,2048]{1,0:T(8,128)(2,1)} %refs_2_.5) | copy-start | bytes 1966084
  0.7 1.8 %collective-permute-start = (bf16[160,256]{1,0:T(8,128)(2,1)}, bf16[160,256]{1,0:T(8,128)(2,1)S(1)}, u32[]{:S(2)}, u32[]{:S(2)}) collective-permute-start(bf16[160,256]{1,0:T(8,128)(2,1)} %refs_0_.4), channel_id=1, source_target_pairs={{0,4},{4,0},{8,12},{12,8},{16,20},{20,16},{24,28},{28,24},{1,5},{5... | collective-permute-start | bytes 245768 | tf_op jit(solution)/shard_map/ppermute | solution.py:340
  1.2 1.5 %collective-permute-start.1 = (bf16[160,256]{1,0:T(8,128)(2,1)}, bf16[160,256]{1,0:T(8,128)(2,1)S(1)}, u32[]{:S(2)}, u32[]{:S(2)}) collective-permute-start(bf16[160,256]{1,0:T(8,128)(2,1)} %refs_2_.4), channel_id=1, source_target_pairs={{0,4},{4,0},{8,12},{12,8},{16,20},{20,16},{24,28},{28,24},{1,5},{5... | collective-permute-start | bytes 245768 | tf_op jit(solution)/shard_map/ppermute | solution.py:340
  2.7 4.6 %copy-start.5 = (f32[160,16]{0,1:T(8,128)S(1)}, f32[160,16]{0,1:T(8,128)}, u32[]{:S(2)}) copy-start(f32[160,16]{0,1:T(8,128)} %param.13) | copy-start | bytes 30724
  2.7 4.6 %collective-permute-start.2 = (bf16[2,160,1024]{2,1,0:T(8,128)(2,1)S(1)}, bf16[2,160,1024]{2,1,0:T(8,128)(2,1)S(1)}, u32[]{:S(2)}, u32[]{:S(2)}) collective-permute-start(bf16[2,160,1024]{2,1,0:T(8,128)(2,1)S(1)} %get-tuple-element.34), channel_id=1, source_target_pairs={{0,4},{4,0},{8,12},{12,8},{16,20},{20,16},{24,28},{28,24},{1,5},{5... | collective-permute-start | bytes 1966088 | tf_op jit(solution)/shard_map/ppermute | solution.py:340
  3.0 7.5 %collective-permute-start.5 = (bf16[640,128]{1,0:T(8,128)(2,1)S(1)}, bf16[640,128]{1,0:T(8,128)(2,1)S(1)}, u32[]{:S(2)}, u32[]{:S(2)}) collective-permute-start(bf16[640,128]{1,0:T(8,128)(2,1)S(1)} %shard_map.95.refs_5_.refs_7_.refs_3_.refs_4_), channel_id=1, source_target_pairs={{0,16},{4,20},{8,24},{12,28},{16,0},{20,4},{24,8},{28,12},{1,17},{... | collective-permute-start | bytes 491528 | tf_op jit(solution)/shard_map/ppermute | solution.py:340
  5.8 6.6 %collective-permute-start.4 = (bf16[640,128]{1,0:T(8,128)(2,1)S(1)}, bf16[640,128]{1,0:T(8,128)(2,1)S(1)}, u32[]{:S(2)}, u32[]{:S(2)}) collective-permute-start(bf16[640,128]{1,0:T(8,128)(2,1)S(1)} %shard_map.95.refs_5_.refs_7_.refs_3_.refs_4_), channel_id=1, source_target_pairs={{0,8},{4,12},{8,0},{12,4},{16,24},{20,28},{24,16},{28,20},{1,9},{5... | collective-permute-start | bytes 491528 | tf_op jit(solution)/shard_map/ppermute | solution.py:340
  8.3 2.2 %collective-permute-start.3 = (f32[8,640]{1,0:T(8,128)S(1)}, f32[8,640]{1,0:T(8,128)S(1)}, u32[]{:S(2)}, u32[]{:S(2)}) collective-permute-start(f32[8,640]{1,0:T(8,128)S(1)} %get-tuple-element.40), channel_id=1, source_target_pairs={{0,4},{4,0},{8,12},{12,8},{16,20},{20,16},{24,28},{28,24},{1,5},{5... | collective-permute-start | bytes 61448 | tf_op jit(solution)/shard_map/ppermute | solution.py:340
  8.4 7.8 %collective-permute-start.6 = (bf16[640,128]{1,0:T(8,128)(2,1)S(1)}, bf16[640,128]{1,0:T(8,128)(2,1)S(1)}, u32[]{:S(2)}, u32[]{:S(2)}) collective-permute-start(bf16[640,128]{1,0:T(8,128)(2,1)S(1)} %get-tuple-element.41), channel_id=1, source_target_pairs={{0,24},{4,28},{8,16},{12,20},{16,8},{20,12},{24,0},{28,4},{1,25},{... | collective-permute-start | bytes 491528 | tf_op jit(solution)/shard_map/ppermute | solution.py:340
  13.6 7.5 %collective-permute-start.7 = (bf16[640,128]{1,0:T(8,128)(2,1)S(1)}, bf16[640,128]{1,0:T(8,128)(2,1)S(1)}, u32[]{:S(2)}, u32[]{:S(2)}) collective-permute-start(bf16[640,128]{1,0:T(8,128)(2,1)S(1)} %shard_map.100.refs_8_), channel_id=1, source_target_pairs={{0,16},{4,20},{8,24},{12,28},{16,0},{20,4},{24,8},{28,12},{1,17},{... | collective-permute-start | bytes 491528 | tf_op jit(solution)/shard_map/ppermute | solution.py:340
  14.7 6.4 %collective-permute-start.8 = (bf16[640,128]{1,0:T(8,128)(2,1)S(1)}, bf16[640,128]{1,0:T(8,128)(2,1)S(1)}, u32[]{:S(2)}, u32[]{:S(2)}) collective-permute-start(bf16[640,128]{1,0:T(8,128)(2,1)S(1)} %shard_map.101), channel_id=1, source_target_pairs={{0,8},{4,12},{8,0},{12,4},{16,24},{20,28},{24,16},{28,20},{1,9},{5... | collective-permute-start | bytes 491528 | tf_op jit(solution)/shard_map/ppermute | solution.py:340
  16.8 7.6 %collective-permute-start.11 = (bf16[320,128]{1,0:T(8,128)(2,1)S(1)}, bf16[320,128]{1,0:T(8,128)(2,1)S(1)}, u32[]{:S(2)}, u32[]{:S(2)}) collective-permute-start(bf16[320,128]{1,0:T(8,128)(2,1)S(1)} %shard_map.97.refs_8_), channel_id=1, source_target_pairs={{0,28},{4,24},{8,20},{12,16},{16,12},{20,8},{24,4},{28,0},{1,29},{... | collective-permute-start | bytes 245768 | tf_op jit(solution)/shard_map/ppermute | solution.py:340
  18.3 6.1 %collective-permute-start.9 = (bf16[320,128]{1,0:T(8,128)(2,1)S(1)}, bf16[320,128]{1,0:T(8,128)(2,1)S(1)}, u32[]{:S(2)}, u32[]{:S(2)}) collective-permute-start(bf16[320,128]{1,0:T(8,128)(2,1)S(1)} %shard_map.98.refs_8_), channel_id=1, source_target_pairs={{0,24},{4,28},{8,16},{12,20},{16,8},{20,12},{24,0},{28,4},{1,25},{... | collective-permute-start | bytes 245768 | tf_op jit(solution)/shard_map/ppermute | solution.py:340
  21.1 3.3 %collective-permute-start.10 = (f32[320,128]{1,0:T(8,128)S(1)}, f32[320,128]{1,0:T(8,128)S(1)}, u32[]{:S(2)}, u32[]{:S(2)}) collective-permute-start(f32[320,128]{1,0:T(8,128)S(1)} %get-tuple-element.49), channel_id=1, source_target_pairs={{0,4},{4,0},{8,12},{12,8},{16,20},{20,16},{24,28},{28,24},{1,5},{5... | collective-permute-start | bytes 491528 | tf_op jit(solution)/shard_map/ppermute | solution.py:340
  24.5 4.4 %collective-permute-start.12 = (bf16[2,640,128]{2,1,0:T(8,128)(2,1)S(1)}, bf16[2,640,128]{2,1,0:T(8,128)(2,1)S(1)}, u32[]{:S(2)}, u32[]{:S(2)}) collective-permute-start(bf16[2,640,128]{2,1,0:T(8,128)(2,1)S(1)} %shard_map.103), channel_id=1, source_target_pairs={{0,4},{4,0},{8,12},{12,8},{16,20},{20,16},{24,28},{28,24},{1,5},{5... | collective-permute-start | bytes 983048 | tf_op jit(solution)/shard_map/ppermute | solution.py:340
  24.7 7.5 %collective-permute-start.13 = (bf16[2,40,256]{2,1,0:T(8,128)(2,1)S(1)}, bf16[2,40,256]{2,1,0:T(8,128)(2,1)S(1)}, u32[]{:S(2)}, u32[]{:S(2)}) collective-permute-start(bf16[2,40,256]{2,1,0:T(8,128)(2,1)S(1)} %get-tuple-element.56), channel_id=1, source_target_pairs={{0,2},{1,3},{2,0},{3,1},{4,6},{5,7},{6,4},{7,5},{8,10},{9,11},{10,... | collective-permute-start | bytes 122888 | tf_op jit(solution)/shard_map/ppermute | solution.py:340
  27.3 5.8 %collective-permute-start.14 = (bf16[2,40,256]{2,1,0:T(8,128)(2,1)S(1)}, bf16[2,40,256]{2,1,0:T(8,128)(2,1)S(1)}, u32[]{:S(2)}, u32[]{:S(2)}) collective-permute-start(bf16[2,40,256]{2,1,0:T(8,128)(2,1)S(1)} %get-tuple-element.57), channel_id=1, source_target_pairs={{0,3},{1,2},{2,1},{3,0},{4,7},{5,6},{6,5},{7,4},{8,11},{9,10},{10,... | collective-permute-start | bytes 122888 | tf_op jit(solution)/shard_map/ppermute | solution.py:340
  28.7 4.5 %collective-permute-start.15 = (bf16[2,40,256]{2,1,0:T(8,128)(2,1)S(1)}, bf16[2,40,256]{2,1,0:T(8,128)(2,1)S(1)}, u32[]{:S(2)}, u32[]{:S(2)}) collective-permute-start(bf16[2,40,256]{2,1,0:T(8,128)(2,1)S(1)} %get-tuple-element.58), channel_id=1, source_target_pairs={{0,1},{1,0},{2,3},{3,2},{4,5},{5,4},{6,7},{7,6},{8,9},{9,8},{10,11... | collective-permute-start | bytes 122888 | tf_op jit(solution)/shard_map/ppermute | solution.py:340

commit v8 on v7

--- a/solution.py
+++ b/solution.py
@@ -395,9 +395,9 @@
     crossing = kv_grads(late, [half_piece], (1,))
     diagonal = kv_grads(late, [half_piece], (0,), crossing) + crossing
     local = kv_grads(0, [(half_piece[0], F32)] * 2, after=diagonal[:1])
-    flat = lax.optimization_barrier(tuple(partials[pair][0] for pair in (2, 1)))
-    flat = dict(zip((2, 1), flat))
-    received = [swap(flat[pair], "ctx", 2 * pair) for pair in (2, 1)]
+    back = list(reversed(range(1, late)))
+    sent = lax.optimization_barrier(tuple(partials[pair][0] for pair in back))
+    received = [swap(x, "ctx", 2 * pair) for pair, x in zip(back, sent)]
     last = [swap(x, "ctx", 2 * late + a) for a, x in enumerate(diagonal)]
 
     sums = ((2 * tokens, HEAD_SIZE), F32)

time: 34 us -> 34 us (level)
  transfers between devices with their start and end apart: 16 -> 16, of which waited for: 5 -> 4; matrix products, arithmetic and copies ran while one was open for 0% -> 0% of each run, Pallas kernels for 39% -> 38%
where the time goes in v8:
time: 34 us; the launch traced here: 33.8 us
  starting transfers between devices  16.6 us (49%)
  Pallas kernels  13.8 us (41%)
  waiting for transfers between devices  2.65 us (8%)
  between operations  0.81 us (2%)
    ppermute x16, starting transfers between devices, swap(): return lax.ppermute(x, axis, [(i, i ^ shift) for i in range(count)])  16.6 us
    pallas_call x13, Pallas kernels, call(): pl.pallas_call(body, cost_estimate=pl.CostEstimate(flops=int(cost * FLOPS...  13.8 us
    ppermute x16, waiting for transfers between devices, swap(): return lax.ppermute(x, axis, [(i, i ^ shift) for i in range(count)])  2.65 us
  transfers between devices with their start and end apart: 16, of which 4 were waited for; matrix products, arithmetic and copies ran while one was open for 0% of the time, Pallas kernels for 38%

profile of v8, /device:TPU:0, one launch (start us, length us, event | category | flops | bytes accessed | tf_op | source)
XLA Modules:
  0.0 33.8 jit_solution(845696240908224116)
XLA Ops:
  0.7 0.5 %collective-permute-start = (bf16[160,256]{1,0:T(8,128)(2,1)}, bf16[160,256]{1,0:T(8,128)(2,1)S(1)}, u32[]{:S(2)}, u32[]{:S(2)}) collective-permute-start(bf16[160,256]{1,0:T(8,128)(2,1)} %refs_0_.4), channel_id=1, source_target_pairs={{0,4},{4,0},{8,12},{12,8},{16,20},{20,16},{24,28},{28,24},{1,5},{5... | collective-permute-start | bytes 245768 | tf_op jit(solution)/shard_map/ppermute | solution.py:340
  1.2 0.1 collective-permute-start.1
  1.3 1.1 %shard_map.94 = (bf16[2,160,1024]{2,1,0:T(8,128)(2,1)S(1)}, f32[16,128]{1,0:T(8,128)S(1)}) custom-call(bf16[160,2048]{1,0:T(8,128)(2,1)} %refs_0_.5, bf16[160,2048]{1,0:T(8,128)(2,1)} %refs_1_.3, s32[1280]{0:T(1024)} %refs_2_.3), custom_call_target="tpu_custom_call" | custom-call | flops 1100000000 | bytes 1315840 | tf_op jit(solution)/shard_map/pallas_call | solution.py:35
  2.4 0.2 collective-permute-done.1.refs_3_
  2.7 0.3 collective-permute-start.2
  3.0 2.8 %collective-permute-start.5 = (bf16[640,128]{1,0:T(8,128)(2,1)S(1)}, bf16[640,128]{1,0:T(8,128)(2,1)S(1)}, u32[]{:S(2)}, u32[]{:S(2)}) collective-permute-start(bf16[640,128]{1,0:T(8,128)(2,1)S(1)} %shard_map.95.refs_5_.refs_7_.refs_3_.refs_4_), channel_id=1, source_target_pairs={{0,16},{4,20},{8,24},{12,28},{16,0},{20,4},{24,8},{28,12},{1,17},{... | collective-permute-start | bytes 491528 | tf_op jit(solution)/shard_map/ppermute | solution.py:340
  5.8 1.5 %collective-permute-start.4 = (bf16[640,128]{1,0:T(8,128)(2,1)S(1)}, bf16[640,128]{1,0:T(8,128)(2,1)S(1)}, u32[]{:S(2)}, u32[]{:S(2)}) collective-permute-start(bf16[640,128]{1,0:T(8,128)(2,1)S(1)} %shard_map.95.refs_5_.refs_7_.refs_3_.refs_4_), channel_id=1, source_target_pairs={{0,8},{4,12},{8,0},{12,4},{16,24},{20,28},{24,16},{28,20},{1,9},{5... | collective-permute-start | bytes 491528 | tf_op jit(solution)/shard_map/ppermute | solution.py:340
  7.3 0.9 %shard_map.96 = (f32[8,640]{1,0:T(8,128)S(1)}, f32[8,640]{1,0:T(8,128)S(1)}, bf16[4,640,128]{2,1,0:T(8,128)(2,1)S(1)}, bf16[4,128,640]{2,1,0:T(8,128)(2,1)S(1)},...) custom-call(bf16[160,2048]{1,0:T(8,128)(2,1)S(1)} %copy-done.2, ...), custom_call_target="tpu_custom_call" | custom-call | flops 1100000000 | bytes 2795520 | tf_op jit(solution)/shard_map/pallas_call | solution.py:35
  8.3 0.1 collective-permute-start.3
  8.4 1.4 %collective-permute-start.6 = (bf16[640,128]{1,0:T(8,128)(2,1)S(1)}, bf16[640,128]{1,0:T(8,128)(2,1)S(1)}, u32[]{:S(2)}, u32[]{:S(2)}) collective-permute-start(bf16[640,128]{1,0:T(8,128)(2,1)S(1)} %get-tuple-element.41), channel_id=1, source_target_pairs={{0,24},{4,28},{8,16},{12,20},{16,8},{20,12},{24,0},{28,4},{1,25},{... | collective-permute-start | bytes 491528 | tf_op jit(solution)/shard_map/ppermute | solution.py:340
  9.8 0.7 %collective-permute-done.5.refs_7_.refs_5_.refs_6_ = bf16[640,128]{1,0:T(8,128)(2,1)S(1)} collective-permute-done((bf16[640,128]{1,0:T(8,128)(2,1)S(1)}, bf16[640,128]{1,0:T(8,128)(2,1)S(1)}, u32[]{:S(2)}, u32[]{:S(2)}) %collective-permute-start.5) | collective-permute-done | bytes 163872 | tf_op jit(solution)/shard_map/ppermute | solution.py:340
  10.5 1.2 %shard_map.100.refs_8_ = bf16[640,128]{1,0:T(8,128)(2,1)S(1)} custom-call(f32[16,128]{1,0:T(8,128)S(1)} %get-tuple-element.32.refs_0_, bf16[4,640,128]{2,1,0:T(8,128)(2,1)S(1)} %get-tuple-element.37.refs_1_, bf16[4,640,128]{2,1,0:T(8,128)(2,1)S(1)} %get-tuple-element.39.refs_2_.refs_1_, bf16[4,128,640]{2,1,0:T(8,128)(2,1)S(1)} %get-tuple-element.42.refs_3_, ...), custom_call_target="tpu_custom_call" | custom-call | flops 550000000 | bytes 2834432 | tf_op jit(solution)/shard_map/pallas_call | solution.py:35
  11.6 0.7 %collective-permute-done.4.refs_7_.refs_4_.refs_5_ = bf16[640,128]{1,0:T(8,128)(2,1)S(1)} collective-permute-done((bf16[640,128]{1,0:T(8,128)(2,1)S(1)}, bf16[640,128]{1,0:T(8,128)(2,1)S(1)}, u32[]{:S(2)}, u32[]{:S(2)}) %collective-permute-start.4) | collective-permute-done | bytes 163872 | tf_op jit(solution)/shard_map/ppermute | solution.py:340
  12.4 1.2 %shard_map.101 = bf16[640,128]{1,0:T(8,128)(2,1)S(1)} custom-call(f32[16,128]{1,0:T(8,128)S(1)} %get-tuple-element.32.refs_0_, bf16[4,640,128]{2,1,0:T(8,128)(2,1)S(1)} %get-tuple-element.37.refs_1_, bf16[4,640,128]{2,1,0:T(8,128)(2,1)S(1)} %get-tuple-element.39.refs_2_.refs_1_, bf16[4,128,640]{2,1,0:T(8,128)(2,1)S(1)} %get-tuple-element.42.refs_3_, ...), custom_call_target="tpu_custom_call" | custom-call | flops 550000000 | bytes 2834432 | tf_op jit(solution)/shard_map/pallas_call | solution.py:35
  13.6 1.1 %collective-permute-start.7 = (bf16[640,128]{1,0:T(8,128)(2,1)S(1)}, bf16[640,128]{1,0:T(8,128)(2,1)S(1)}, u32[]{:S(2)}, u32[]{:S(2)}) collective-permute-start(bf16[640,128]{1,0:T(8,128)(2,1)S(1)} %shard_map.100.refs_8_), channel_id=1, source_target_pairs={{0,16},{4,20},{8,24},{12,28},{16,0},{20,4},{24,8},{28,12},{1,17},{... | collective-permute-start | bytes 491528 | tf_op jit(solution)/shard_map/ppermute | solution.py:340
  14.7 1.5 %collective-permute-start.8 = (bf16[640,128]{1,0:T(8,128)(2,1)S(1)}, bf16[640,128]{1,0:T(8,128)(2,1)S(1)}, u32[]{:S(2)}, u32[]{:S(2)}) collective-permute-start(bf16[640,128]{1,0:T(8,128)(2,1)S(1)} %shard_map.101), channel_id=1, source_target_pairs={{0,8},{4,12},{8,0},{12,4},{16,24},{20,28},{24,16},{28,20},{1,9},{5... | collective-permute-start | bytes 491528 | tf_op jit(solution)/shard_map/ppermute | solution.py:340
  16.2 0.7 %shard_map.97.refs_8_ = bf16[320,128]{1,0:T(8,128)(2,1)S(1)} custom-call(f32[16,128]{1,0:T(8,128)S(1)} %get-tuple-element.32.refs_0_, bf16[4,640,128]{2,1,0:T(8,128)(2,1)S(1)} %get-tuple-element.37.refs_1_, bf16[4,640,128]{2,1,0:T(8,128)(2,1)S(1)} %get-tuple-element.39.refs_2_.refs_1_, bf16[4,128,640]{2,1,0:T(8,128)(2,1)S(1)} %get-tuple-element.42.refs_3_, ...), custom_call_target="tpu_custom_call" | custom-call | flops 275000000 | bytes 2834432 | tf_op jit(solution)/shard_map/pallas_call | solution.py:35
  16.9 0.7 %collective-permute-start.11 = (bf16[320,128]{1,0:T(8,128)(2,1)S(1)}, bf16[320,128]{1,0:T(8,128)(2,1)S(1)}, u32[]{:S(2)}, u32[]{:S(2)}) collective-permute-start(bf16[320,128]{1,0:T(8,128)(2,1)S(1)} %shard_map.97.refs_8_), channel_id=1, source_target_pairs={{0,28},{4,24},{8,20},{12,16},{16,12},{20,8},{24,4},{28,0},{1,29},{... | collective-permute-start | bytes 245768 | tf_op jit(solution)/shard_map/ppermute | solution.py:340
  17.6 0.7 %shard_map.98.refs_8_ = bf16[320,128]{1,0:T(8,128)(2,1)S(1)} custom-call(f32[16,128]{1,0:T(8,128)S(1)} %get-tuple-element.32.refs_0_, bf16[4,640,128]{2,1,0:T(8,128)(2,1)S(1)} %get-tuple-element.37.refs_1_, bf16[4,640,128]{2,1,0:T(8,128)(2,1)S(1)} %get-tuple-element.39.refs_2_.refs_1_, bf16[4,128,640]{2,1,0:T(8,128)(2,1)S(1)} %get-tuple-element.42.refs_3_, ...), custom_call_target="tpu_custom_call" | custom-call | flops 275000000 | bytes 2834432 | tf_op jit(solution)/shard_map/pallas_call | solution.py:35
  18.3 1.3 %collective-permute-start.9 = (bf16[320,128]{1,0:T(8,128)(2,1)S(1)}, bf16[320,128]{1,0:T(8,128)(2,1)S(1)}, u32[]{:S(2)}, u32[]{:S(2)}) collective-permute-start(bf16[320,128]{1,0:T(8,128)(2,1)S(1)} %shard_map.98.refs_8_), channel_id=1, source_target_pairs={{0,24},{4,28},{8,16},{12,20},{16,8},{20,12},{24,0},{28,4},{1,25},{... | collective-permute-start | bytes 245768 | tf_op jit(solution)/shard_map/ppermute | solution.py:340
  19.6 1.4 %shard_map.99 = (f32[320,128]{1,0:T(8,128)S(1)}, f32[320,128]{1,0:T(8,128)S(1)}) custom-call(f32[16,128]{1,0:T(8,128)S(1)} %get-tuple-element.32.refs_0_, bf16[4,640,128]{2,1,0:T(8,128)(2,1)S(1)} %get-tuple-element.37.refs_1_, bf16[4,640,128]{2,1,0:T(8,128)(2,1)S(1)} %get-tuple-element.39.refs_2_.refs_1_, ...), custom_call_target="tpu_custom_call" | custom-call | flops 550000000 | bytes 2834432 | tf_op jit(solution)/shard_map/pallas_call | solution.py:35
  21.1 0.1 shard_map.102
  21.1 0.9 %collective-permute-start.10 = (f32[320,128]{1,0:T(8,128)S(1)}, f32[320,128]{1,0:T(8,128)S(1)}, u32[]{:S(2)}, u32[]{:S(2)}) collective-permute-start(f32[320,128]{1,0:T(8,128)S(1)} %get-tuple-element.49), channel_id=1, source_target_pairs={{0,4},{4,0},{8,12},{12,8},{16,20},{20,16},{24,28},{28,24},{1,5},{5... | collective-permute-start | bytes 491528 | tf_op jit(solution)/shard_map/ppermute | solution.py:340
  22.1 2.3 %shard_map.103 = bf16[2,640,128]{2,1,0:T(8,128)(2,1)S(1)} custom-call(f32[16,128]{1,0:T(8,128)S(1)} %get-tuple-element.32.refs_0_, bf16[4,640,128]{2,1,0:T(8,128)(2,1)S(1)} %get-tuple-element.39.refs_2_.refs_1_, f32[8,640]{1,0:T(8,128)S(1)} %collective-permute-done.3.refs_6_.refs_2_, bf16[640,128]{1,0:T(8,128)(2,1)S(1)} %shard_map.95.refs_5_.refs_7_.refs_3_.refs_4_, ...), custom_call_target="tpu_custom_call" | custom-call | flops 2750000128 | bytes 1339392 | tf_op jit(solution)/shard_map/pallas_call | solution.py:35
  24.4 0.1 shard_map.104
  24.5 0.2 collective-permute-start.12
  24.7 2.6 %collective-permute-start.13 = (bf16[2,40,256]{2,1,0:T(8,128)(2,1)S(1)}, bf16[2,40,256]{2,1,0:T(8,128)(2,1)S(1)}, u32[]{:S(2)}, u32[]{:S(2)}) collective-permute-start(bf16[2,40,256]{2,1,0:T(8,128)(2,1)S(1)} %get-tuple-element.56), channel_id=1, source_target_pairs={{0,2},{1,3},{2,0},{3,1},{4,6},{5,7},{6,4},{7,5},{8,10},{9,11},{10,... | collective-permute-start | bytes 122888 | tf_op jit(solution)/shard_map/ppermute | solution.py:340
  27.3 1.3 %collective-permute-start.14 = (bf16[2,40,256]{2,1,0:T(8,128)(2,1)S(1)}, bf16[2,40,256]{2,1,0:T(8,128)(2,1)S(1)}, u32[]{:S(2)}, u32[]{:S(2)}) collective-permute-start(bf16[2,40,256]{2,1,0:T(8,128)(2,1)S(1)} %get-tuple-element.57), channel_id=1, source_target_pairs={{0,3},{1,2},{2,1},{3,0},{4,7},{5,6},{6,5},{7,4},{8,11},{9,10},{10,... | collective-permute-start | bytes 122888 | tf_op jit(solution)/shard_map/ppermute | solution.py:340
  28.7 0.2 collective-permute-start.15
  28.9 3.3 %shard_map.105.refs_4_ = bf16[160,2048]{1,0:T(8,128)(2,1)} custom-call(f32[16,128]{1,0:T(8,128)S(1)} %get-tuple-element.32.refs_0_, bf16[4,640,128]{2,1,0:T(8,128)(2,1)S(1)} %get-tuple-element.37.refs_1_, f32[8,640]{1,0:T(8,128)S(1)} %get-tuple-element.38.refs_5_.refs_2_, bf16[2,640,128]{2,1,0:T(8,128)(2,1)S(1)} %collective-permute-done.12.refs_3_, ...), custom_call_target="tpu_custom_call" | custom-call | flops 3300000000 | bytes 1667072 | tf_op jit(solution)/shard_map/pallas_call | solution.py:35
  32.3 0.9 %collective-permute-done.14.refs_2_ = bf16[2,40,256]{2,1,0:T(8,128)(2,1)S(1)} collective-permute-done((bf16[2,40,256]{2,1,0:T(8,128)(2,1)S(1)}, bf16[2,40,256]{2,1,0:T(8,128)(2,1)S(1)}, u32[]{:S(2)}, u32[]{:S(2)}) %collective-permute-start.14) | collective-permute-done | bytes 40992 | tf_op jit(solution)/shard_map/ppermute | solution.py:340
  33.2 0.7 %shard_map.106 = (bf16[40,1024]{1,0:T(8,128)(2,1)}, bf16[40,1024]{1,0:T(8,128)(2,1)}) custom-call(bf16[2,40,256]{2,1,0:T(8,128)(2,1)S(1)} %get-tuple-element.55.refs_8_.refs_0_, bf16[2,40,256]{2,1,0:T(8,128)(2,1)S(1)} %collective-permute-done.13.refs_1_, bf16[2,40,256]{2,1,0:T(8,128)(2,1)S(1)} %collective-permute-done.14.refs_2_, ...), custom_call_target="tpu_custom_call" | custom-call | flops 110000000 | bytes 163840 | tf_op jit(solution)/shard_map/pallas_call | solution.py:35
  (25 shorter events, 0.1 us)
Async XLA Ops:
  0.6 2.3 %copy-start = (bf16[160,256]{1,0:T(8,128)(2,1)S(1)}, bf16[160,256]{1,0:T(8,128)(2,1)}, u32[]{:S(2)}) copy-start(bf16[160,256]{1,0:T(8,128)(2,1)} %refs_0_.4) | copy-start | bytes 245764
  0.6 2.3 %copy-start.1 = (bf16[160,256]{1,0:T(8,128)(2,1)S(1)}, bf16[160,256]{1,0:T(8,128)(2,1)}, u32[]{:S(2)}) copy-start(bf16[160,256]{1,0:T(8,128)(2,1)} %refs_2_.4) | copy-start | bytes 245764
  0.7 6.7 %copy-start.2 = (bf16[160,2048]{1,0:T(8,128)(2,1)S(1)}, bf16[160,2048]{1,0:T(8,128)(2,1)}, u32[]{:S(2)}) copy-start(bf16[160,2048]{1,0:T(8,128)(2,1)} %refs_0_.5) | copy-start | bytes 1966084
  0.7 6.7 %copy-start.3 = (bf16[160,2048]{1,0:T(8,128)(2,1)S(1)}, bf16[160,2048]{1,0:T(8,128)(2,1)}, u32[]{:S(2)}) copy-start(bf16[160,2048]{1,0:T(8,128)(2,1)} %refs_1_.3) | copy-start | bytes 1966084
  0.7 6.7 %copy-start.4 = (bf16[160,2048]{1,0:T(8,128)(2,1)S(1)}, bf16[160,2048]{1,0:T(8,128)(2,1)}, u32[]{:S(2)}) copy-start(bf16[160,2048]{1,0:T(8,128)(2,1)} %refs_2_.5) | copy-start | bytes 1966084
  0.7 1.8 %collective-permute-start = (bf16[160,256]{1,0:T(8,128)(2,1)}, bf16[160,256]{1,0:T(8,128)(2,1)S(1)}, u32[]{:S(2)}, u32[]{:S(2)}) collective-permute-start(bf16[160,256]{1,0:T(8,128)(2,1)} %refs_0_.4), channel_id=1, source_target_pairs={{0,4},{4,0},{8,12},{12,8},{16,20},{20,16},{24,28},{28,24},{1,5},{5... | collective-permute-start | bytes 245768 | tf_op jit(solution)/shard_map/ppermute | solution.py:340
  1.2 1.5 %collective-permute-start.1 = (bf16[160,256]{1,0:T(8,128)(2,1)}, bf16[160,256]{1,0:T(8,128)(2,1)S(1)}, u32[]{:S(2)}, u32[]{:S(2)}) collective-permute-start(bf16[160,256]{1,0:T(8,128)(2,1)} %refs_2_.4), channel_id=1, source_target_pairs={{0,4},{4,0},{8,12},{12,8},{16,20},{20,16},{24,28},{28,24},{1,5},{5... | collective-permute-start | bytes 245768 | tf_op jit(solution)/shard_map/ppermute | solution.py:340
  2.7 4.6 %copy-start.5 = (f32[160,16]{0,1:T(8,128)S(1)}, f32[160,16]{0,1:T(8,128)}, u32[]{:S(2)}) copy-start(f32[160,16]{0,1:T(8,128)} %param.13) | copy-start | bytes 30724
  2.7 4.6 %collective-permute-start.2 = (bf16[2,160,1024]{2,1,0:T(8,128)(2,1)S(1)}, bf16[2,160,1024]{2,1,0:T(8,128)(2,1)S(1)}, u32[]{:S(2)}, u32[]{:S(2)}) collective-permute-start(bf16[2,160,1024]{2,1,0:T(8,128)(2,1)S(1)} %get-tuple-element.34), channel_id=1, source_target_pairs={{0,4},{4,0},{8,12},{12,8},{16,20},{20,16},{24,28},{28,24},{1,5},{5... | collective-permute-start | bytes 1966088 | tf_op jit(solution)/shard_map/ppermute | solution.py:340
  3.0 7.5 %collective-permute-start.5 = (bf16[640,128]{1,0:T(8,128)(2,1)S(1)}, bf16[640,128]{1,0:T(8,128)(2,1)S(1)}, u32[]{:S(2)}, u32[]{:S(2)}) collective-permute-start(bf16[640,128]{1,0:T(8,128)(2,1)S(1)} %shard_map.95.refs_5_.refs_7_.refs_3_.refs_4_), channel_id=1, source_target_pairs={{0,16},{4,20},{8,24},{12,28},{16,0},{20,4},{24,8},{28,12},{1,17},{... | collective-permute-start | bytes 491528 | tf_op jit(solution)/shard_map/ppermute | solution.py:340
  5.8 6.6 %collective-permute-start.4 = (bf16[640,128]{1,0:T(8,128)(2,1)S(1)}, bf16[640,128]{1,0:T(8,128)(2,1)S(1)}, u32[]{:S(2)}, u32[]{:S(2)}) collective-permute-start(bf16[640,128]{1,0:T(8,128)(2,1)S(1)} %shard_map.95.refs_5_.refs_7_.refs_3_.refs_4_), channel_id=1, source_target_pairs={{0,8},{4,12},{8,0},{12,4},{16,24},{20,28},{24,16},{28,20},{1,9},{5... | collective-permute-start | bytes 491528 | tf_op jit(solution)/shard_map/ppermute | solution.py:340
  8.3 2.2 %collective-permute-start.3 = (f32[8,640]{1,0:T(8,128)S(1)}, f32[8,640]{1,0:T(8,128)S(1)}, u32[]{:S(2)}, u32[]{:S(2)}) collective-permute-start(f32[8,640]{1,0:T(8,128)S(1)} %get-tuple-element.40), channel_id=1, source_target_pairs={{0,4},{4,0},{8,12},{12,8},{16,20},{20,16},{24,28},{28,24},{1,5},{5... | collective-permute-start | bytes 61448 | tf_op jit(solution)/shard_map/ppermute | solution.py:340
  8.4 7.8 %collective-permute-start.6 = (bf16[640,128]{1,0:T(8,128)(2,1)S(1)}, bf16[640,128]{1,0:T(8,128)(2,1)S(1)}, u32[]{:S(2)}, u32[]{:S(2)}) collective-permute-start(bf16[640,128]{1,0:T(8,128)(2,1)S(1)} %get-tuple-element.41), channel_id=1, source_target_pairs={{0,24},{4,28},{8,16},{12,20},{16,8},{20,12},{24,0},{28,4},{1,25},{... | collective-permute-start | bytes 491528 | tf_op jit(solution)/shard_map/ppermute | solution.py:340
  13.6 7.5 %collective-permute-start.7 = (bf16[640,128]{1,0:T(8,128)(2,1)S(1)}, bf16[640,128]{1,0:T(8,128)(2,1)S(1)}, u32[]{:S(2)}, u32[]{:S(2)}) collective-permute-start(bf16[640,128]{1,0:T(8,128)(2,1)S(1)} %shard_map.100.refs_8_), channel_id=1, source_target_pairs={{0,16},{4,20},{8,24},{12,28},{16,0},{20,4},{24,8},{28,12},{1,17},{... | collective-permute-start | bytes 491528 | tf_op jit(solution)/shard_map/ppermute | solution.py:340
  14.7 6.4 %collective-permute-start.8 = (bf16[640,128]{1,0:T(8,128)(2,1)S(1)}, bf16[640,128]{1,0:T(8,128)(2,1)S(1)}, u32[]{:S(2)}, u32[]{:S(2)}) collective-permute-start(bf16[640,128]{1,0:T(8,128)(2,1)S(1)} %shard_map.101), channel_id=1, source_target_pairs={{0,8},{4,12},{8,0},{12,4},{16,24},{20,28},{24,16},{28,20},{1,9},{5... | collective-permute-start | bytes 491528 | tf_op jit(solution)/shard_map/ppermute | solution.py:340
  16.9 7.6 %collective-permute-start.11 = (bf16[320,128]{1,0:T(8,128)(2,1)S(1)}, bf16[320,128]{1,0:T(8,128)(2,1)S(1)}, u32[]{:S(2)}, u32[]{:S(2)}) collective-permute-start(bf16[320,128]{1,0:T(8,128)(2,1)S(1)} %shard_map.97.refs_8_), channel_id=1, source_target_pairs={{0,28},{4,24},{8,20},{12,16},{16,12},{20,8},{24,4},{28,0},{1,29},{... | collective-permute-start | bytes 245768 | tf_op jit(solution)/shard_map/ppermute | solution.py:340
  18.3 6.1 %collective-permute-start.9 = (bf16[320,128]{1,0:T(8,128)(2,1)S(1)}, bf16[320,128]{1,0:T(8,128)(2,1)S(1)}, u32[]{:S(2)}, u32[]{:S(2)}) collective-permute-start(bf16[320,128]{1,0:T(8,128)(2,1)S(1)} %shard_map.98.refs_8_), channel_id=1, source_target_pairs={{0,24},{4,28},{8,16},{12,20},{16,8},{20,12},{24,0},{28,4},{1,25},{... | collective-permute-start | bytes 245768 | tf_op jit(solution)/shard_map/ppermute | solution.py:340
  21.1 3.3 %collective-permute-start.10 = (f32[320,128]{1,0:T(8,128)S(1)}, f32[320,128]{1,0:T(8,128)S(1)}, u32[]{:S(2)}, u32[]{:S(2)}) collective-permute-start(f32[320,128]{1,0:T(8,128)S(1)} %get-tuple-element.49), channel_id=1, source_target_pairs={{0,4},{4,0},{8,12},{12,8},{16,20},{20,16},{24,28},{28,24},{1,5},{5... | collective-permute-start | bytes 491528 | tf_op jit(solution)/shard_map/ppermute | solution.py:340
  24.5 4.4 %collective-permute-start.12 = (bf16[2,640,128]{2,1,0:T(8,128)(2,1)S(1)}, bf16[2,640,128]{2,1,0:T(8,128)(2,1)S(1)}, u32[]{:S(2)}, u32[]{:S(2)}) collective-permute-start(bf16[2,640,128]{2,1,0:T(8,128)(2,1)S(1)} %shard_map.103), channel_id=1, source_target_pairs={{0,4},{4,0},{8,12},{12,8},{16,20},{20,16},{24,28},{28,24},{1,5},{5... | collective-permute-start | bytes 983048 | tf_op jit(solution)/shard_map/ppermute | solution.py:340
  24.7 7.5 %collective-permute-start.13 = (bf16[2,40,256]{2,1,0:T(8,128)(2,1)S(1)}, bf16[2,40,256]{2,1,0:T(8,128)(2,1)S(1)}, u32[]{:S(2)}, u32[]{:S(2)}) collective-permute-start(bf16[2,40,256]{2,1,0:T(8,128)(2,1)S(1)} %get-tuple-element.56), channel_id=1, source_target_pairs={{0,2},{1,3},{2,0},{3,1},{4,6},{5,7},{6,4},{7,5},{8,10},{9,11},{10,... | collective-permute-start | bytes 122888 | tf_op jit(solution)/shard_map/ppermute | solution.py:340
  27.3 5.8 %collective-permute-start.14 = (bf16[2,40,256]{2,1,0:T(8,128)(2,1)S(1)}, bf16[2,40,256]{2,1,0:T(8,128)(2,1)S(1)}, u32[]{:S(2)}, u32[]{:S(2)}) collective-permute-start(bf16[2,40,256]{2,1,0:T(8,128)(2,1)S(1)} %get-tuple-element.57), channel_id=1, source_target_pairs={{0,3},{1,2},{2,1},{3,0},{4,7},{5,6},{6,5},{7,4},{8,11},{9,10},{10,... | collective-permute-start | bytes 122888 | tf_op jit(solution)/shard_map/ppermute | solution.py:340
  28.7 4.5 %collective-permute-start.15 = (bf16[2,40,256]{2,1,0:T(8,128)(2,1)S(1)}, bf16[2,40,256]{2,1,0:T(8,128)(2,1)S(1)}, u32[]{:S(2)}, u32[]{:S(2)}) collective-permute-start(bf16[2,40,256]{2,1,0:T(8,128)(2,1)S(1)} %get-tuple-element.58), channel_id=1, source_target_pairs={{0,1},{1,0},{2,3},{3,2},{4,5},{5,4},{6,7},{7,6},{8,9},{9,8},{10,11... | collective-permute-start | bytes 122888 | tf_op jit(solution)/shard_map/ppermute | solution.py:340
